TPU v7x, 32 devices: a whole 2x2x4 slice. The times are simulated.
32 devices in a mesh: expert: 16 (over z, y, core), fsdp: 2 (over x).
Axes of the slice: x: 2, y: 2, z: 4, core: 2. Of those that a mesh axis runs over, the one named last changes fastest.
Arguments:
- tokens: bfloat16 [4096, 2048], P(('expert', 'fsdp')), may hold values from -6 to 6
- cotangent: bfloat16 [4096, 2048], P(('expert', 'fsdp')), may hold values from -6 to 6
- routes: int32 [4096, 6], P(('expert', 'fsdp')), may hold values from 0 to 15, all different within a row; in each aligned block of 128 rows (0 to 127, 128 to 255, ...) at most 60 rows name the same one
- lengths: int32 [16], P('expert'), may hold values from 64 to 256, as said below
- attn_gain: bfloat16 [2048], P(('expert', 'fsdp')), may hold values from 0.099609375 to 1.8984375
- q_weight: bfloat16 [2048, 3072], P(('expert', 'fsdp')), may hold values from -0.1875 to 0.1875
- kva_weight: bfloat16 [2048, 576], P(('expert', 'fsdp')), may hold values from -0.125 to 0.125
- kv_gain: bfloat16 [512], P(('expert', 'fsdp')), may hold values from 0.099609375 to 1.8984375
- kvb_weight: bfloat16 [512, 4096], P(('expert', 'fsdp')), may hold values from -0.25 to 0.25
- out_weight: bfloat16 [2048, 2048], P(('expert', 'fsdp')), may hold values from -1 to 1
- ffn_gain: bfloat16 [2048], P(('expert', 'fsdp')), may hold values from 0.099609375 to 1.8984375
- router_weight: bfloat16 [2048, 16], P(('expert', 'fsdp')), may hold values from -0.0625 to 0.0625
- shared_gate: bfloat16 [2048, 1408], P(('expert', 'fsdp')), may hold values from -0.125 to 0.125
- shared_up: bfloat16 [2048, 1408], P(('expert', 'fsdp')), may hold values from -0.125 to 0.125
- shared_down: bfloat16 [1408, 2048], P(('expert', 'fsdp')), may hold values from -0.15625 to 0.15625
- expert_gate: bfloat16 [16, 2048, 1408], P('expert', 'fsdp'), may hold values from -0.125 to 0.125
- expert_up: bfloat16 [16, 2048, 1408], P('expert', 'fsdp'), may hold values from -0.125 to 0.125
- expert_down: bfloat16 [16, 1408, 2048], P('expert', None, 'fsdp'), may hold values from -6 to 6
Outputs:
- mixed: bfloat16 [4096, 2048], P(('expert', 'fsdp'))
- tokens_grad: float32 [4096, 2048], P(('expert', 'fsdp'))
- balance: float32 [], replicated
- attn_gain_grad: float32 [2048], P(('expert', 'fsdp'))
- q_weight_grad: float32 [2048, 3072], P(('expert', 'fsdp'))
- kva_weight_grad: float32 [2048, 576], P(('expert', 'fsdp'))
- kv_gain_grad: float32 [512], P(('expert', 'fsdp'))
- kvb_weight_grad: float32 [512, 4096], P(('expert', 'fsdp'))
- out_weight_grad: float32 [2048, 2048], P(('expert', 'fsdp'))
- ffn_gain_grad: float32 [2048], P(('expert', 'fsdp'))
- router_weight_grad: float32 [2048, 16], P(('expert', 'fsdp'))
- shared_gate_grad: float32 [2048, 1408], P(('expert', 'fsdp'))
- shared_up_grad: float32 [2048, 1408], P(('expert', 'fsdp'))
- shared_down_grad: float32 [1408, 2048], P(('expert', 'fsdp'))
- expert_gate_grad: float32 [16, 2048, 1408], P('expert', 'fsdp')
- expert_up_grad: float32 [16, 2048, 1408], P('expert', 'fsdp')
- expert_down_grad: float32 [16, 1408, 2048], P('expert', None, 'fsdp')
Inputs may be any that keep to these rules, and one draw needn't show every extreme that they name: `routes`: in each device's 128 rows (aligned blocks) no expert is named by more than 60 pairs, and in every draw some expert is named by exactly 60 in some block. Valid slots are the first ones of a sequence; lengths never fall from one sequence to the next; the first sequence has a quarter of its slots valid and the last is full.
All inputs are finite; a program needn't handle non-finite values.
Results may differ from a plain program's by a relative error of at most 0.024.
Values may be sent and summed in bfloat16 or wider, within the bound.
A program may use at most 384 MiB of HBM per device.

v0:
```python
import jax
import jax.numpy as jnp
from jax import lax
from jax.sharding import PartitionSpec as P

D = 2048
H = 16
DN = 128
DR = 64
DV = 128
KVR = 512
TOPK = 6


epsilon = 1e-06
balance_weight = 0.001
masked_value = -1e30


def rms_norm(vector, gain_row):
    inverse = lax.rsqrt(jnp.mean(vector * vector, axis=-1, keepdims=True) + epsilon)
    return (vector * inverse * gain_row, inverse)


def norm_back(grad_in, vector, inverse, gain_row):
    scaled = grad_in * gain_row
    gain_grad = jnp.sum(grad_in * vector * inverse, axis=0)
    vector_grad = inverse * scaled - vector * inverse**3 * jnp.mean(
        scaled * vector, axis=-1, keepdims=True
    )
    return (vector_grad, gain_grad)


def rope_tables(positions):
    half_width = DR // 2
    frequency = 10000.0 ** (-jnp.arange(half_width, dtype=jnp.float32) / half_width)
    angles = positions.astype(jnp.float32)[:, None] * frequency[None, :]
    return (jnp.cos(angles), jnp.sin(angles))


def rotate(vector, cosine, sine_vals):
    half_width = vector.shape[-1] // 2
    first_half = vector[..., :half_width]
    second_half = vector[..., half_width:]
    return jnp.concatenate(
        [
            first_half * cosine - second_half * sine_vals,
            second_half * cosine + first_half * sine_vals,
        ],
        axis=-1,
    )


def rotate_back(grad_in, cosine, sine_vals):
    half_width = grad_in.shape[-1] // 2
    first_half = grad_in[..., :half_width]
    second_half = grad_in[..., half_width:]
    return jnp.concatenate(
        [
            first_half * cosine + second_half * sine_vals,
            second_half * cosine - first_half * sine_vals,
        ],
        axis=-1,
    )


def silu_slope(vector):
    sigmoid_vals = jax.nn.sigmoid(vector)
    return sigmoid_vals * (1.0 + vector * (1.0 - sigmoid_vals))


def body(
    tokens,
    cotangent,
    routes,
    lengths,
    attn_gain,
    q_weight,
    kva_weight,
    kv_gain,
    kvb_weight,
    out_weight,
    ffn_gain,
    router_weight,
    shared_gate,
    shared_up,
    shared_down,
    expert_gate,
    expert_up,
    expert_down,
):
    (
        g_attn,
        w_query,
        w_compress,
        g_latent,
        w_expand,
        w_output,
        g_ffn,
        w_router,
        w_sgate,
        w_sup,
        w_sdown,
    ) = (
        lax.all_gather(attn_gain, ("expert", "fsdp"), axis=0, tiled=True),
        lax.all_gather(q_weight, ("expert", "fsdp"), axis=0, tiled=True),
        lax.all_gather(kva_weight, ("expert", "fsdp"), axis=0, tiled=True),
        lax.all_gather(kv_gain, ("expert", "fsdp"), axis=0, tiled=True),
        lax.all_gather(kvb_weight, ("expert", "fsdp"), axis=0, tiled=True),
        lax.all_gather(out_weight, ("expert", "fsdp"), axis=0, tiled=True),
        lax.all_gather(ffn_gain, ("expert", "fsdp"), axis=0, tiled=True),
        lax.all_gather(router_weight, ("expert", "fsdp"), axis=0, tiled=True),
        lax.all_gather(shared_gate, ("expert", "fsdp"), axis=0, tiled=True),
        lax.all_gather(shared_up, ("expert", "fsdp"), axis=0, tiled=True),
        lax.all_gather(shared_down, ("expert", "fsdp"), axis=0, tiled=True),
    )
    expert_gate_weight, expert_up_weight, expert_down_weight = (
        lax.all_gather(expert_gate, "fsdp", axis=1, tiled=True),
        lax.all_gather(expert_up, "fsdp", axis=1, tiled=True),
        lax.all_gather(expert_down, "fsdp", axis=2, tiled=True),
    )
    tok_rows = tokens.shape[0]
    seq_len = tok_rows * lax.axis_size("fsdp")
    column_count = lax.axis_size("expert")
    slot_total = seq_len * column_count
    expert_count = router_weight.shape[1]
    exp_local = expert_gate.shape[0]
    capacity = max(4, 5 * tok_rows * TOPK // (4 * expert_count))
    slot_count = expert_count * capacity
    positions = lax.axis_index("fsdp") * tok_rows + jnp.arange(tok_rows, dtype=jnp.int32)
    seq_length = lengths[0]
    valid_mask = (positions < seq_length).astype(jnp.float32)
    cosine, sine_vals = rope_tables(positions)
    tokens_f = tokens.astype(jnp.float32)
    gain_attn = g_attn.astype(jnp.float32)
    normed_one, inverse_one = rms_norm(tokens_f, gain_attn)
    hidden_one = normed_one.astype(jnp.bfloat16)
    query_proj = jnp.dot(hidden_one, w_query, preferred_element_type=jnp.float32).reshape(
        tok_rows, H, DN + DR
    )
    query_all = jnp.concatenate(
        [
            query_proj[..., :DN],
            rotate(query_proj[..., DN:], cosine[:, None, :], sine_vals[:, None, :]),
        ],
        axis=-1,
    ).astype(jnp.bfloat16)
    compressed = jnp.dot(hidden_one, w_compress, preferred_element_type=jnp.float32)
    latent_raw = compressed[:, :KVR]
    gain_latent = g_latent.astype(jnp.float32)
    latent_norm, inverse_kv = rms_norm(latent_raw, gain_latent)
    latent = latent_norm.astype(jnp.bfloat16)
    key_rot = rotate(compressed[:, KVR:], cosine, sine_vals).astype(jnp.bfloat16)
    all_latent, all_rot = (
        lax.all_gather(latent, "fsdp", axis=0, tiled=True),
        lax.all_gather(key_rot, "fsdp", axis=0, tiled=True),
    )
    keyval = jnp.dot(all_latent, w_expand, preferred_element_type=jnp.float32).astype(jnp.bfloat16)
    keyval = keyval.reshape(seq_len, H, DN + DV)
    key_nope = keyval[..., :DN]
    value_all = keyval[..., DN:]
    query_nope = query_all[..., :DN]
    query_rope = query_all[..., DN:]
    score_scale = (DN + DR) ** (-0.5)
    key_place = jnp.arange(seq_len, dtype=jnp.int32)
    allowed = (key_place[None, :] <= positions[:, None]) & (key_place[None, :] < seq_length)

    def scores_of():
        raw_scores = jnp.einsum(
            "thd,shd->hts", query_nope, key_nope, preferred_element_type=jnp.float32
        ) + jnp.einsum("thr,sr->hts", query_rope, all_rot, preferred_element_type=jnp.float32)
        return jnp.where(allowed[None], raw_scores * score_scale, masked_value)

    scores = scores_of()
    row_max = jnp.max(scores, axis=-1, keepdims=True)
    exp_scores = jnp.exp(scores - row_max)
    row_sum = jnp.sum(exp_scores, axis=-1, keepdims=True)
    log_total = row_max + jnp.log(row_sum)
    weights_low = (exp_scores / row_sum).astype(jnp.bfloat16)
    context = (
        jnp.einsum("hts,shd->thd", weights_low, value_all, preferred_element_type=jnp.float32)
        .reshape(tok_rows, H * DV)
        .astype(jnp.bfloat16)
    )
    residual = tokens_f + jnp.dot(context, w_output, preferred_element_type=jnp.float32)
    gain_ffn = g_ffn.astype(jnp.float32)
    normed_two, inverse_two = rms_norm(residual, gain_ffn)
    hidden_two = normed_two.astype(jnp.bfloat16)
    router_probs = jax.nn.softmax(
        jnp.dot(hidden_two, w_router, preferred_element_type=jnp.float32), axis=-1
    )
    expert_ids = jnp.arange(expert_count, dtype=jnp.int32)
    hot_pairs = (routes[:, :, None] == expert_ids[None, None, :]).astype(jnp.float32)
    gate_vals = jnp.sum(hot_pairs * router_probs[:, None, :], axis=-1)
    local_counts = jnp.sum(hot_pairs * valid_mask[:, None, None], axis=(0, 1))
    local_shares = jnp.sum(router_probs * valid_mask[:, None], axis=0)
    route_counts, share_sums, valid_total = lax.psum(
        (local_counts, local_shares, jnp.sum(valid_mask)), ("expert", "fsdp")
    )
    frequency = expert_count / (TOPK * valid_total) * route_counts
    balance = jnp.sum(frequency * (share_sums / valid_total))
    flat_routes = routes.reshape(-1)
    hot_int = (flat_routes[:, None] == expert_ids[None, :]).astype(jnp.int32)
    rank_index = jnp.sum((jnp.cumsum(hot_int, axis=0) - 1) * hot_int, axis=1)
    slot_index = (
        flat_routes % exp_local * (column_count * capacity)
        + flat_routes // exp_local * capacity
        + rank_index
    )
    slot_ids = jnp.arange(slot_count, dtype=jnp.int32)
    placement = (slot_index[None, :] == slot_ids[:, None]).astype(jnp.bfloat16)
    pair_owner = (
        (jnp.arange(tok_rows * TOPK, dtype=jnp.int32) // TOPK)[:, None]
        == jnp.arange(tok_rows, dtype=jnp.int32)[None, :]
    ).astype(jnp.bfloat16)
    picker = jnp.dot(placement, pair_owner, preferred_element_type=jnp.float32).astype(jnp.bfloat16)
    send_rows = (
        jnp.dot(picker, hidden_two, preferred_element_type=jnp.float32)
        .astype(jnp.bfloat16)
        .reshape(exp_local, column_count, capacity, D)
    )
    expert_input_rows = lax.all_to_all(
        send_rows, "expert", split_axis=1, concat_axis=1, tiled=True
    ).reshape(exp_local, column_count * capacity, D)
    hidden_gate_values = jnp.einsum(
        "suo,soc->suc", expert_input_rows, expert_gate_weight, preferred_element_type=jnp.float32
    )
    hidden_up_values = jnp.einsum(
        "suo,soc->suc", expert_input_rows, expert_up_weight, preferred_element_type=jnp.float32
    )
    expert_activation = (jax.nn.silu(hidden_gate_values) * hidden_up_values).astype(jnp.bfloat16)
    expert_out = jnp.einsum(
        "qko,qoy->qky", expert_activation, expert_down_weight, preferred_element_type=jnp.float32
    ).astype(jnp.bfloat16)
    returned = lax.all_to_all(
        expert_out.reshape(exp_local, column_count, capacity, D),
        "expert",
        split_axis=1,
        concat_axis=1,
        tiled=True,
    ).reshape(slot_count, D)
    pair_out = returned[slot_index].astype(jnp.float32).reshape(tok_rows, TOPK, D)
    routed = jnp.sum(gate_vals[:, :, None] * pair_out, axis=1)
    shared_g = jnp.dot(hidden_two, w_sgate, preferred_element_type=jnp.float32)
    shared_u = jnp.dot(hidden_two, w_sup, preferred_element_type=jnp.float32)
    shared_act = (jax.nn.silu(shared_g) * shared_u).astype(jnp.bfloat16)
    shared_out = jnp.dot(shared_act, w_sdown, preferred_element_type=jnp.float32)
    mixed = (residual + shared_out + routed).astype(jnp.bfloat16)
    fill_scale = slot_total / valid_total
    grad_out = cotangent.astype(jnp.float32) * (valid_mask * fill_scale)[:, None]
    grad_low = grad_out.astype(jnp.bfloat16)
    d_shared_act = jnp.dot(grad_low, w_sdown.T, preferred_element_type=jnp.float32)
    d_sdown_w = jnp.dot(shared_act.T, grad_low, preferred_element_type=jnp.float32)
    d_sgate = (d_shared_act * shared_u * silu_slope(shared_g)).astype(jnp.bfloat16)
    d_sup = (d_shared_act * jax.nn.silu(shared_g)).astype(jnp.bfloat16)
    d_sgate_w = jnp.dot(hidden_two.T, d_sgate, preferred_element_type=jnp.float32)
    d_sup_w = jnp.dot(hidden_two.T, d_sup, preferred_element_type=jnp.float32)
    d_hidden_two = jnp.dot(d_sgate, w_sgate.T, preferred_element_type=jnp.float32) + jnp.dot(
        d_sup, w_sup.T, preferred_element_type=jnp.float32
    )
    d_gate = jnp.sum(grad_out[:, None, :] * pair_out, axis=-1)
    d_pair_out = (
        (gate_vals[:, :, None] * grad_out[:, None, :])
        .astype(jnp.bfloat16)
        .reshape(tok_rows * TOPK, D)
    )
    d_send = (
        jnp.dot(placement, d_pair_out, preferred_element_type=jnp.float32)
        .astype(jnp.bfloat16)
        .reshape(exp_local, column_count, capacity, D)
    )
    expert_output_gradient = lax.all_to_all(
        d_send, "expert", split_axis=1, concat_axis=1, tiled=True
    ).reshape(exp_local, column_count * capacity, D)
    expert_activation_gradient = jnp.einsum(
        "pin,psn->pis",
        expert_output_gradient,
        expert_down_weight,
        preferred_element_type=jnp.float32,
    )
    d_edown_w = jnp.einsum(
        "tuy,tuq->tyq",
        expert_activation,
        expert_output_gradient,
        preferred_element_type=jnp.float32,
    )
    expert_gate_hidden_gradient = (
        expert_activation_gradient * hidden_up_values * silu_slope(hidden_gate_values)
    ).astype(jnp.bfloat16)
    expert_up_hidden_gradient = (
        expert_activation_gradient * jax.nn.silu(hidden_gate_values)
    ).astype(jnp.bfloat16)
    expert_gate_weight_gradient = jnp.einsum(
        "jtg,jtz->jgz",
        expert_input_rows,
        expert_gate_hidden_gradient,
        preferred_element_type=jnp.float32,
    )
    expert_up_weight_gradient = jnp.einsum(
        "jtg,jtz->jgz",
        expert_input_rows,
        expert_up_hidden_gradient,
        preferred_element_type=jnp.float32,
    )
    d_expert_in = (
        jnp.einsum(
            "yow,ypw->yop",
            expert_gate_hidden_gradient,
            expert_gate_weight,
            preferred_element_type=jnp.float32,
        )
        + jnp.einsum(
            "yow,ypw->yop",
            expert_up_hidden_gradient,
            expert_up_weight,
            preferred_element_type=jnp.float32,
        )
    ).astype(jnp.bfloat16)
    d_returned = lax.all_to_all(
        d_expert_in.reshape(exp_local, column_count, capacity, D),
        "expert",
        split_axis=1,
        concat_axis=1,
        tiled=True,
    ).reshape(slot_count, D)
    d_hidden_two = d_hidden_two + jnp.dot(picker.T, d_returned, preferred_element_type=jnp.float32)
    expert_gate_partial, expert_up_partial, expert_down_partial = (
        lax.psum_scatter(
            expert_gate_weight_gradient.astype(jnp.bfloat16),
            "fsdp",
            scatter_dimension=1,
            tiled=True,
        ).astype(jnp.float32),
        lax.psum_scatter(
            expert_up_weight_gradient.astype(jnp.bfloat16), "fsdp", scatter_dimension=1, tiled=True
        ).astype(jnp.float32),
        lax.psum_scatter(
            d_edown_w.astype(jnp.bfloat16), "fsdp", scatter_dimension=2, tiled=True
        ).astype(jnp.float32),
    )
    d_probs = (
        jnp.sum(hot_pairs * d_gate[:, :, None], axis=1)
        + balance_weight * valid_mask[:, None] * frequency[None, :] / valid_total
    )
    d_logits = (
        router_probs * (d_probs - jnp.sum(router_probs * d_probs, axis=-1, keepdims=True))
    ).astype(jnp.bfloat16)
    d_router_w = jnp.dot(hidden_two.T, d_logits, preferred_element_type=jnp.float32)
    d_hidden_two = d_hidden_two + jnp.dot(d_logits, w_router.T, preferred_element_type=jnp.float32)
    d_residual, d_ffn_gain = norm_back(d_hidden_two, residual, inverse_two, gain_ffn)
    d_residual = d_residual + grad_out
    d_residual_low = d_residual.astype(jnp.bfloat16)
    d_output_w = jnp.dot(context.T, d_residual_low, preferred_element_type=jnp.float32)
    d_context = (
        jnp.dot(d_residual_low, w_output.T, preferred_element_type=jnp.float32)
        .astype(jnp.bfloat16)
        .reshape(tok_rows, H, DV)
    )
    again_scores = scores_of()
    probs_attn = jnp.exp(again_scores - log_total)
    probs_low = probs_attn.astype(jnp.bfloat16)
    d_value = jnp.einsum("hts,thd->shd", probs_low, d_context, preferred_element_type=jnp.float32)
    d_weights = jnp.einsum("thd,shd->hts", d_context, value_all, preferred_element_type=jnp.float32)
    d_scores = (
        probs_attn * (d_weights - jnp.sum(probs_attn * d_weights, axis=-1, keepdims=True))
    ).astype(jnp.bfloat16)
    d_query_nope = score_scale * jnp.einsum(
        "hts,shd->thd", d_scores, key_nope, preferred_element_type=jnp.float32
    )
    d_query_rope = score_scale * jnp.einsum(
        "hts,sr->thr", d_scores, all_rot, preferred_element_type=jnp.float32
    )
    d_key_nope = score_scale * jnp.einsum(
        "hts,thd->shd", d_scores, query_nope, preferred_element_type=jnp.float32
    )
    d_key_rot = score_scale * jnp.einsum(
        "hts,thr->sr", d_scores, query_rope, preferred_element_type=jnp.float32
    )
    d_keyval_all = jnp.concatenate([d_key_nope, d_value], axis=-1).reshape(seq_len, H * (DN + DV))
    own_dkeyval, own_dkeyrot = (
        lax.psum_scatter(
            d_keyval_all.astype(jnp.bfloat16), "fsdp", scatter_dimension=0, tiled=True
        ).astype(jnp.float32),
        lax.psum_scatter(
            d_key_rot.astype(jnp.bfloat16), "fsdp", scatter_dimension=0, tiled=True
        ).astype(jnp.float32),
    )
    d_keyval = own_dkeyval.astype(jnp.bfloat16)
    d_expand_w = jnp.dot(latent.T, d_keyval, preferred_element_type=jnp.float32)
    d_latent = jnp.dot(d_keyval, w_expand.T, preferred_element_type=jnp.float32)
    d_latent_raw, d_latent_gain = norm_back(d_latent, latent_raw, inverse_kv, gain_latent)
    d_compressed = jnp.concatenate(
        [d_latent_raw, rotate_back(own_dkeyrot, cosine, sine_vals)], axis=-1
    ).astype(jnp.bfloat16)
    d_compress_w = jnp.dot(hidden_one.T, d_compressed, preferred_element_type=jnp.float32)
    d_query = (
        jnp.concatenate(
            [d_query_nope, rotate_back(d_query_rope, cosine[:, None, :], sine_vals[:, None, :])],
            axis=-1,
        )
        .reshape(tok_rows, H * (DN + DR))
        .astype(jnp.bfloat16)
    )
    d_query_w = jnp.dot(hidden_one.T, d_query, preferred_element_type=jnp.float32)
    d_hidden_one = jnp.dot(d_query, w_query.T, preferred_element_type=jnp.float32) + jnp.dot(
        d_compressed, w_compress.T, preferred_element_type=jnp.float32
    )
    d_tokens, d_attn_gain = norm_back(d_hidden_one, tokens_f, inverse_one, gain_attn)
    tokens_grad = d_tokens + d_residual
    (
        attn_gain_part,
        query_part,
        compress_part,
        latent_gain_part,
        expand_part,
        output_part,
        ffn_gain_part,
        router_part,
        sgate_part,
        sup_part,
        sdown_part,
    ) = (
        lax.psum_scatter(d_attn_gain, ("expert", "fsdp"), scatter_dimension=0, tiled=True),
        lax.psum_scatter(d_query_w, ("expert", "fsdp"), scatter_dimension=0, tiled=True),
        lax.psum_scatter(d_compress_w, ("expert", "fsdp"), scatter_dimension=0, tiled=True),
        lax.psum_scatter(d_latent_gain, ("expert", "fsdp"), scatter_dimension=0, tiled=True),
        lax.psum_scatter(d_expand_w, ("expert", "fsdp"), scatter_dimension=0, tiled=True),
        lax.psum_scatter(d_output_w, ("expert", "fsdp"), scatter_dimension=0, tiled=True),
        lax.psum_scatter(d_ffn_gain, ("expert", "fsdp"), scatter_dimension=0, tiled=True),
        lax.psum_scatter(d_router_w, ("expert", "fsdp"), scatter_dimension=0, tiled=True),
        lax.psum_scatter(d_sgate_w, ("expert", "fsdp"), scatter_dimension=0, tiled=True),
        lax.psum_scatter(d_sup_w, ("expert", "fsdp"), scatter_dimension=0, tiled=True),
        lax.psum_scatter(d_sdown_w, ("expert", "fsdp"), scatter_dimension=0, tiled=True),
    )
    return (
        mixed,
        tokens_grad,
        balance,
        attn_gain_part,
        query_part,
        compress_part,
        latent_gain_part,
        expand_part,
        output_part,
        ffn_gain_part,
        router_part,
        sgate_part,
        sup_part,
        sdown_part,
        expert_gate_partial,
        expert_up_partial,
        expert_down_partial,
    )


def solution(mesh):
    return jax.shard_map(
        body,
        mesh=mesh,
        in_specs=(
            P(("expert", "fsdp"), None),
            P(("expert", "fsdp"), None),
            P(("expert", "fsdp"), None),
            P("expert"),
            P(("expert", "fsdp")),
            P(("expert", "fsdp"), None),
            P(("expert", "fsdp"), None),
            P(("expert", "fsdp")),
            P(("expert", "fsdp"), None),
            P(("expert", "fsdp"), None),
            P(("expert", "fsdp")),
            P(("expert", "fsdp"), None),
            P(("expert", "fsdp"), None),
            P(("expert", "fsdp"), None),
            P(("expert", "fsdp"), None),
            P("expert", "fsdp", None),
            P("expert", "fsdp", None),
            P("expert", None, "fsdp"),
        ),
        out_specs=(
            P(("expert", "fsdp"), None),
            P(("expert", "fsdp"), None),
            P(),
            P(("expert", "fsdp")),
            P(("expert", "fsdp"), None),
            P(("expert", "fsdp"), None),
            P(("expert", "fsdp")),
            P(("expert", "fsdp"), None),
            P(("expert", "fsdp"), None),
            P(("expert", "fsdp")),
            P(("expert", "fsdp"), None),
            P(("expert", "fsdp"), None),
            P(("expert", "fsdp"), None),
            P(("expert", "fsdp"), None),
            P("expert", "fsdp", None),
            P("expert", "fsdp", None),
            P("expert", None, "fsdp"),
        ),
        check_vma=False,
    )
```

profile of v0, /device:TPU:0, one launch (start us, length us, event | category | flops | bytes accessed | tf_op | source)
XLA Modules:
  0.0 3044.8 jit_solution(2852124954818947561)
XLA Ops:
  14.5 42.2 %all-reduce.9 = (bf16[2048]{0:T(1024)(128)(2,1)S(1)}, bf16[512]{0:T(512)(128)(2,1)S(1)}, bf16[2048]{0:T(1024)(128)(2,1)S(1)}) all-reduce(bf16[2048]{0:T(1024)(128)(2,1)S(1)} %dynamic-update-slice, bf16[512]{0:T(512)(128)(2,1)S(1)} %dynamic-update-slice.1, ...), channel_id=1, replica_groups=mesh['expert'=16,'fsdp'=2] {'expert','fsdp'}, use_global_device_ids=true, to_apply=%add | all-reduce | flops 4608 | bytes 18432
  59.8 12.0 all-gather.13.cloned.1.call-done
  87.1 48.7 %all-gather.15.cloned.1.call-done = bf16[512,4096]{1,0:T(8,128)(2,1)} async-done(((bf16[16,4096]{1,0:T(8,128)(2,1)}), bf16[512,4096]{1,0:T(8,128)(2,1)}) %all-gather.15.cloned.1.call-update) | async-done | bytes 4194320 | tf_op jit(solution)/shard_map/all_gather | solution.py:109
  143.3 90.0 %all-gather.17.cloned.1.call-done = bf16[2048,3072]{1,0:T(8,128)(2,1)} async-done(((bf16[64,3072]{1,0:T(8,128)(2,1)}), bf16[2048,3072]{1,0:T(8,128)(2,1)}) %all-gather.17.cloned.1.call-update) | async-done | bytes 12582928 | tf_op jit(solution)/shard_map/all_gather | solution.py:106
  245.5 66.3 %all-gather.19.cloned.1.call-done = bf16[2048,2048]{1,0:T(8,128)(2,1)} async-done(((bf16[64,2048]{1,0:T(8,128)(2,1)}), bf16[2048,2048]{1,0:T(8,128)(2,1)}) %all-gather.19.cloned.1.call-update) | async-done | bytes 8388624 | tf_op jit(solution)/shard_map/all_gather | solution.py:110
  331.7 112.9 %psum.21 = f32[]{:T(128)} all-reduce(f32[]{:T(128)} %convert_reduce_fusion), channel_id=1, replica_groups=mesh['expert'=16,'fsdp'=2] {'expert','fsdp'}, use_global_device_ids=true, to_apply=%region_13.14 | all-reduce | flops 1 | bytes 8 | tf_op jit(solution)/shard_map/psum | solution.py:197
  444.6 78.3 %all-gather.1 = bf16[32,64,16]{1,2,0:T(8,128)(2,1)S(1)} all-gather(bf16[1,64,16]{1,2,0:T(8,128)(2,1)S(1)} %bitcast.183), channel_id=1, replica_groups=mesh['expert'=16,'fsdp'=2] {'expert','fsdp'}, dimensions={0}, use_global_device_ids=true | all-gather | bytes 67584 | tf_op jit(solution)/shard_map/all_gather | solution.py:112
  560.8 83.4 %all-to-all-done.2 = bf16[1,16,60,2048]{3,2,0,1:T(8,128)(2,1)} async-done(((bf16[1,16,60,2048]{3,2,0,1:T(8,128)(2,1)}), bf16[1,16,60,2048]{3,2,0,1:T(8,128)(2,1)}, u32[]{:S(2)}, u32[]{:S(2)}) %all-to-all-start.2) | async-done | bytes 3932192 | tf_op jit(solution)/shard_map/all_to_all | solution.py:272
  671.6 15.6 multiply_convert_fusion.2
  701.3 36.3 %all-to-all-start.1 = ((bf16[1,16,60,2048]{3,2,0,1:T(8,128)(2,1)}), bf16[1,16,60,2048]{3,2,0,1:T(8,128)(2,1)}, u32[]{:S(2)}, u32[]{:S(2)}) async-start(bf16[1,16,60,2048]{3,2,0,1:T(8,128)(2,1)} %bitcast.167), calls=%async_computation.1 | async-start | bytes 8388608 | tf_op jit(solution)/shard_map/all_to_all | solution.py:235
  763.1 63.7 %all-to-all-done.1 = bf16[1,16,60,2048]{3,2,0,1:T(8,128)(2,1)} async-done(((bf16[1,16,60,2048]{3,2,0,1:T(8,128)(2,1)}), bf16[1,16,60,2048]{3,2,0,1:T(8,128)(2,1)}, u32[]{:S(2)}, u32[]{:S(2)}) %all-to-all-start.1) | async-done | bytes 3932192 | tf_op jit(solution)/shard_map/all_to_all | solution.py:235
  826.8 35.2 %all-to-all-start.3 = ((bf16[1,16,60,2048]{3,2,0,1:T(8,128)(2,1)}), bf16[1,16,60,2048]{3,2,0,1:T(8,128)(2,1)}, u32[]{:S(2)}, u32[]{:S(2)}) async-start(bf16[1,16,60,2048]{3,2,0,1:T(8,128)(2,1)} %bitcast.165), calls=%async_computation.3 | async-start | bytes 8388608 | tf_op jit(solution)/shard_map/all_to_all | solution.py:319
  918.7 57.1 %psum.22 = f32[16]{0:T(128)S(1)} all-reduce(f32[16]{0:T(128)S(1)} %get-tuple-element.27), channel_id=1, replica_groups=mesh['expert'=16,'fsdp'=2] {'expert','fsdp'}, use_global_device_ids=true, to_apply=%region_17.18 | all-reduce | flops 16 | bytes 128 | tf_op jit(solution)/shard_map/psum | solution.py:197
  1020.9 11.5 fusion.1
  1103.2 437.1 %fusion = f32[48,2048]{1,0:T(8,128)} fusion(f32[1408,2048]{1,0:T(8,128)} %fusion.58), kind=kCustom, calls=%all-reduce-scatter | all-reduce-scatter fusion | flops 3145729 | bytes 11927552
  1540.3 18.0 collective-permute-start.1
  1567.5 14.1 collective-permute-done.2
  1625.3 42.6 %all-reduce.8 = (f32[16]{0:T(128)S(1)}, f32[2048]{0:T(1024)S(1)}, f32[512]{0:T(512)S(1)}, f32[2048]{0:T(1024)S(1)}) all-reduce(f32[16]{0:T(128)S(1)} %copy-done.60, f32[2048]{0:T(1024)S(1)} %get-tuple-element.21, f32[512]{0:T(512)S(1)} %copy-done.59, f32[2048]{0:T(1024)S(1)} %copy-done.53), channel_id=1, replica_groups=mesh['expert'=16,'fsdp'=2] {'expert','fsdp'}, use_global_device_ids=true, to_apply=%region_26.27 | all-reduce | flops 4624 | bytes 36992 | tf_op jit(solution)/shard_map/psum | solution.py:197
  1672.3 163.6 %reduce-scatter.29.cloned.1.call-done = f32[64,1408]{1,0:T(8,128)} async-done(((f32[2048,1408]{1,0:T(8,128)}), f32[64,1408]{1,0:T(8,128)}) %reduce-scatter.29.cloned.1.call-update) | async-done | bytes 360464 | tf_op jit(solution)/shard_map/reduce_scatter | solution.py:431
  1836.0 253.0 %reduce-scatter.31.cloned.1.call-done = f32[64,1408]{1,0:T(8,128)} async-done(((f32[2048,1408]{1,0:T(8,128)}), f32[64,1408]{1,0:T(8,128)}) %reduce-scatter.31.cloned.1.call-update) | async-done | bytes 360464 | tf_op jit(solution)/shard_map/reduce_scatter | solution.py:432
  2088.9 148.1 %reduce-scatter.23.cloned.1.call-done = f32[64,576]{1,0:T(8,128)} async-done(((f32[2048,576]{1,0:T(8,128)}), f32[64,576]{1,0:T(8,128)}) %reduce-scatter.23.cloned.1.call-update) | async-done | bytes 147472 | tf_op jit(solution)/shard_map/reduce_scatter | solution.py:425
  2237.0 184.5 %reduce-scatter.25.cloned.1.call-done = f32[16,4096]{1,0:T(8,128)} async-done(((f32[512,4096]{1,0:T(8,128)}), f32[16,4096]{1,0:T(8,128)}) %reduce-scatter.25.cloned.1.call-update) | async-done | bytes 262160 | tf_op jit(solution)/shard_map/reduce_scatter | solution.py:427
  2421.5 361.3 %reduce-scatter.27.cloned.1.call-done = f32[64,2048]{1,0:T(8,128)} async-done(((f32[2048,2048]{1,0:T(8,128)}), f32[64,2048]{1,0:T(8,128)}) %reduce-scatter.27.cloned.1.call-update) | async-done | bytes 524304 | tf_op jit(solution)/shard_map/reduce_scatter | solution.py:428
  2782.9 254.9 %reduce-scatter.21.cloned.1.call-done = f32[64,3072]{1,0:T(8,128)} async-done(((f32[2048,3072]{1,0:T(8,128)}), f32[64,3072]{1,0:T(8,128)}) %reduce-scatter.21.cloned.1.call-update) | async-done | bytes 786448 | tf_op jit(solution)/shard_map/reduce_scatter | solution.py:424
  (371 shorter events, 396.6 us)
Async XLA Ops:
  7.9 127.9 %all-gather.15.cloned.1.call-start = ((), (), s32[]{:S(2)}) async-start(), calls=%async_computation.17 | async-start | bytes 4325376 | tf_op jit(solution)/shard_map/all_gather | solution.py:109
  8.7 224.6 %all-gather.17.cloned.1.call-start = ((), (), s32[]{:S(2)}) async-start(), calls=%async_computation.18 | async-start | bytes 12976128 | tf_op jit(solution)/shard_map/all_gather | solution.py:106
  9.4 302.4 %all-gather.19.cloned.1.call-start = ((), (), s32[]{:S(2)}) async-start(), calls=%async_computation.19 | async-start | bytes 8650752 | tf_op jit(solution)/shard_map/all_gather | solution.py:110
  10.0 639.1 %all-gather.27.cloned.1.call-start = ((), (), s32[]{:S(2)}) async-start(), calls=%async_computation.23 | async-start | bytes 8650752 | tf_op jit(solution)/shard_map/all_gather | solution.py:119
  10.6 649.7 %all-gather.29.cloned.1.call-start = ((), (), s32[]{:S(2)}) async-start(), calls=%async_computation.24 | async-start | bytes 8650752 | tf_op jit(solution)/shard_map/all_gather | solution.py:120
  11.2 660.4 %all-gather.25.cloned.1.call-start = ((), (), s32[]{:S(2)}) async-start(), calls=%async_computation.22 | async-start | bytes 8650752 | tf_op jit(solution)/shard_map/all_gather | solution.py:118
  325.7 224.9 %all-to-all-start = ((bf16[1,16,60,2048]{3,2,0,1:T(8,128)(2,1)}), bf16[1,16,60,2048]{3,2,0,1:T(8,128)(2,1)}, u32[]{:S(2)}, u32[]{:S(2)}) async-start(bf16[1,16,60,2048]{3,2,0,1:T(8,128)(2,1)} %bitcast.166), calls=%async_computation | async-start | bytes 8388608 | tf_op jit(solution)/shard_map/all_to_all | solution.py:222
  330.4 532.8 %all-gather.31.cloned.1.call-start = ((), (), s32[]{:S(2)}) async-start(), calls=%async_computation.34 | async-start | bytes 6488064 | tf_op jit(solution)/shard_map/all_gather | solution.py:115
  550.6 93.6 %all-to-all-start.2 = ((bf16[1,16,60,2048]{3,2,0,1:T(8,128)(2,1)}), bf16[1,16,60,2048]{3,2,0,1:T(8,128)(2,1)}, u32[]{:S(2)}, u32[]{:S(2)}) async-start(bf16[1,16,60,2048]{3,2,0,1:T(8,128)(2,1)} %bitcast.168), calls=%async_computation.2 | async-start | bytes 8388608 | tf_op jit(solution)/shard_map/all_to_all | solution.py:272
  555.2 315.9 %all-gather.23.cloned.1.call-start = ((), (), s32[]{:S(2)}) async-start(), calls=%async_computation.21 | async-start | bytes 5947392 | tf_op jit(solution)/shard_map/all_gather | solution.py:114
  701.3 125.5 %all-to-all-start.1 = ((bf16[1,16,60,2048]{3,2,0,1:T(8,128)(2,1)}), bf16[1,16,60,2048]{3,2,0,1:T(8,128)(2,1)}, u32[]{:S(2)}, u32[]{:S(2)}) async-start(bf16[1,16,60,2048]{3,2,0,1:T(8,128)(2,1)} %bitcast.167), calls=%async_computation.1 | async-start | bytes 8388608 | tf_op jit(solution)/shard_map/all_to_all | solution.py:235
  737.6 138.1 %all-gather.21.cloned.1.call-start = ((), (), s32[]{:S(2)}) async-start(), calls=%async_computation.20 | async-start | bytes 5947392 | tf_op jit(solution)/shard_map/all_gather | solution.py:113
  826.8 149.1 %all-to-all-start.3 = ((bf16[1,16,60,2048]{3,2,0,1:T(8,128)(2,1)}), bf16[1,16,60,2048]{3,2,0,1:T(8,128)(2,1)}, u32[]{:S(2)}, u32[]{:S(2)}) async-start(bf16[1,16,60,2048]{3,2,0,1:T(8,128)(2,1)} %bitcast.165), calls=%async_computation.3 | async-start | bytes 8388608 | tf_op jit(solution)/shard_map/all_to_all | solution.py:319
  862.0 195.7 %reduce-scatter.41.cloned.1.call-start = ((), (), s32[]{:S(2)}) async-start(), calls=%async_computation.36 | async-start | bytes 98304
  1008.1 599.8 %reduce-scatter.43.cloned.1.call-start = ((), (), s32[]{:S(2)}) async-start(), calls=%async_computation.37 | async-start | bytes 1081344
  1010.2 599.1 %reduce-scatter.37.cloned.1.call-start = ((), (), s32[]{:S(2)}) async-start(), calls=%async_computation.33 | async-start | bytes 8650752 | tf_op jit(solution)/shard_map/reduce_scatter | solution.py:337
  1020.6 593.8 %reduce-scatter.33.cloned.1.call-start = ((), (), s32[]{:S(2)}) async-start(), calls=%async_computation.31 | async-start | bytes 8650752 | tf_op jit(solution)/shard_map/reduce_scatter | solution.py:328
  1032.4 586.7 %reduce-scatter.35.cloned.1.call-start = ((), (), s32[]{:S(2)}) async-start(), calls=%async_computation.32 | async-start | bytes 8650752 | tf_op jit(solution)/shard_map/reduce_scatter | solution.py:334
  1043.4 792.6 %reduce-scatter.29.cloned.1.call-start = ((), (), s32[]{:S(2)}) async-start(), calls=%async_computation.29 | async-start | bytes 11894784 | tf_op jit(solution)/shard_map/reduce_scatter | solution.py:431
  1050.2 1038.7 %reduce-scatter.31.cloned.1.call-start = ((), (), s32[]{:S(2)}) async-start(), calls=%async_computation.30 | async-start | bytes 11894784 | tf_op jit(solution)/shard_map/reduce_scatter | solution.py:432
  1057.2 1179.8 %reduce-scatter.23.cloned.1.call-start = ((), (), s32[]{:S(2)}) async-start(), calls=%async_computation.26 | async-start | bytes 5406720 | tf_op jit(solution)/shard_map/reduce_scatter | solution.py:425
  1066.8 1354.7 %reduce-scatter.25.cloned.1.call-start = ((), (), s32[]{:S(2)}) async-start(), calls=%async_computation.27 | async-start | bytes 8650752 | tf_op jit(solution)/shard_map/reduce_scatter | solution.py:427
  1072.8 1710.1 %reduce-scatter.27.cloned.1.call-start = ((), (), s32[]{:S(2)}) async-start(), calls=%async_computation.28 | async-start | bytes 17301504 | tf_op jit(solution)/shard_map/reduce_scatter | solution.py:428
  1082.2 1955.5 %reduce-scatter.21.cloned.1.call-start = ((), (), s32[]{:S(2)}) async-start(), calls=%async_computation.25 | async-start | bytes 25952256 | tf_op jit(solution)/shard_map/reduce_scatter | solution.py:424
  (85 other events, 3438.2 us)
Sparse Core Ops, SparseCore 0:
  10.9 60.8 all-gather.12
  74.8 60.9 all-gather.14
  138.7 94.5 all-gather.16
  236.1 75.6 all-gather.18
  313.2 73.7 all-gather.26
  388.4 75.5 all-gather.28
  465.5 76.2 all-gather.24
  544.7 126.7 all-gather.30
  674.4 67.5 all-gather.22
  744.7 111.7 all-gather.20
  1003.5 10.0 reduce-scatter.40
  1015.7 31.8 reduce-scatter.38
  1049.9 136.7 reduce-scatter.42
  1189.4 131.0 reduce-scatter.36
  1323.3 133.7 reduce-scatter.32
  1459.3 117.4 reduce-scatter.34
  1579.6 256.3 reduce-scatter.28
  1838.8 250.0 reduce-scatter.30
  2091.9 145.0 reduce-scatter.22
  2239.8 181.6 reduce-scatter.24
  2424.5 358.2 reduce-scatter.26
  2791.0 246.6 reduce-scatter.20
where the time goes:
time: 3050 us; the launch traced here: 3040 us
  waiting for transfers between devices  1750 us (57%)
  blocking collectives  782 us (26%)
  matrix products  235 us (8%)
  local copies, waits for them, and re-layouts  117 us (4%)
  starting transfers between devices  108 us (4%)
  other arithmetic  35.3 us (1%)
    unnamed x2, blocking collectives  479 us
    reduce_scatter x1, waiting for transfers between devices, body(): lax.psum_scatter(d_output_w, ('expert', 'fsdp'), scatter_dimension=0, til...  361 us
    reduce_scatter x1, waiting for transfers between devices, body(): lax.psum_scatter(d_query_w, ('expert', 'fsdp'), scatter_dimension=0, tile...  255 us
    reduce_scatter x1, waiting for transfers between devices, body(): lax.psum_scatter(d_sup_w, ('expert', 'fsdp'), scatter_dimension=0, tiled=...  253 us
    psum x3, blocking collectives, body(): lax.psum((local_counts, local_shares, jnp.sum(valid_mask)), ('expert', 'f...  213 us
    reduce_scatter x1, waiting for transfers between devices, body(): lax.psum_scatter(d_expand_w, ('expert', 'fsdp'), scatter_dimension=0, til...  185 us
    reduce_scatter x1, waiting for transfers between devices, body(): lax.psum_scatter(d_sgate_w, ('expert', 'fsdp'), scatter_dimension=0, tile...  164 us
    reduce_scatter x1, waiting for transfers between devices, body(): lax.psum_scatter(d_compress_w, ('expert', 'fsdp'), scatter_dimension=0, t...  148 us
  transfers between devices with their start and end apart: 29, of which 13 were waited for; matrix products, arithmetic and copies ran while one was open for 26% of the time, Pallas kernels for 0%

commit v1 on v0

v1 whole, which is shorter than its diff:
```python
import jax
import jax.numpy as jnp
from jax import lax
from jax.sharding import PartitionSpec as P

D = 2048
H = 16
DN = 128
DR = 64
DV = 128
KVR = 512
TOPK = 6


epsilon = 1e-06
balance_weight = 0.001
masked_value = -1e30


def rms_norm(vector, gain_row):
    inverse = lax.rsqrt(jnp.mean(vector * vector, axis=-1, keepdims=True) + epsilon)
    return (vector * inverse * gain_row, inverse)


def norm_back(grad_in, vector, inverse, gain_row):
    scaled = grad_in * gain_row
    gain_grad = jnp.sum(grad_in * vector * inverse, axis=0)
    vector_grad = inverse * scaled - vector * inverse**3 * jnp.mean(
        scaled * vector, axis=-1, keepdims=True
    )
    return (vector_grad, gain_grad)


def rope_tables(positions):
    half_width = DR // 2
    frequency = 10000.0 ** (-jnp.arange(half_width, dtype=jnp.float32) / half_width)
    angles = positions.astype(jnp.float32)[:, None] * frequency[None, :]
    return (jnp.cos(angles), jnp.sin(angles))


def rotate(vector, cosine, sine_vals):
    half_width = vector.shape[-1] // 2
    first_half = vector[..., :half_width]
    second_half = vector[..., half_width:]
    return jnp.concatenate(
        [
            first_half * cosine - second_half * sine_vals,
            second_half * cosine + first_half * sine_vals,
        ],
        axis=-1,
    )


def rotate_back(grad_in, cosine, sine_vals):
    half_width = grad_in.shape[-1] // 2
    first_half = grad_in[..., :half_width]
    second_half = grad_in[..., half_width:]
    return jnp.concatenate(
        [
            first_half * cosine + second_half * sine_vals,
            second_half * cosine - first_half * sine_vals,
        ],
        axis=-1,
    )


def silu_slope(vector):
    sigmoid_vals = jax.nn.sigmoid(vector)
    return sigmoid_vals * (1.0 + vector * (1.0 - sigmoid_vals))


def gather_all(shard):
    return lax.all_gather(shard, ("expert", "fsdp"), axis=0, tiled=True)


def gather_plane(shard):
    return lax.all_gather(shard, "expert", axis=0, tiled=True)


def scatter_all(partial):
    return lax.psum_scatter(
        partial.astype(jnp.bfloat16), ("expert", "fsdp"), scatter_dimension=0, tiled=True
    ).astype(jnp.float32)


def scatter_plane(partial):
    return lax.psum_scatter(partial, "expert", scatter_dimension=0, tiled=True)


def from_peers(block):
    size = lax.axis_size("fsdp")
    return [block] + [
        lax.ppermute(block, "fsdp", [(j, (j - r) % size) for j in range(size)])
        for r in range(1, size)
    ]


def sum_to_peers(term):
    size = lax.axis_size("fsdp")
    arrived = [
        lax.ppermute(term(r), "fsdp", [(j, (j + r) % size) for j in range(size)])
        for r in range(1, size)
    ]
    return arrived


def body(
    tokens,
    cotangent,
    routes,
    lengths,
    attn_gain,
    q_weight,
    kva_weight,
    kv_gain,
    kvb_weight,
    out_weight,
    ffn_gain,
    router_weight,
    shared_gate,
    shared_up,
    shared_down,
    expert_gate,
    expert_up,
    expert_down,
):
    bf16, f32 = jnp.bfloat16, jnp.float32
    tok_rows, dim = tokens.shape
    peers = lax.axis_size("fsdp")
    group = lax.axis_size("expert")
    fid, eid = lax.axis_index("fsdp"), lax.axis_index("expert")
    seq_len = tok_rows * peers
    slot_total = seq_len * group
    expert_count = router_weight.shape[1]
    capacity = max(4, 5 * tok_rows * TOPK // (4 * expert_count))
    capacity = -(-capacity // 16) * 16
    half = dim // peers
    plane_rows = group * tok_rows
    pairs = group * capacity

    def roll_in(array, axis):
        return jnp.roll(array, -fid * half, axis=axis)

    def roll_out(array, axis):
        return jnp.roll(array, fid * half, axis=axis)

    positions = fid * tok_rows + jnp.arange(tok_rows, dtype=jnp.int32)
    seq_length = lengths[0]
    valid_mask = (positions < seq_length).astype(f32)
    expert_ids = jnp.arange(expert_count, dtype=jnp.int32)
    hot_sum = jnp.sum((routes[:, :, None] == expert_ids[None, None, :]).astype(f32), axis=1)
    local_counts = jnp.sum(hot_sum * valid_mask[:, None], axis=0)

    def lane_row(vector):
        return jnp.pad(vector.astype(f32), (0, tok_rows - vector.shape[0]))[None, :]

    small = jnp.concatenate(
        [routes.T.astype(f32)]
        + [lane_row(v) for v in (attn_gain, ffn_gain, kv_gain, local_counts, lengths)]
        + [jnp.zeros((16 - TOPK - 5, tok_rows), f32)],
        axis=0,
    )
    gate_parts = from_peers(expert_gate[0])
    up_parts = from_peers(expert_up[0])
    down_parts = from_peers(expert_down[0])
    small_all = gather_all(small[None])
    w_compress = gather_all(kva_weight)
    w_expand = gather_all(kvb_weight)
    w_query = gather_all(q_weight)
    w_output = gather_all(out_weight)
    w_router = gather_all(router_weight)
    gain_attn = small_all[:, TOPK, : attn_gain.shape[0]].reshape(-1)
    gain_ffn = small_all[:, TOPK + 1, : ffn_gain.shape[0]].reshape(-1)
    gain_latent = small_all[:, TOPK + 2, : kv_gain.shape[0]].reshape(-1)
    route_counts = jnp.sum(small_all[:, TOPK + 3, :expert_count], axis=0)
    all_lengths = small_all.reshape(group, peers, 16, tok_rows)[:, 0, TOPK + 4, 0]
    valid_total = jnp.sum(all_lengths)
    fill_scale = slot_total / valid_total
    plane_small = lax.dynamic_index_in_dim(
        small_all.reshape(group, peers, 16, tok_rows), fid, axis=1, keepdims=False
    )
    units = shared_gate.shape[1] // group
    pieces = jnp.concatenate(
        [
            shared_gate.reshape(-1, group, units),
            shared_up.reshape(-1, group, units),
        ],
        axis=2,
    ).transpose(1, 0, 2)
    pieces = lax.all_to_all(pieces, "expert", split_axis=0, concat_axis=0, tiled=True)
    gu_weight = jnp.roll(jnp.stack(from_peers(pieces)), fid, axis=0)
    gu_weight = gu_weight.transpose(1, 0, 2, 3).reshape(dim, 2 * units)
    gu_weight = roll_in(gu_weight, 0)
    sd_weight = jnp.roll(jnp.stack(from_peers(shared_down)), fid, axis=0).reshape(units, dim)
    sd_weight = roll_in(sd_weight, 1)
    cosine, sine_vals = rope_tables(positions)
    tokens_f = tokens.astype(f32)
    cot_plane = gather_plane(roll_in(cotangent, 1))
    normed_one, inverse_one = rms_norm(tokens_f, gain_attn)
    hidden_one = normed_one.astype(bf16)
    query_proj = jnp.dot(hidden_one, w_query, preferred_element_type=f32).reshape(
        tok_rows, H, DN + DR
    )
    query_all = jnp.concatenate(
        [
            query_proj[..., :DN],
            rotate(query_proj[..., DN:], cosine[:, None, :], sine_vals[:, None, :]),
        ],
        axis=-1,
    ).astype(bf16)
    compressed = jnp.dot(hidden_one, w_compress, preferred_element_type=f32)
    latent_raw = compressed[:, :KVR]
    latent_norm, inverse_kv = rms_norm(latent_raw, gain_latent)
    latent = latent_norm.astype(bf16)
    key_rot = rotate(compressed[:, KVR:], cosine, sine_vals).astype(bf16)
    all_latent, all_rot = (
        lax.all_gather(latent, "fsdp", axis=0, tiled=True),
        lax.all_gather(key_rot, "fsdp", axis=0, tiled=True),
    )
    keyval = jnp.dot(all_latent, w_expand, preferred_element_type=f32).astype(bf16)
    keyval = keyval.reshape(seq_len, H, DN + DV)
    key_nope = keyval[..., :DN]
    value_all = keyval[..., DN:]
    query_nope = query_all[..., :DN]
    query_rope = query_all[..., DN:]
    score_scale = (DN + DR) ** (-0.5)
    key_place = jnp.arange(seq_len, dtype=jnp.int32)
    allowed = (key_place[None, :] <= positions[:, None]) & (key_place[None, :] < seq_length)
    raw_scores = jnp.einsum(
        "thd,shd->hts", query_nope, key_nope, preferred_element_type=f32
    ) + jnp.einsum("thr,sr->hts", query_rope, all_rot, preferred_element_type=f32)
    scores = jnp.where(allowed[None], raw_scores * score_scale, masked_value)
    row_max = jnp.max(scores, axis=-1, keepdims=True)
    exp_scores = jnp.exp(scores - row_max)
    probs_attn = exp_scores / jnp.sum(exp_scores, axis=-1, keepdims=True)
    probs_low = probs_attn.astype(bf16)
    context = (
        jnp.einsum("hts,shd->thd", probs_low, value_all, preferred_element_type=f32)
        .reshape(tok_rows, H * DV)
        .astype(bf16)
    )
    residual = tokens_f + jnp.dot(context, w_output, preferred_element_type=f32)
    normed_two, inverse_two = rms_norm(residual, gain_ffn)
    hidden_two = normed_two.astype(bf16)
    hid_plane = gather_plane(roll_in(hidden_two, 1))
    router_probs = jax.nn.softmax(jnp.dot(hidden_two, w_router, preferred_element_type=f32), axis=-1)
    local_shares = jnp.sum(router_probs * valid_mask[:, None], axis=0)
    frequency = expert_count / (TOPK * valid_total) * route_counts
    d_probs_own = balance_weight * valid_mask[:, None] * frequency[None, :] / valid_total
    dlog_own = (
        router_probs * (d_probs_own - jnp.sum(router_probs * d_probs_own, axis=-1, keepdims=True))
    ).astype(bf16)
    named = jnp.any(plane_small[:, :TOPK, :] == eid.astype(f32), axis=1)
    rank = jnp.cumsum(named.astype(jnp.int32), axis=1) - 1
    slots = jnp.arange(capacity, dtype=jnp.int32)
    picker = (named[:, None, :] & (rank[:, None, :] == slots[None, :, None])).astype(bf16)
    plane_valid = (positions[None, :] < all_lengths[:, None]).astype(f32)
    plane_scale = (plane_valid * fill_scale).reshape(plane_rows, 1)
    hid3 = hid_plane.reshape(group, tok_rows, dim)
    cot3 = cot_plane.reshape(group, tok_rows, dim)
    rows_in = jnp.einsum("sji,sid->sjd", picker, hid3, preferred_element_type=f32)
    rows_in = rows_in.astype(bf16).reshape(pairs, dim)
    rows_cot = jnp.einsum("sji,sid->sjd", picker, cot3, preferred_element_type=f32)
    rows_cot = rows_cot.astype(bf16).reshape(pairs, dim)
    rows_scale = fill_scale * jnp.sum(
        picker.astype(f32) * plane_valid[:, None, :], axis=-1
    ).reshape(pairs, 1)
    w_router_in = roll_in(w_router, 0)
    probs_rows = jax.nn.softmax(jnp.dot(rows_in, w_router_in, preferred_element_type=f32), axis=-1)
    own_expert = (expert_ids == eid).astype(f32)[None, :]
    gate_rows = jnp.sum(probs_rows * own_expert, axis=-1, keepdims=True)

    def cut(array, r):
        return array[:, r * half : (r + 1) * half]

    def summed(term):
        total = term(0)
        for r in range(1, peers):
            total = total + term(r)
        return total

    hidden_g = summed(lambda r: jnp.dot(cut(rows_in, r), gate_parts[r], preferred_element_type=f32))
    hidden_u = summed(lambda r: jnp.dot(cut(rows_in, r), up_parts[r], preferred_element_type=f32))
    act = (jax.nn.silu(hidden_g) * hidden_u).astype(bf16)
    out_rows = jnp.concatenate(
        [jnp.dot(act, w, preferred_element_type=f32).astype(bf16) for w in down_parts], axis=1
    )
    d_gate = rows_scale * jnp.sum(
        rows_cot.astype(f32) * out_rows.astype(f32), axis=-1, keepdims=True
    )
    weighted = (gate_rows * out_rows.astype(f32)).astype(bf16)
    d_out = (gate_rows * rows_scale * rows_cot.astype(f32)).astype(bf16)
    d_act = summed(
        lambda r: lax.dot_general(
            cut(d_out, r), down_parts[r], (((1,), (1,)), ((), ())), preferred_element_type=f32
        )
    )
    d_hidden_g = (d_act * hidden_u * silu_slope(hidden_g)).astype(bf16)
    d_hidden_u = (d_act * jax.nn.silu(hidden_g)).astype(bf16)

    def outer(left, right):
        return lax.dot_general(left, right, (((0,), (0,)), ((), ())), preferred_element_type=f32)

    def with_peers(term):
        arrived = sum_to_peers(lambda r: term(r).astype(bf16))
        total = term(0)
        for block in arrived:
            total = total + block.astype(f32)
        return total

    egate_grad = with_peers(lambda r: outer(cut(rows_in, r), d_hidden_g))[None]
    eup_grad = with_peers(lambda r: outer(cut(rows_in, r), d_hidden_u))[None]
    edown_grad = with_peers(lambda r: outer(act, cut(d_out, r)))[None]
    dlog_rows = (gate_rows * d_gate * (own_expert - probs_rows)).astype(bf16)

    def back(left, weight):
        return lax.dot_general(left, weight, (((1,), (1,)), ((), ())), preferred_element_type=f32)

    d_rows = jnp.concatenate(
        [back(d_hidden_g, gate_parts[r]) + back(d_hidden_u, up_parts[r]) for r in range(peers)],
        axis=1,
    )
    d_rows = (d_rows + back(dlog_rows, w_router_in)).astype(bf16)
    gu = jnp.dot(hid_plane, gu_weight, preferred_element_type=f32)
    shared_g, shared_u = gu[:, :units], gu[:, units:]
    shared_act = jax.nn.silu(shared_g) * shared_u
    d_shared_act = back(cot_plane, sd_weight) * plane_scale
    d_gu = jnp.concatenate(
        [
            d_shared_act * shared_u * silu_slope(shared_g),
            d_shared_act * jax.nn.silu(shared_g),
        ],
        axis=1,
    ).astype(bf16)
    shared_low = shared_act.astype(bf16)
    d_sd = outer((shared_act * plane_scale).astype(bf16), cot_plane)
    d_gu_weight = outer(hid_plane, d_gu)
    out_part = jnp.einsum(
        "sji,sjd->sid", picker, weighted.reshape(group, capacity, dim), preferred_element_type=f32
    ).reshape(plane_rows, dim) + jnp.dot(shared_low, sd_weight, preferred_element_type=f32)
    back_part = jnp.einsum(
        "sji,sjd->sid", picker, d_rows.reshape(group, capacity, dim), preferred_element_type=f32
    ).reshape(plane_rows, dim) + back(d_gu, gu_weight)
    d_hidden_two = scatter_plane(back_part.astype(bf16))
    out_sum = scatter_plane(out_part.astype(bf16))
    mixed = (residual + roll_out(out_sum, 1).astype(f32)).astype(bf16)
    d_hidden_two = roll_out(d_hidden_two, 1).astype(f32) + back(dlog_own, w_router)
    router_grad = roll_out(outer(rows_in, dlog_rows), 0) + outer(hidden_two, dlog_own)
    d_gu_blocks = roll_out(d_gu_weight, 0).reshape(group, peers, dim // (group * peers), 2 * units)

    def gu_term(r):
        return lax.dynamic_index_in_dim(d_gu_blocks, (fid + r) % peers, axis=1, keepdims=False)

    gu_sum = gu_term(0)
    for block in sum_to_peers(gu_term):
        gu_sum = gu_sum + block
    gu_sum = lax.all_to_all(gu_sum, "expert", split_axis=0, concat_axis=0, tiled=True)
    gu_sum = gu_sum.transpose(1, 0, 2)
    sgate_grad = gu_sum[:, :, :units].reshape(shared_gate.shape)
    sup_grad = gu_sum[:, :, units:].reshape(shared_up.shape)
    d_sd_blocks = roll_out(d_sd, 1).reshape(peers, units // peers, dim)

    def sd_term(r):
        return lax.dynamic_index_in_dim(d_sd_blocks, (fid + r) % peers, axis=0, keepdims=False)

    sdown_grad = sd_term(0)
    for block in sum_to_peers(sd_term):
        sdown_grad = sdown_grad + block
    grad_out = cotangent.astype(f32) * (valid_mask * fill_scale)[:, None]
    d_residual, d_ffn_gain = norm_back(d_hidden_two, residual, inverse_two, gain_ffn)
    d_residual = d_residual + grad_out
    d_residual_low = d_residual.astype(bf16)
    d_output_w = outer(context, d_residual_low)
    d_context = back(d_residual_low, w_output).astype(bf16).reshape(tok_rows, H, DV)
    d_value = jnp.einsum("hts,thd->shd", probs_low, d_context, preferred_element_type=f32)
    d_weights = jnp.einsum("thd,shd->hts", d_context, value_all, preferred_element_type=f32)
    d_scores = (
        probs_attn * (d_weights - jnp.sum(probs_attn * d_weights, axis=-1, keepdims=True))
    ).astype(bf16)
    d_query_nope = score_scale * jnp.einsum(
        "hts,shd->thd", d_scores, key_nope, preferred_element_type=f32
    )
    d_query_rope = score_scale * jnp.einsum(
        "hts,sr->thr", d_scores, all_rot, preferred_element_type=f32
    )
    d_key_nope = score_scale * jnp.einsum(
        "hts,thd->shd", d_scores, query_nope, preferred_element_type=f32
    )
    d_key_rot = score_scale * jnp.einsum(
        "hts,thr->sr", d_scores, query_rope, preferred_element_type=f32
    )
    d_keyval_all = jnp.concatenate([d_key_nope, d_value], axis=-1).reshape(
        peers, tok_rows, H * (DN + DV)
    )
    d_key_rot = d_key_rot.reshape(peers, tok_rows, DR)

    def own_rows(array, r):
        return lax.dynamic_index_in_dim(array, (fid + r) % peers, axis=0, keepdims=False)

    own_dkeyval = with_peers(lambda r: own_rows(d_keyval_all, r))
    own_dkeyrot = with_peers(lambda r: own_rows(d_key_rot, r))
    d_keyval = own_dkeyval.astype(bf16)
    d_expand_w = outer(latent, d_keyval)
    d_latent = back(d_keyval, w_expand)
    d_latent_raw, d_latent_gain = norm_back(d_latent, latent_raw, inverse_kv, gain_latent)
    d_compressed = jnp.concatenate(
        [d_latent_raw, rotate_back(own_dkeyrot, cosine, sine_vals)], axis=-1
    ).astype(bf16)
    d_compress_w = outer(hidden_one, d_compressed)
    d_query = (
        jnp.concatenate(
            [d_query_nope, rotate_back(d_query_rope, cosine[:, None, :], sine_vals[:, None, :])],
            axis=-1,
        )
        .reshape(tok_rows, H * (DN + DR))
        .astype(bf16)
    )
    d_query_w = outer(hidden_one, d_query)
    d_hidden_one = back(d_query, w_query) + back(d_compressed, w_compress)
    d_tokens, d_attn_gain = norm_back(d_hidden_one, tokens_f, inverse_one, gain_attn)
    tokens_grad = d_tokens + d_residual
    smalls = lax.psum(
        jnp.concatenate([d_attn_gain, d_latent_gain, d_ffn_gain, local_shares]), ("expert", "fsdp")
    )
    device = eid * peers + fid

    def own_piece(start, size):
        count = size // (group * peers)
        return lax.dynamic_slice(smalls, (start + device * count,), (count,))

    attn_gain_grad = own_piece(0, dim)
    kv_gain_grad = own_piece(dim, KVR)
    ffn_gain_grad = own_piece(dim + KVR, dim)
    share_sums = smalls[2 * dim + KVR :]
    balance = jnp.sum(frequency * (share_sums / valid_total))
    return (
        mixed,
        tokens_grad,
        balance,
        attn_gain_grad,
        scatter_all(d_query_w),
        scatter_all(d_compress_w),
        kv_gain_grad,
        scatter_all(d_expand_w),
        scatter_all(d_output_w),
        ffn_gain_grad,
        scatter_all(router_grad),
        sgate_grad,
        sup_grad,
        sdown_grad,
        egate_grad,
        eup_grad,
        edown_grad,
    )


def solution(mesh):
    return jax.shard_map(
        body,
        mesh=mesh,
        in_specs=(
            P(("expert", "fsdp"), None),
            P(("expert", "fsdp"), None),
            P(("expert", "fsdp"), None),
            P("expert"),
            P(("expert", "fsdp")),
            P(("expert", "fsdp"), None),
            P(("expert", "fsdp"), None),
            P(("expert", "fsdp")),
            P(("expert", "fsdp"), None),
            P(("expert", "fsdp"), None),
            P(("expert", "fsdp")),
            P(("expert", "fsdp"), None),
            P(("expert", "fsdp"), None),
            P(("expert", "fsdp"), None),
            P(("expert", "fsdp"), None),
            P("expert", "fsdp", None),
            P("expert", "fsdp", None),
            P("expert", None, "fsdp"),
        ),
        out_specs=(
            P(("expert", "fsdp"), None),
            P(("expert", "fsdp"), None),
            P(),
            P(("expert", "fsdp")),
            P(("expert", "fsdp"), None),
            P(("expert", "fsdp"), None),
            P(("expert", "fsdp")),
            P(("expert", "fsdp"), None),
            P(("expert", "fsdp"), None),
            P(("expert", "fsdp")),
            P(("expert", "fsdp"), None),
            P(("expert", "fsdp"), None),
            P(("expert", "fsdp"), None),
            P(("expert", "fsdp"), None),
            P("expert", "fsdp", None),
            P("expert", "fsdp", None),
            P("expert", None, "fsdp"),
        ),
        check_vma=False,
    )
```

time: 3050 us -> 1770 us (0.58)
  waiting for transfers between devices: 1750 us -> 965 us
  blocking collectives: 782 us -> 360 us
  starting transfers between devices: 108 us -> 22.9 us
  matrix products: 235 us -> 291 us
  local copies, waits for them, and re-layouts: 117 us -> 61.5 us
    reduce_scatter x9 -> x6, waiting for transfers between devices: 1370 us -> 420 us  [the longest x4 248 us: scatter_all(): lax.psum_scatter(partial.astype(jnp.bfloat16), ('expert', 'fsdp'), scatte...]
    unnamed x2 -> x0, blocking collectives: 479 us -> none
    ppermute x0 -> x12, waiting for transfers between devices: none -> 341 us  [the longest x7 341 us: sum_to_peers(): lax.ppermute(term(r), 'fsdp', [(j, (j + r) % size) for j in range(size)])]
    all_gather x1 -> x2, blocking collectives: 78.3 us -> 308 us  [gather_all(): return lax.all_gather(shard, ('expert', 'fsdp'), axis=0, tiled=True)]
    psum x3 -> x1, blocking collectives: 213 us -> 39.3 us  [body(): lax.psum(jnp.concatenate([d_attn_gain, d_latent_gain, d_ffn_gain, local_s...]
    all_to_all x4 -> x2, waiting for transfers between devices: 147 us -> 17.4 us  [the longest x1 17.4 us: body(): lax.all_to_all(pieces, 'expert', split_axis=0, concat_axis=0, tiled=True)]
    all_to_all x4 -> x2, starting transfers between devices: 80.8 us -> 8.2 us  [the longest x1 4.63 us: body(): lax.all_to_all(gu_sum, 'expert', split_axis=0, concat_axis=0, tiled=True)]
    dot_general x45 -> x55, matrix products: 233 us -> 291 us  [the longest x14 75.1 us: outer(): lax.dot_general(left, right, (((0,), (0,)), ((), ())), preferred_element_...]
  transfers between devices with their start and end apart: 29 -> 27, of which waited for: 13 -> 11; matrix products, arithmetic and copies ran while one was open for 26% -> 17% of each run, Pallas kernels for 0% -> 0%
where the time goes in v1:
time: 1770 us; the launch traced here: 1760 us
  waiting for transfers between devices  965 us (55%)
  blocking collectives  360 us (20%)
  matrix products  291 us (16%)
  local copies, waits for them, and re-layouts  61.5 us (3%)
  other arithmetic  42.3 us (2%)
  starting transfers between devices  22.9 us (1%)
  between operations  18 us (1%)
    ppermute x7, waiting for transfers between devices, sum_to_peers(): lax.ppermute(term(r), 'fsdp', [(j, (j + r) % size) for j in range(size)])  341 us
    all_gather x2, blocking collectives, gather_all(): return lax.all_gather(shard, ('expert', 'fsdp'), axis=0, tiled=True)  308 us
    reduce_scatter x4, waiting for transfers between devices, scatter_all(): lax.psum_scatter(partial.astype(jnp.bfloat16), ('expert', 'fsdp'), scatte...  248 us
    all_gather x4, waiting for transfers between devices, gather_all(): return lax.all_gather(shard, ('expert', 'fsdp'), axis=0, tiled=True)  183 us
    reduce_scatter x2, waiting for transfers between devices, scatter_plane(): return lax.psum_scatter(partial, 'expert', scatter_dimension=0, tiled=True)  172 us
    dot_general x14, matrix products, outer(): lax.dot_general(left, right, (((0,), (0,)), ((), ())), preferred_element_...  75.1 us
    dot_general x12, matrix products, back(): lax.dot_general(left, weight, (((1,), (1,)), ((), ())), preferred_element...  63.3 us
    psum x1, blocking collectives, body(): lax.psum(jnp.concatenate([d_attn_gain, d_latent_gain, d_ffn_gain, local_s...  39.3 us
  transfers between devices with their start and end apart: 27, of which 11 were waited for; matrix products, arithmetic and copies ran while one was open for 17% of the time, Pallas kernels for 0%

profile of v1, /device:TPU:0, one launch (start us, length us, event | category | flops | bytes accessed | tf_op | source)
XLA Modules:
  0.0 1760.6 jit_solution(13204872315375965156)
XLA Ops:
  15.8 71.8 %all-gather = f32[512,128]{1,0:T(8,128)S(1)} all-gather(f32[16,128]{1,0:T(8,128)S(1)} %concatenate.82), channel_id=2, replica_groups=mesh['expert'=16,'fsdp'=2] {'expert','fsdp'}, dimensions={0}, use_global_device_ids=true | all-gather | bytes 270336 | tf_op jit(solution)/shard_map/all_gather | solution.py:73
  98.3 8.0 all_gather.32
  106.3 29.9 %all-gather.11.cloned.1.call-done = bf16[512,4096]{1,0:T(8,128)(2,1)} async-done(((bf16[16,4096]{1,0:T(8,128)(2,1)}), bf16[512,4096]{1,0:T(8,128)(2,1)}) %all-gather.11.cloned.1.call-update) | async-done | bytes 4194320 | tf_op jit(solution)/shard_map/all_gather | solution.py:73
  142.5 91.2 %all-gather.13.cloned.1.call-done = bf16[2048,3072]{1,0:T(8,128)(2,1)} async-done(((bf16[64,3072]{1,0:T(8,128)(2,1)}), bf16[2048,3072]{1,0:T(8,128)(2,1)}) %all-gather.13.cloned.1.call-update) | async-done | bytes 12582928 | tf_op jit(solution)/shard_map/all_gather | solution.py:73
  233.7 8.1 fusion.153
  250.0 62.3 %all-gather.15.cloned.1.call-done = bf16[2048,2048]{1,0:T(8,128)(2,1)} async-done(((bf16[64,2048]{1,0:T(8,128)(2,1)}), bf16[2048,2048]{1,0:T(8,128)(2,1)}) %all-gather.15.cloned.1.call-update) | async-done | bytes 8388624 | tf_op jit(solution)/shard_map/all_gather | solution.py:73
  332.9 17.4 all-to-all-done
  351.5 236.4 %all-gather.1 = bf16[32,64,16]{1,2,0:T(8,128)(2,1)S(1)} all-gather(bf16[1,64,16]{1,2,0:T(8,128)(2,1)S(1)} %bitcast.251), channel_id=1, replica_groups=mesh['expert'=16,'fsdp'=2] {'expert','fsdp'}, dimensions={0}, use_global_device_ids=true | all-gather | bytes 67584 | tf_op jit(solution)/shard_map/all_gather | solution.py:73
  590.2 7.9 convert_convert_fusion
  629.5 8.0 convolution_add_fusion
  637.5 13.2 multiply_convert_fusion.1
  694.4 10.4 fusion.69
  720.1 9.5 fusion.1
  730.1 11.8 fusion.8
  741.9 12.9 fusion.2
  762.6 67.7 %reduce-scatter.12.cloned.1.call-done = bf16[128,2048]{1,0:T(8,128)(2,1)} async-done(((bf16[2048,2048]{1,0:T(8,128)(2,1)}), bf16[128,2048]{1,0:T(8,128)(2,1)}) %reduce-scatter.12.cloned.1.call-update) | async-done | bytes 524304 | tf_op jit(solution)/shard_map/reduce_scatter | solution.py:87
  834.2 104.5 %reduce-scatter.10.cloned.1.call-done = bf16[128,2048]{1,0:T(8,128)(2,1)} async-done(((bf16[2048,2048]{1,0:T(8,128)(2,1)}), bf16[128,2048]{1,0:T(8,128)(2,1)}) %reduce-scatter.10.cloned.1.call-update) | async-done | bytes 524304 | tf_op jit(solution)/shard_map/reduce_scatter | solution.py:87
  994.9 14.7 collective-permute-done.6
  1052.5 7.9 convolution_convert_fusion.4
  1096.2 319.7 %collective-permute-done.8 = f32[44,2048]{1,0:T(8,128)} collective-permute-done((f32[44,2048]{1,0:T(8,128)}, f32[44,2048]{1,0:T(8,128)}, u32[]{:S(2)}, u32[]{:S(2)}) %collective-permute-start.8) | collective-permute-done | bytes 360480 | tf_op jit(solution)/shard_map/ppermute | solution.py:101
  1423.8 9.2 add_bitcast_fusion
  1455.6 39.3 %psum.7 = f32[4624]{0:T(1024)S(1)} all-reduce(f32[4624]{0:T(1024)S(1)} %pad_maximum_fusion.13), channel_id=1, replica_groups=mesh['expert'=16,'fsdp'=2] {'expert','fsdp'}, use_global_device_ids=true, to_apply=%region_29.31 | all-reduce | flops 4624 | bytes 36992 | tf_op jit(solution)/shard_map/psum | solution.py:422
  1502.0 86.6 %reduce-scatter.20.cloned.1.call-done = bf16[64,2048]{1,0:T(8,128)(2,1)} async-done(((bf16[2048,2048]{1,0:T(8,128)(2,1)}), bf16[64,2048]{1,0:T(8,128)(2,1)}) %reduce-scatter.20.cloned.1.call-update) | async-done | bytes 262160 | tf_op jit(solution)/shard_map/reduce_scatter | solution.py:81
  1590.4 161.2 %reduce-scatter.14.cloned.1.call-done = bf16[64,3072]{1,0:T(8,128)(2,1)} async-done(((bf16[2048,3072]{1,0:T(8,128)(2,1)}), bf16[64,3072]{1,0:T(8,128)(2,1)}) %reduce-scatter.14.cloned.1.call-update) | async-done | bytes 393232 | tf_op jit(solution)/shard_map/reduce_scatter | solution.py:81
  (409 shorter events, 333.0 us)
Async XLA Ops:
  7.2 82.2 %all-gather.9.cloned.1.call-start = ((), (), s32[]{:S(2)}) async-start(), calls=%async_computation.9 | async-start | bytes 2703360 | tf_op jit(solution)/shard_map/all_gather | solution.py:73
  7.9 128.3 %all-gather.11.cloned.1.call-start = ((), (), s32[]{:S(2)}) async-start(), calls=%async_computation.10 | async-start | bytes 4325376 | tf_op jit(solution)/shard_map/all_gather | solution.py:73
  8.7 225.0 %all-gather.13.cloned.1.call-start = ((), (), s32[]{:S(2)}) async-start(), calls=%async_computation.11 | async-start | bytes 12976128 | tf_op jit(solution)/shard_map/all_gather | solution.py:73
  9.4 302.8 %all-gather.15.cloned.1.call-start = ((), (), s32[]{:S(2)}) async-start(), calls=%async_computation.12 | async-start | bytes 8650752 | tf_op jit(solution)/shard_map/all_gather | solution.py:73
  10.0 580.2 %all-gather.19.cloned.1.call-start = ((), (), s32[]{:S(2)}) async-start(), calls=%async_computation.15 | async-start | bytes 8912896 | tf_op jit(solution)/shard_map/all_gather | solution.py:77
  12.1 586.0 %all-gather.17.cloned.1.call-start = ((), (), s32[]{:S(2)}) async-start(), calls=%async_computation.13 | async-start | bytes 8912896 | tf_op jit(solution)/shard_map/all_gather | solution.py:77
  320.0 268.3 %collective-permute-start.4 = (bf16[44,2048]{1,0:T(8,128)(2,1)S(1)}, bf16[44,2048]{1,0:T(8,128)(2,1)S(1)}, u32[]{:S(2)}, u32[]{:S(2)}) collective-permute-start(bf16[44,2048]{1,0:T(8,128)(2,1)S(1)} %copy-done.41), channel_id=1, source_target_pairs={{0,1},{1,0},{2,3},{3,2},{4,5},{5,4},{6,7},{7,6},{8,9},{9,8},{10,11... | collective-permute-start | bytes 540680 | tf_op jit(solution)/shard_map/ppermute | solution.py:93
  327.3 503.0 %reduce-scatter.12.cloned.1.call-start = ((), (), s32[]{:S(2)}) async-start(), calls=%async_computation.16 | async-start | bytes 8912896 | tf_op jit(solution)/shard_map/reduce_scatter | solution.py:87
  327.3 302.2 %collective-permute-start.2 = (bf16[1408,1024]{1,0:T(8,128)(2,1)}, bf16[1408,1024]{1,0:T(8,128)(2,1)}, u32[]{:S(2)}, u32[]{:S(2)}) collective-permute-start(bf16[1408,1024]{1,0:T(8,128)(2,1)} %bitcast.252), channel_id=1, source_target_pairs={{0,1},{1,0},{2,3},{3,2},{4,5},{5,4},{6,7},{7,6},{8,9},{9,8},{10,11... | collective-permute-start | bytes 8650760 | tf_op jit(solution)/shard_map/ppermute | solution.py:93
  328.6 293.8 %collective-permute-start.1 = (bf16[1024,1408]{1,0:T(8,128)(2,1)}, bf16[1024,1408]{1,0:T(8,128)(2,1)}, u32[]{:S(2)}, u32[]{:S(2)}) collective-permute-start(bf16[1024,1408]{1,0:T(8,128)(2,1)} %bitcast.254), channel_id=1, source_target_pairs={{0,1},{1,0},{2,3},{3,2},{4,5},{5,4},{6,7},{7,6},{8,9},{9,8},{10,11... | collective-permute-start | bytes 8650760 | tf_op jit(solution)/shard_map/ppermute | solution.py:93
  329.4 308.1 %collective-permute-start = (bf16[1024,1408]{1,0:T(8,128)(2,1)}, bf16[1024,1408]{1,0:T(8,128)(2,1)}, u32[]{:S(2)}, u32[]{:S(2)}) collective-permute-start(bf16[1024,1408]{1,0:T(8,128)(2,1)} %bitcast.253), channel_id=1, source_target_pairs={{0,1},{1,0},{2,3},{3,2},{4,5},{5,4},{6,7},{7,6},{8,9},{9,8},{10,11... | collective-permute-start | bytes 8650760 | tf_op jit(solution)/shard_map/ppermute | solution.py:93
  350.2 239.1 %collective-permute-start.3 = (bf16[16,64,176]{2,1,0:T(8,128)(2,1)S(1)}, bf16[16,64,176]{2,1,0:T(8,128)(2,1)S(1)}, u32[]{:S(2)}, u32[]{:S(2)}) collective-permute-start(bf16[16,64,176]{2,1,0:T(8,128)(2,1)S(1)} %all-to-all-done), channel_id=1, source_target_pairs={{0,1},{1,0},{2,3},{3,2},{4,5},{5,4},{6,7},{7,6},{8,9},{9,8},{10,11... | collective-permute-start | bytes 1081352 | tf_op jit(solution)/shard_map/ppermute | solution.py:93
  729.6 209.1 %reduce-scatter.10.cloned.1.call-start = ((), (), s32[]{:S(2)}) async-start(), calls=%async_computation.14 | async-start | bytes 8912896 | tf_op jit(solution)/shard_map/reduce_scatter | solution.py:87
  754.8 339.9 %reduce-scatter.22.cloned.1.call-start = ((), (), s32[]{:S(2)}) async-start(), calls=%async_computation.21 | async-start | bytes 540672
  762.5 736.3 %reduce-scatter.16.cloned.1.call-start = ((), (), s32[]{:S(2)}) async-start(), calls=%async_computation.18 | async-start | bytes 2703360 | tf_op jit(solution)/shard_map/reduce_scatter | solution.py:81
  982.0 27.9 %collective-permute-start.5 = (bf16[128,4096]{1,0:T(8,128)(2,1)}, bf16[128,4096]{1,0:T(8,128)(2,1)}, u32[]{:S(2)}, u32[]{:S(2)}) collective-permute-start(bf16[128,4096]{1,0:T(8,128)(2,1)} %bitcast.236), channel_id=1, source_target_pairs={{0,1},{1,0},{2,3},{3,2},{4,5},{5,4},{6,7},{7,6},{8,9},{9,8},{10,11... | collective-permute-start | bytes 3145736 | tf_op jit(solution)/shard_map/ppermute | solution.py:101
  1017.7 482.7 %reduce-scatter.18.cloned.1.call-start = ((), (), s32[]{:S(2)}) async-start(), calls=%async_computation.19 | async-start | bytes 4325376 | tf_op jit(solution)/shard_map/reduce_scatter | solution.py:81
  1022.9 565.8 %reduce-scatter.20.cloned.1.call-start = ((), (), s32[]{:S(2)}) async-start(), calls=%async_computation.20 | async-start | bytes 8650752 | tf_op jit(solution)/shard_map/reduce_scatter | solution.py:81
  1029.6 722.0 %reduce-scatter.14.cloned.1.call-start = ((), (), s32[]{:S(2)}) async-start(), calls=%async_computation.17 | async-start | bytes 12976128 | tf_op jit(solution)/shard_map/reduce_scatter | solution.py:81
  1060.4 363.3 %collective-permute-start.11 = (bf16[1408,1024]{1,0:T(8,128)(2,1)}, bf16[1408,1024]{1,0:T(8,128)(2,1)}, u32[]{:S(2)}, u32[]{:S(2)}) collective-permute-start(bf16[1408,1024]{1,0:T(8,128)(2,1)} %convolution_convert_fusion.4), channel_id=1, source_target_pairs={{0,1},{1,0},{2,3},{3,2},{4,5},{5,4},{6,7},{7,6},{8,9},{9,8},{10,11... | collective-permute-start | bytes 8650760 | tf_op jit(solution)/shard_map/ppermute | solution.py:101
  1065.6 367.4 %collective-permute-start.10 = (bf16[1024,1408]{1,0:T(8,128)(2,1)}, bf16[1024,1408]{1,0:T(8,128)(2,1)}, u32[]{:S(2)}, u32[]{:S(2)}) collective-permute-start(bf16[1024,1408]{1,0:T(8,128)(2,1)} %convolution_convert_fusion.5), channel_id=1, source_target_pairs={{0,1},{1,0},{2,3},{3,2},{4,5},{5,4},{6,7},{7,6},{8,9},{9,8},{10,11... | collective-permute-start | bytes 8650760 | tf_op jit(solution)/shard_map/ppermute | solution.py:101
  1079.8 337.9 %all-to-all-start.1 = ((f32[16,64,176]{2,1,0:T(8,128)}), f32[16,64,176]{2,1,0:T(8,128)}, u32[]{:S(2)}, u32[]{:S(2)}) async-start(f32[16,64,176]{2,1,0:T(8,128)} %bitcast_add_fusion.4), calls=%async_computation.7 | async-start | bytes 2097152 | tf_op jit(solution)/shard_map/all_to_all | solution.py:357
  1091.9 348.0 %collective-permute-start.9 = (bf16[1024,1408]{1,0:T(8,128)(2,1)}, bf16[1024,1408]{1,0:T(8,128)(2,1)}, u32[]{:S(2)}, u32[]{:S(2)}) collective-permute-start(bf16[1024,1408]{1,0:T(8,128)(2,1)} %convolution_convert_fusion.6), channel_id=1, source_target_pairs={{0,1},{1,0},{2,3},{3,2},{4,5},{5,4},{6,7},{7,6},{8,9},{9,8},{10,11... | collective-permute-start | bytes 8650760 | tf_op jit(solution)/shard_map/ppermute | solution.py:101
  1094.4 321.5 %collective-permute-start.8 = (f32[44,2048]{1,0:T(8,128)}, f32[44,2048]{1,0:T(8,128)}, u32[]{:S(2)}, u32[]{:S(2)}) collective-permute-start(f32[44,2048]{1,0:T(8,128)} %dynamic-slice_bitcast_fusion.1), channel_id=1, source_target_pairs={{0,1},{1,0},{2,3},{3,2},{4,5},{5,4},{6,7},{7,6},{8,9},{9,8},{10,11... | collective-permute-start | bytes 1081352 | tf_op jit(solution)/shard_map/ppermute | solution.py:101
  (97 other events, 2822.0 us)
Sparse Core Ops, SparseCore 0:
  10.9 61.4 all-gather.8
  75.4 60.7 all-gather.10
  139.1 94.5 all-gather.12
  236.5 75.6 all-gather.14
  314.8 84.6 all-gather.18
  402.0 73.1 all-gather.16
  729.7 100.4 reduce-scatter.11
  834.3 104.3 reduce-scatter.9
  941.5 134.9 reduce-scatter.21
  1078.7 137.6 reduce-scatter.15
  1218.8 181.9 reduce-scatter.17
  1403.0 185.6 reduce-scatter.19
  1595.7 155.8 reduce-scatter.13

commit v2 on v1

--- a/solution.py
+++ b/solution.py
@@ -1,6 +1,10 @@
+import functools
+
 import jax
 import jax.numpy as jnp
 from jax import lax
+from jax.experimental import pallas as pl
+from jax.experimental.pallas import tpu as pltpu
 from jax.sharding import PartitionSpec as P
 
 D = 2048
@@ -69,22 +73,660 @@
     return sigmoid_vals * (1.0 + vector * (1.0 - sigmoid_vals))
 
 
-def gather_all(shard):
-    return lax.all_gather(shard, ("expert", "fsdp"), axis=0, tiled=True)
-
-
-def gather_plane(shard):
-    return lax.all_gather(shard, "expert", axis=0, tiled=True)
-
-
-def scatter_all(partial):
-    return lax.psum_scatter(
-        partial.astype(jnp.bfloat16), ("expert", "fsdp"), scatter_dimension=0, tiled=True
-    ).astype(jnp.float32)
-
-
-def scatter_plane(partial):
-    return lax.psum_scatter(partial, "expert", scatter_dimension=0, tiled=True)
+MESH_IDS = pl.DeviceIdType.MESH
+
+
+class Place:
+    def __init__(self, group, peers, wide):
+        self.wide = wide
+        self.depth = min(4, group // 2)
+        self.tall = group // 2 // self.depth
+        self.across = peers if wide else 1
+        self.peers = peers
+        self.units = self.depth * self.tall * self.across
+        self.slots = 2 * self.units
+
+    def here(self):
+        e = lax.axis_index("expert")
+        self.fsdp = lax.axis_index("fsdp")
+        self.c = e % 2
+        self.y = e // 2 % self.tall
+        self.z = e // (2 * self.tall)
+        self.x = self.fsdp if self.wide else 0
+        return self
+
+    def slot(self, z, y, c, x):
+        return ((z * self.tall + y) * 2 + c) * self.across + x
+
+    def device(self, z, y, c, x=None):
+        return ((z * self.tall + y) * 2 + c, self.fsdp if x is None else x)
+
+    def greet(self, swapping):
+        barrier = pltpu.get_barrier_semaphore()
+        partners = self.peers if swapping or self.wide else 1
+        count = 1 + (self.tall - 1) + (partners - 1)
+
+        def signal(target):
+            pl.semaphore_signal(barrier, inc=1, device_id=target, device_id_type=MESH_IDS)
+
+        signal(self.device(self.z, self.y, 1 - self.c))
+        for k in range(1, self.tall):
+            signal(self.device(self.z, (self.y + k) % self.tall, self.c))
+        for k in range(1, partners):
+            signal(self.device(self.z, self.y, self.c, (self.fsdp + k) % self.peers))
+
+        @pl.when(self.z > 0)
+        def _():
+            signal(self.device(self.z - 1, self.y, self.c))
+
+        @pl.when(self.z < self.depth - 1)
+        def _():
+            signal(self.device(self.z + 1, self.y, self.c))
+
+        last = self.depth - 1
+        pl.semaphore_wait(barrier, count + 2 - self.z // last - (last - self.z) // last)
+
+
+def remote(src, dst, send_sem, recv_sem, target):
+    return pltpu.make_async_remote_copy(
+        src_ref=src,
+        dst_ref=dst,
+        send_sem=send_sem,
+        recv_sem=recv_sem,
+        device_id=target,
+        device_id_type=MESH_IDS,
+    )
+
+
+class Swaps:
+    def __init__(self, place, shifts, given, taken, send_sem, recv_sem):
+        self.copies = [
+            remote(
+                given[i],
+                taken[i],
+                send_sem.at[i],
+                recv_sem.at[i],
+                place.device(place.z, place.y, place.c, (place.fsdp + shift) % place.peers),
+            )
+            for i, shift in enumerate(shifts)
+        ]
+
+    def start(self):
+        for copy in self.copies:
+            copy.start()
+
+    def wait(self):
+        for copy in self.copies:
+            copy.wait()
+
+
+def gather_kernel(place, count, shifts, *refs):
+    total = count + len(shifts)
+    ins, outs = refs[:count], refs[total : total + count]
+    given, taken = refs[count:total], refs[total + count : 2 * total]
+    near, xs, ys, cs, rc, zs, got, given_sem, taken_sem = refs[2 * total :]
+    p = place.here()
+    depth, tall, across = p.depth, p.tall, p.across
+    p.greet(len(shifts) > 0)
+    sibling = p.device(p.z, p.y, 1 - p.c)
+
+    def unit(z, y, x):
+        return (z * tall + y) * across + x
+
+    def block(a, z, y, x):
+        return outs[a].at[p.slot(z, y, p.c, x)]
+
+    def to_z(a, src, z, x, way):
+        return remote(
+            src,
+            block(a, z, p.y, x),
+            zs.at[a, way, z * across + x],
+            got.at[a, unit(z, p.y, x)],
+            p.device(p.z + 2 * way - 1, p.y, p.c),
+        )
+
+    def to_y(a, src, z, x, k):
+        return remote(
+            src,
+            block(a, z, p.y, x),
+            ys.at[a],
+            got.at[a, unit(z, p.y, x)],
+            p.device(p.z, (p.y + k) % tall, p.c),
+        )
+
+    def to_sibling(a, src, z, y, x):
+        return remote(src, block(a, z, y, x), cs.at[a], rc.at[a], sibling)
+
+    def arrived(a, z, y, x):
+        remote(block(a, z, y, x), block(a, z, y, x), cs.at[a], got.at[a, unit(z, y, x)], sibling).wait_recv()
+
+    def spread(a, src, z, x, ways):
+        for way in ways:
+
+            @pl.when((p.z < depth - 1) if way else (p.z > 0))
+            def _():
+                to_z(a, src, z, x, way).start()
+
+        for k in range(1, tall):
+            to_y(a, src, z, x, k).start()
+        to_sibling(a, src, z, p.y, x).start()
+
+    def over_x(step):
+        if across == 1:
+            step(0)
+        else:
+            lax.fori_loop(0, across, lambda k, _: (step((p.x + k) % across), 0)[1], 0)
+
+    for a in range(count):
+        for k in range(1, across):
+            remote(
+                ins[a],
+                block(a, p.z, p.y, p.x),
+                xs.at[a],
+                got.at[a, unit(p.z, p.y, p.x)],
+                p.device(p.z, p.y, p.c, (p.x + k) % across),
+            ).start()
+        spread(a, ins[a], p.z, p.x, (0, 1))
+        pltpu.make_async_copy(ins[a], block(a, p.z, p.y, p.x), near.at[a]).start()
+
+    swaps = Swaps(p, shifts, given, taken, given_sem, taken_sem)
+    swaps.start()
+    for k in range(1, across):
+        x = (p.x + k) % across
+        for a in range(count):
+            arrived(a, p.z, p.y, x)
+            spread(a, block(a, p.z, p.y, x), p.z, x, (0, 1))
+
+    def from_y(z):
+        def step(x):
+            for k in range(1, tall):
+                y = (p.y + k) % tall
+                for a in range(count):
+                    arrived(a, z, y, x)
+                    to_sibling(a, block(a, z, y, x), z, y, x).start()
+
+        over_x(step)
+
+    for d in range(1, depth + 1):
+        if d < depth:
+
+            @pl.when(p.z >= d)
+            def _(d=d):
+                def step(x):
+                    for a in range(count):
+                        arrived(a, p.z - d, p.y, x)
+                        spread(a, block(a, p.z - d, p.y, x), p.z - d, x, (1,))
+
+                over_x(step)
+
+            @pl.when(p.z + d < depth)
+            def _(d=d):
+                def step(x):
+                    for a in range(count):
+                        arrived(a, p.z + d, p.y, x)
+                        spread(a, block(a, p.z + d, p.y, x), p.z + d, x, (0,))
+
+                over_x(step)
+
+        if d == 1:
+            from_y(p.z)
+        else:
+
+            @pl.when(p.z >= d - 1)
+            def _(d=d):
+                from_y(p.z - d + 1)
+
+            @pl.when(p.z + d - 1 < depth)
+            def _(d=d):
+                from_y(p.z + d - 1)
+
+    for a in range(count):
+        pltpu.make_async_copy(ins[a], block(a, p.z, p.y, p.x), near.at[a]).wait()
+
+        def many(number, send, recv):
+            part = outs[a].at[pl.ds(0, number)]
+            return remote(part, part, send.at[a], recv.at[a], sibling)
+
+        if across > 1:
+            many(across - 1, xs, rc).wait_send()
+        if tall > 1:
+            many((tall - 1) * depth * across, ys, rc).wait_send()
+        many(p.units, cs, rc).wait()
+        for z in range(depth):
+            for way in (0, 1):
+
+                @pl.when(
+                    ((p.z >= z) & (p.z < depth - 1)) if way else ((p.z <= z) & (p.z > 0))
+                )
+                def _(z=z, way=way, a=a):
+                    for x in range(across):
+                        to_z(a, block(a, z, p.y, x), z, x, way).wait_send()
+
+    swaps.wait()
+
+
+def split_swaps(swapped):
+    return [w for w, _ in swapped], [shift for _, shift in swapped]
+
+
+def gather(shards, wide, collective_id, swapped=()):
+    group, peers = lax.axis_size("expert"), lax.axis_size("fsdp")
+    place = Place(group, peers, wide)
+    given, shifts = split_swaps(swapped)
+    count, extra = len(shards), len(given)
+    dma = pltpu.SemaphoreType.DMA
+    return pl.pallas_call(
+        functools.partial(gather_kernel, place, count, shifts),
+        out_shape=[jax.ShapeDtypeStruct((place.slots,) + s.shape, s.dtype) for s in shards]
+        + [jax.ShapeDtypeStruct(s.shape, s.dtype) for s in given],
+        in_specs=[pl.BlockSpec(memory_space=pl.ANY)] * (count + extra),
+        out_specs=[pl.BlockSpec(memory_space=pl.ANY)] * (count + extra),
+        scratch_shapes=[dma((count,))] * 5
+        + [
+            dma((count, 2, place.depth * place.across)),
+            dma((count, place.units)),
+            dma((max(extra, 1),)),
+            dma((max(extra, 1),)),
+        ],
+        compiler_params=pltpu.CompilerParams(
+            collective_id=collective_id, has_side_effects=True, vmem_limit_bytes=58 << 20
+        ),
+        name=f"gather{collective_id}",
+    )(*shards, *given)
+
+
+def scatter_kernel(place, count, shifts, *refs):
+    total = count + len(shifts)
+    ins, outs = refs[:count], refs[total : total + count]
+    given, taken = refs[count:total], refs[total + count : 2 * total]
+    refs = refs[2 * total :]
+    held, side, rows_y, rows_z, rows_x = (refs[i * count : (i + 1) * count] for i in range(5))
+    la, rc, yr, zr, zs, cs, ys, xs, xr, given_sem, taken_sem = refs[5 * count :]
+    p = place.here()
+    depth, tall, across = p.depth, p.tall, p.across
+    p.greet(len(shifts) > 0)
+    sibling = p.device(p.z, p.y, 1 - p.c)
+    half = max(depth // 2, 1)
+
+    def in_order(step):
+        lower = 1 - p.z // half
+
+        def right(total):
+            def go(j, _):
+                step(depth - 1 - j // across, (p.x + 1 + j % across) % across, 1)
+                return 0
+
+            lax.fori_loop(0, total * across, go, 0)
+
+        def left(total):
+            def go(j, _):
+                step(j // across, (p.x + 1 + j % across) % across, 0)
+                return 0
+
+            lax.fori_loop(0, total * across, go, 0)
+
+        right((depth - 1 - p.z) * lower)
+        left(p.z)
+        right((depth - 1 - p.z) * (1 - lower))
+
+        def own(j, _):
+            step(p.z, (p.x + 1 + j) % across, None)
+            return 0
+
+        lax.fori_loop(0, across, own, 0)
+
+    def local(a, k, z, y, x):
+        return pltpu.make_async_copy(ins[a].at[p.slot(z, y, p.c, x)], held[a].at[k, y], la.at[a, k])
+
+    def begin(z, x, way):
+        k = z * across + x
+        for a in range(count):
+            for y in range(tall):
+                remote(
+                    ins[a].at[p.slot(z, y, 1 - p.c, x)],
+                    side[a].at[k, y],
+                    cs.at[a],
+                    rc.at[a, k],
+                    sibling,
+                ).start()
+                local(a, k, z, y, x).start()
+
+    def add(a, target, sources):
+        rows = ins[a].shape[1]
+        chunk = 16 if rows % 16 == 0 else rows
+
+        def go(i, _):
+            part = pl.ds(i * chunk, chunk)
+            total = target[part].astype(jnp.float32)
+            for source in sources:
+                total = total + source[part].astype(jnp.float32)
+            target[part] = total.astype(target.dtype)
+            return 0
+
+        lax.fori_loop(0, rows // chunk, go, 0)
+
+    def first(z, x, way):
+        k = z * across + x
+        for a in range(count):
+            pltpu.make_async_copy(held[a].at[k], held[a].at[k], la.at[a, k]).wait()
+            remote(side[a].at[k], side[a].at[k], cs.at[a], rc.at[a, k], sibling).wait_recv()
+            for j in range(1, tall):
+                y = (p.y + j) % tall
+                add(a, held[a].at[k, y], [side[a].at[k, y]])
+                remote(
+                    held[a].at[k, y],
+                    rows_y[a].at[k, tall - j - 1],
+                    ys.at[a],
+                    yr.at[a, k],
+                    p.device(p.z, y, p.c),
+                ).start()
+            add(a, held[a].at[k, p.y], [side[a].at[k, p.y]])
+
+    def second(z, x, way):
+        k = z * across + x
+        for a in range(count):
+            mine = held[a].at[k, p.y]
+            if tall > 1:
+                remote(rows_y[a].at[k], rows_y[a].at[k], cs.at[a], yr.at[a, k], sibling).wait_recv()
+                add(a, mine, [rows_y[a].at[k, j] for j in range(tall - 1)])
+
+            def from_z(index):
+                part = rows_z[a].at[index]
+                remote(part, part, cs.at[a], zr.at[a, index], sibling).wait_recv()
+                add(a, mine, [part])
+
+            def send(index, target):
+                remote(mine, rows_z[a].at[index], zs.at[a, k], zr.at[a, index], target).start()
+
+            if way is None or way == 1:
+                pl.when(p.z > 0)(functools.partial(from_z, k))
+            if way is None:
+                pl.when(p.z < depth - 1)(functools.partial(from_z, depth * across + x))
+            if way == 0:
+                pl.when(p.z < depth - 1)(functools.partial(from_z, k))
+            if way == 1:
+                send(k, p.device(p.z + 1, p.y, p.c))
+            if way == 0:
+                left = p.device(p.z - 1, p.y, p.c)
+
+                @pl.when(z == p.z - 1)
+                def _():
+                    send(depth * across + x, left)
+
+                @pl.when(z < p.z - 1)
+                def _():
+                    send(k, left)
+
+            if way is None and across > 1:
+
+                @pl.when(x != p.x)
+                def _():
+                    remote(
+                        mine,
+                        rows_x[a].at[(p.x - x + across) % across - 1],
+                        xs.at[a],
+                        xr.at[a],
+                        p.device(p.z, p.y, p.c, x),
+                    ).start()
+
+    swaps = Swaps(p, shifts, given, taken, given_sem, taken_sem)
+    swaps.start()
+    in_order(begin)
+    in_order(first)
+    in_order(second)
+    k = p.z * across + p.x
+    for a in range(count):
+        mine = held[a].at[k, p.y]
+        sources = []
+        if across > 1:
+            remote(rows_x[a], rows_x[a], xs.at[a], xr.at[a], sibling).wait()
+            sources = [rows_x[a].at[j] for j in range(across - 1)]
+        rows = ins[a].shape[1]
+        chunk = 16 if rows % 16 == 0 else rows
+
+        def go(i, _):
+            part = pl.ds(i * chunk, chunk)
+            total = mine[part].astype(jnp.float32)
+            for source in sources:
+                total = total + source[part].astype(jnp.float32)
+            outs[a][part] = total
+            return 0
+
+        lax.fori_loop(0, rows // chunk, go, 0)
+        remote(side[a], side[a], cs.at[a], rc.at[a, 0], sibling).wait_send()
+        if tall > 1:
+            remote(rows_y[a], rows_y[a], ys.at[a], rc.at[a, 0], sibling).wait_send()
+
+        def wait_z(k, _):
+            @pl.when(k // across != p.z)
+            def _():
+                remote(mine, rows_z[a].at[0], zs.at[a, k], rc.at[a, 0], sibling).wait_send()
+
+            return 0
+
+        lax.fori_loop(0, depth * across, wait_z, 0)
+
+    swaps.wait()
+
+
+def scatter(partials, wide, collective_id, swapped=()):
+    group, peers = lax.axis_size("expert"), lax.axis_size("fsdp")
+    place = Place(group, peers, wide)
+    given, shifts = split_swaps(swapped)
+    count, extra = len(partials), len(given)
+    dma = pltpu.SemaphoreType.DMA
+    items = place.depth * place.across
+
+    def room(*lead):
+        return [pltpu.VMEM(lead + s.shape[1:], s.dtype) for s in partials]
+
+    return pl.pallas_call(
+        functools.partial(scatter_kernel, place, count, shifts),
+        out_shape=[jax.ShapeDtypeStruct(s.shape[1:], jnp.float32) for s in partials]
+        + [jax.ShapeDtypeStruct(s.shape, s.dtype) for s in given],
+        in_specs=[pl.BlockSpec(memory_space=pl.ANY)] * (count + extra),
+        out_specs=[pl.BlockSpec(memory_space=pltpu.VMEM)] * count
+        + [pl.BlockSpec(memory_space=pl.ANY)] * extra,
+        scratch_shapes=room(items, place.tall)
+        + room(items, place.tall)
+        + room(items, max(place.tall - 1, 1))
+        + room(items + place.across)
+        + room(max(place.across - 1, 1))
+        + [
+            dma((count, items)),
+            dma((count, items)),
+            dma((count, items)),
+            dma((count, items + place.across)),
+            dma((count, items)),
+            dma((count,)),
+            dma((count,)),
+            dma((count,)),
+            dma((count,)),
+            dma((max(extra, 1),)),
+            dma((max(extra, 1),)),
+        ],
+        compiler_params=pltpu.CompilerParams(
+            collective_id=collective_id, has_side_effects=True, vmem_limit_bytes=60 << 20
+        ),
+        name=f"scatter{collective_id}",
+    )(*partials, *given)
+
+
+def dot_plain(left, right):
+    return jnp.dot(left, right, preferred_element_type=jnp.float32)
+
+
+def dot_across(left, right):
+    return lax.dot_general(left, right, (((1,), (1,)), ((), ())), preferred_element_type=jnp.float32)
+
+
+def ffn_kernel(peers, sources, numbers, fill, *refs):
+    hid, cot, pick, turned = refs[:4]
+    gates, ups, downs = (refs[4 + i * peers : 4 + (i + 1) * peers] for i in range(3))
+    router, shared_in, shared_out = refs[4 + 3 * peers : 7 + 3 * peers]
+    out_part, back_part, rows, d_out, act, d_g, d_u, d_log, s_act, s_grad = refs[7 + 3 * peers :]
+    f32, bf16 = jnp.float32, jnp.bfloat16
+    step = pl.program_id(0)
+    slots, capacity, tok_rows = pick.shape
+    width = hid.shape[2] // peers
+    eid, start = numbers[0], numbers[1]
+    scale = fill[0]
+
+    def length(s):
+        return numbers[2 + step * sources + s]
+
+    scales = []
+    cots = []
+    for s in range(sources):
+        part = pl.ds(s * capacity, capacity)
+        rows[part, :] = dot_plain(pick[s], hid[s]).astype(bf16)
+        cots.append(dot_plain(pick[s], cot[s]))
+        lane = start + lax.broadcasted_iota(jnp.int32, (1, tok_rows), 1)
+        alive = jnp.where(lane < length(s), scale, 0.0)
+        scales.append(jnp.sum(pick[s].astype(f32) * alive, axis=1, keepdims=True))
+    row_scale = jnp.concatenate(scales, axis=0)
+    row_cot = jnp.concatenate(cots, axis=0)
+    rows_now = rows[...]
+    logits = dot_plain(rows_now, router[...])
+    top = jnp.max(logits, axis=1, keepdims=True)
+    powers = jnp.exp(logits - top)
+    probs = powers / jnp.sum(powers, axis=1, keepdims=True)
+    own = (lax.broadcasted_iota(jnp.int32, (1, probs.shape[1]), 1) == eid).astype(f32)
+    gate = jnp.sum(probs * own, axis=1, keepdims=True)
+
+    def cut(array, r):
+        return array[:, r * width : (r + 1) * width]
+
+    def summed(terms):
+        total = terms[0]
+        for term in terms[1:]:
+            total = total + term
+        return total
+
+    g = summed([dot_plain(cut(rows_now, r), gates[r][...]) for r in range(peers)])
+    u = summed([dot_plain(cut(rows_now, r), ups[r][...]) for r in range(peers)])
+    sigma = 1.0 / (1.0 + jnp.exp(-g))
+    act_now = (g * sigma * u).astype(bf16)
+    act[...] = act_now
+    d_now = ((gate * row_scale) * row_cot).astype(bf16)
+    d_out[...] = d_now
+    d_gate = jnp.zeros_like(gate)
+    weighted = []
+    for r in range(peers):
+        out = dot_plain(act_now, downs[r][...]).astype(bf16).astype(f32)
+        d_gate = d_gate + jnp.sum(cut(row_cot, r) * out, axis=1, keepdims=True)
+        weighted.append((gate * out).astype(bf16))
+    d_gate = d_gate * row_scale
+    d_act = summed([dot_across(cut(d_now, r), downs[r][...]) for r in range(peers)])
+    dg_now = (d_act * u * (sigma * (1.0 + g * (1.0 - sigma)))).astype(bf16)
+    du_now = (d_act * (g * sigma)).astype(bf16)
+    d_g[...] = dg_now
+    d_u[...] = du_now
+    dl_now = (gate * d_gate * (own - probs)).astype(bf16)
+    d_log[...] = dl_now
+    d_rows = []
+    for r in range(peers):
+        total = dot_across(dg_now, gates[r][...]) + dot_across(du_now, ups[r][...])
+        total = total + dot_across(dl_now, router[pl.ds(r * width, width), :])
+        d_rows.append(total.astype(bf16))
+    units = shared_out.shape[0]
+    total_rows = sources * tok_rows
+    hid_all = hid[...].reshape(total_rows, hid.shape[2])
+    cot_all = cot[...].reshape(total_rows, hid.shape[2])
+    both = dot_plain(hid_all, shared_in[...])
+    sg, su = both[:, :units], both[:, units:]
+    s_sigma = 1.0 / (1.0 + jnp.exp(-sg))
+    s_now = sg * s_sigma * su
+    column = lax.broadcasted_iota(jnp.int32, (tok_rows, 1), 0) + start
+    alive = jnp.concatenate(
+        [jnp.where(column < length(s), scale, 0.0) for s in range(sources)], axis=0
+    )
+    d_s = dot_across(cot_all, shared_out[...]) * alive
+    s_act[...] = (s_now * alive).astype(bf16)
+    s_low = s_now.astype(bf16)
+    d_sg = (d_s * su * (s_sigma * (1.0 + sg * (1.0 - s_sigma)))).astype(bf16)
+    d_su = (d_s * (sg * s_sigma)).astype(bf16)
+    s_grad[:, pl.ds(0, units)] = d_sg
+    s_grad[:, pl.ds(units, units)] = d_su
+    for s in range(sources):
+        part = slice(s * capacity, (s + 1) * capacity)
+        span = slice(s * tok_rows, (s + 1) * tok_rows)
+        for r in range(peers):
+            columns = pl.ds(r * width, width)
+            out_part[s, :, columns] = (
+                dot_plain(turned[s], weighted[r][part])
+                + dot_plain(s_low[span], shared_out[:, columns])
+            ).astype(bf16)
+            back_part[s, :, columns] = (
+                dot_plain(turned[s], d_rows[r][part])
+                + dot_across(d_sg[span], shared_in[columns, pl.ds(0, units)])
+                + dot_across(d_su[span], shared_in[columns, pl.ds(units, units)])
+            ).astype(bf16)
+
+
+def ffn(numbers, fill, hid, cot, pick, turned, gates, ups, downs, router, shared_in, shared_out):
+    group, tok_rows, dim = hid.shape
+    capacity = pick.shape[1]
+    peers = len(gates)
+    sources = max(1, min(4, 256 // capacity))
+    hidden = gates[0].shape[1]
+    units = shared_out.shape[0]
+    rows = sources * capacity
+    bf16 = jnp.bfloat16
+
+    def whole(array):
+        return pl.BlockSpec(
+            array.shape, lambda i, *_: (0,) * array.ndim, pipeline_mode=pl.Buffered(1)
+        )
+
+    def tile(*shape):
+        return pl.BlockSpec(shape, lambda i, *_: (i,) + (0,) * (len(shape) - 1))
+
+    pairs = group * capacity
+    weights = [*gates, *ups, *downs, router, shared_in, shared_out]
+    return pl.pallas_call(
+        functools.partial(ffn_kernel, peers, sources),
+        out_shape=[
+            jax.ShapeDtypeStruct((group, tok_rows, dim), bf16),
+            jax.ShapeDtypeStruct((group, tok_rows, dim), bf16),
+            jax.ShapeDtypeStruct((pairs, dim), bf16),
+            jax.ShapeDtypeStruct((pairs, dim), bf16),
+            jax.ShapeDtypeStruct((pairs, hidden), bf16),
+            jax.ShapeDtypeStruct((pairs, hidden), bf16),
+            jax.ShapeDtypeStruct((pairs, hidden), bf16),
+            jax.ShapeDtypeStruct((pairs, router.shape[1]), bf16),
+            jax.ShapeDtypeStruct((group * tok_rows, units), bf16),
+            jax.ShapeDtypeStruct((group * tok_rows, 2 * units), bf16),
+        ],
+        grid_spec=pltpu.PrefetchScalarGridSpec(
+            num_scalar_prefetch=2,
+            grid=(group // sources,),
+            in_specs=[
+                tile(sources, tok_rows, dim),
+                tile(sources, tok_rows, dim),
+                tile(sources, capacity, tok_rows),
+                tile(sources, tok_rows, capacity),
+            ]
+            + [whole(w) for w in weights],
+            out_specs=[
+                tile(sources, tok_rows, dim),
+                tile(sources, tok_rows, dim),
+                tile(rows, dim),
+                tile(rows, dim),
+                tile(rows, hidden),
+                tile(rows, hidden),
+                tile(rows, hidden),
+                tile(rows, router.shape[1]),
+                tile(sources * tok_rows, units),
+                tile(sources * tok_rows, 2 * units),
+            ],
+        ),
+        compiler_params=pltpu.CompilerParams(vmem_limit_bytes=62 << 20),
+        cost_estimate=pl.CostEstimate(
+            flops=18 * pairs * dim * hidden, bytes_accessed=60 << 20, transcendentals=1 << 22
+        ),
+        name="ffn",
+    )(numbers, fill, hid, cot, pick, turned, *weights)
 
 
 def from_peers(block):
@@ -160,15 +802,19 @@
         + [jnp.zeros((16 - TOPK - 5, tok_rows), f32)],
         axis=0,
     )
-    gate_parts = from_peers(expert_gate[0])
-    up_parts = from_peers(expert_up[0])
-    down_parts = from_peers(expert_down[0])
-    small_all = gather_all(small[None])
-    w_compress = gather_all(kva_weight)
-    w_expand = gather_all(kvb_weight)
-    w_query = gather_all(q_weight)
-    w_output = gather_all(out_weight)
-    w_router = gather_all(router_weight)
+    devices = group * peers
+    turns = range(1, peers)
+    w_query, w_compress, w_expand, w_output, w_router, small_all, *more = gather(
+        [q_weight, kva_weight, kvb_weight, out_weight, router_weight, small],
+        True,
+        0,
+        [(expert_gate[0], -r) for r in turns] + [(expert_up[0], -r) for r in turns],
+    )
+    gate_parts = [expert_gate[0]] + more[: peers - 1]
+    up_parts = [expert_up[0]] + more[peers - 1 :]
+    w_query, w_compress, w_expand, w_output, w_router = (
+        w.reshape(-1, w.shape[-1]) for w in (w_query, w_compress, w_expand, w_output, w_router)
+    )
     gain_attn = small_all[:, TOPK, : attn_gain.shape[0]].reshape(-1)
     gain_ffn = small_all[:, TOPK + 1, : ffn_gain.shape[0]].reshape(-1)
     gain_latent = small_all[:, TOPK + 2, : kv_gain.shape[0]].reshape(-1)
@@ -190,17 +836,24 @@
     pieces = lax.all_to_all(pieces, "expert", split_axis=0, concat_axis=0, tiled=True)
     gu_weight = jnp.roll(jnp.stack(from_peers(pieces)), fid, axis=0)
     gu_weight = gu_weight.transpose(1, 0, 2, 3).reshape(dim, 2 * units)
+    lanes_more = -units % 128
+    gu_weight = jnp.concatenate(
+        [
+            jnp.pad(gu_weight[:, :units], ((0, 0), (0, lanes_more))),
+            jnp.pad(gu_weight[:, units:], ((0, 0), (0, lanes_more))),
+        ],
+        axis=1,
+    )
     gu_weight = roll_in(gu_weight, 0)
     sd_weight = jnp.roll(jnp.stack(from_peers(shared_down)), fid, axis=0).reshape(units, dim)
-    sd_weight = roll_in(sd_weight, 1)
+    sd_weight = jnp.pad(roll_in(sd_weight, 1), ((0, lanes_more), (0, 0)))
     cosine, sine_vals = rope_tables(positions)
     tokens_f = tokens.astype(f32)
-    cot_plane = gather_plane(roll_in(cotangent, 1))
     normed_one, inverse_one = rms_norm(tokens_f, gain_attn)
     hidden_one = normed_one.astype(bf16)
-    query_proj = jnp.dot(hidden_one, w_query, preferred_element_type=f32).reshape(
-        tok_rows, H, DN + DR
-    )
+    query_proj = lax.optimization_barrier(
+        jnp.dot(hidden_one, w_query, preferred_element_type=f32)
+    ).reshape(tok_rows, H, DN + DR)
     query_all = jnp.concatenate(
         [
             query_proj[..., :DN],
@@ -213,10 +866,10 @@
     latent_norm, inverse_kv = rms_norm(latent_raw, gain_latent)
     latent = latent_norm.astype(bf16)
     key_rot = rotate(compressed[:, KVR:], cosine, sine_vals).astype(bf16)
-    all_latent, all_rot = (
-        lax.all_gather(latent, "fsdp", axis=0, tiled=True),
-        lax.all_gather(key_rot, "fsdp", axis=0, tiled=True),
-    )
+    latent_rot = lax.all_gather(
+        jnp.concatenate([latent, key_rot], axis=1), "fsdp", axis=0, tiled=True
+    )
+    all_latent, all_rot = latent_rot[:, :KVR], latent_rot[:, KVR:]
     keyval = jnp.dot(all_latent, w_expand, preferred_element_type=f32).astype(bf16)
     keyval = keyval.reshape(seq_len, H, DN + DV)
     key_nope = keyval[..., :DN]
@@ -242,7 +895,14 @@
     residual = tokens_f + jnp.dot(context, w_output, preferred_element_type=f32)
     normed_two, inverse_two = rms_norm(residual, gain_ffn)
     hidden_two = normed_two.astype(bf16)
-    hid_plane = gather_plane(roll_in(hidden_two, 1))
+    hid3, cot3, *more = gather(
+        [roll_in(hidden_two, 1), roll_in(cotangent, 1)],
+        False,
+        1,
+        [(expert_down[0], -r) for r in turns],
+    )
+    down_parts = [expert_down[0]] + more
+    hid_plane, cot_plane = hid3.reshape(plane_rows, dim), cot3.reshape(plane_rows, dim)
     router_probs = jax.nn.softmax(jnp.dot(hidden_two, w_router, preferred_element_type=f32), axis=-1)
     local_shares = jnp.sum(router_probs * valid_mask[:, None], axis=0)
     frequency = expert_count / (TOPK * valid_total) * route_counts
@@ -254,52 +914,54 @@
     rank = jnp.cumsum(named.astype(jnp.int32), axis=1) - 1
     slots = jnp.arange(capacity, dtype=jnp.int32)
     picker = (named[:, None, :] & (rank[:, None, :] == slots[None, :, None])).astype(bf16)
-    plane_valid = (positions[None, :] < all_lengths[:, None]).astype(f32)
-    plane_scale = (plane_valid * fill_scale).reshape(plane_rows, 1)
-    hid3 = hid_plane.reshape(group, tok_rows, dim)
-    cot3 = cot_plane.reshape(group, tok_rows, dim)
-    rows_in = jnp.einsum("sji,sid->sjd", picker, hid3, preferred_element_type=f32)
-    rows_in = rows_in.astype(bf16).reshape(pairs, dim)
-    rows_cot = jnp.einsum("sji,sid->sjd", picker, cot3, preferred_element_type=f32)
-    rows_cot = rows_cot.astype(bf16).reshape(pairs, dim)
-    rows_scale = fill_scale * jnp.sum(
-        picker.astype(f32) * plane_valid[:, None, :], axis=-1
-    ).reshape(pairs, 1)
+    turned = (named[:, :, None] & (rank[:, :, None] == slots[None, None, :])).astype(bf16)
+    numbers = jnp.concatenate(
+        [jnp.stack([eid, fid * tok_rows]).astype(jnp.int32), all_lengths.astype(jnp.int32)]
+    )
     w_router_in = roll_in(w_router, 0)
-    probs_rows = jax.nn.softmax(jnp.dot(rows_in, w_router_in, preferred_element_type=f32), axis=-1)
-    own_expert = (expert_ids == eid).astype(f32)[None, :]
-    gate_rows = jnp.sum(probs_rows * own_expert, axis=-1, keepdims=True)
+    (
+        out_part,
+        back_part,
+        rows_in,
+        d_out,
+        act,
+        d_hidden_g,
+        d_hidden_u,
+        dlog_rows,
+        shared_scaled,
+        d_gu,
+    ) = ffn(
+        numbers,
+        fill_scale.reshape(1),
+        hid3,
+        cot3,
+        picker,
+        turned,
+        gate_parts,
+        up_parts,
+        down_parts,
+        w_router_in,
+        gu_weight,
+        sd_weight,
+    )
 
     def cut(array, r):
         return array[:, r * half : (r + 1) * half]
 
-    def summed(term):
-        total = term(0)
-        for r in range(1, peers):
-            total = total + term(r)
-        return total
-
-    hidden_g = summed(lambda r: jnp.dot(cut(rows_in, r), gate_parts[r], preferred_element_type=f32))
-    hidden_u = summed(lambda r: jnp.dot(cut(rows_in, r), up_parts[r], preferred_element_type=f32))
-    act = (jax.nn.silu(hidden_g) * hidden_u).astype(bf16)
-    out_rows = jnp.concatenate(
-        [jnp.dot(act, w, preferred_element_type=f32).astype(bf16) for w in down_parts], axis=1
-    )
-    d_gate = rows_scale * jnp.sum(
-        rows_cot.astype(f32) * out_rows.astype(f32), axis=-1, keepdims=True
-    )
-    weighted = (gate_rows * out_rows.astype(f32)).astype(bf16)
-    d_out = (gate_rows * rows_scale * rows_cot.astype(f32)).astype(bf16)
-    d_act = summed(
-        lambda r: lax.dot_general(
-            cut(d_out, r), down_parts[r], (((1,), (1,)), ((), ())), preferred_element_type=f32
-        )
-    )
-    d_hidden_g = (d_act * hidden_u * silu_slope(hidden_g)).astype(bf16)
-    d_hidden_u = (d_act * jax.nn.silu(hidden_g)).astype(bf16)
-
     def outer(left, right):
         return lax.dot_general(left, right, (((0,), (0,)), ((), ())), preferred_element_type=f32)
+
+    def back(left, weight):
+        return lax.dot_general(left, weight, (((1,), (1,)), ((), ())), preferred_element_type=f32)
+
+    def gate_term(r):
+        return outer(cut(rows_in, r), d_hidden_g)
+
+    def up_term(r):
+        return outer(cut(rows_in, r), d_hidden_u)
+
+    def down_term(r):
+        return outer(act, cut(d_out, r))
 
     def with_peers(term):
         arrived = sum_to_peers(lambda r: term(r).astype(bf16))
@@ -308,43 +970,22 @@
             total = total + block.astype(f32)
         return total
 
-    egate_grad = with_peers(lambda r: outer(cut(rows_in, r), d_hidden_g))[None]
-    eup_grad = with_peers(lambda r: outer(cut(rows_in, r), d_hidden_u))[None]
-    edown_grad = with_peers(lambda r: outer(act, cut(d_out, r)))[None]
-    dlog_rows = (gate_rows * d_gate * (own_expert - probs_rows)).astype(bf16)
-
-    def back(left, weight):
-        return lax.dot_general(left, weight, (((1,), (1,)), ((), ())), preferred_element_type=f32)
-
-    d_rows = jnp.concatenate(
-        [back(d_hidden_g, gate_parts[r]) + back(d_hidden_u, up_parts[r]) for r in range(peers)],
-        axis=1,
-    )
-    d_rows = (d_rows + back(dlog_rows, w_router_in)).astype(bf16)
-    gu = jnp.dot(hid_plane, gu_weight, preferred_element_type=f32)
-    shared_g, shared_u = gu[:, :units], gu[:, units:]
-    shared_act = jax.nn.silu(shared_g) * shared_u
-    d_shared_act = back(cot_plane, sd_weight) * plane_scale
-    d_gu = jnp.concatenate(
-        [
-            d_shared_act * shared_u * silu_slope(shared_g),
-            d_shared_act * jax.nn.silu(shared_g),
-        ],
-        axis=1,
-    ).astype(bf16)
-    shared_low = shared_act.astype(bf16)
-    d_sd = outer((shared_act * plane_scale).astype(bf16), cot_plane)
+    def plus(total, blocks):
+        for block in blocks:
+            total = total + block.astype(f32)
+        return total
+
+    d_sd = outer(shared_scaled, cot_plane)[:units]
     d_gu_weight = outer(hid_plane, d_gu)
-    out_part = jnp.einsum(
-        "sji,sjd->sid", picker, weighted.reshape(group, capacity, dim), preferred_element_type=f32
-    ).reshape(plane_rows, dim) + jnp.dot(shared_low, sd_weight, preferred_element_type=f32)
-    back_part = jnp.einsum(
-        "sji,sjd->sid", picker, d_rows.reshape(group, capacity, dim), preferred_element_type=f32
-    ).reshape(plane_rows, dim) + back(d_gu, gu_weight)
-    d_hidden_two = scatter_plane(back_part.astype(bf16))
-    out_sum = scatter_plane(out_part.astype(bf16))
-    mixed = (residual + roll_out(out_sum, 1).astype(f32)).astype(bf16)
-    d_hidden_two = roll_out(d_hidden_two, 1).astype(f32) + back(dlog_own, w_router)
+    d_gu_weight = jnp.concatenate(
+        [d_gu_weight[:, :units], d_gu_weight[:, units + lanes_more : 2 * units + lanes_more]], axis=1
+    )
+    d_hidden_two, out_sum, *gate_blocks = scatter(
+        [back_part, out_part], False, 2, [(gate_term(r).astype(bf16), r) for r in turns]
+    )
+    egate_grad = plus(gate_term(0), gate_blocks)[None]
+    mixed = (residual + roll_out(out_sum, 1)).astype(bf16)
+    d_hidden_two = roll_out(d_hidden_two, 1) + back(dlog_own, w_router)
     router_grad = roll_out(outer(rows_in, dlog_rows), 0) + outer(hidden_two, dlog_own)
     d_gu_blocks = roll_out(d_gu_weight, 0).reshape(group, peers, dim // (group * peers), 2 * units)
 
@@ -390,12 +1031,11 @@
         "hts,thr->sr", d_scores, query_rope, preferred_element_type=f32
     )
     d_keyval_all = jnp.concatenate([d_key_nope, d_value], axis=-1).reshape(
-        peers, tok_rows, H * (DN + DV)
-    )
-    d_key_rot = d_key_rot.reshape(peers, tok_rows, DR)
+        seq_len, H * (DN + DV)
+    )
 
     def own_rows(array, r):
-        return lax.dynamic_index_in_dim(array, (fid + r) % peers, axis=0, keepdims=False)
+        return lax.dynamic_slice_in_dim(array, (fid + r) % peers * tok_rows, tok_rows, axis=0)
 
     own_dkeyval = with_peers(lambda r: own_rows(d_keyval_all, r))
     own_dkeyrot = with_peers(lambda r: own_rows(d_key_rot, r))
@@ -419,32 +1059,49 @@
     d_hidden_one = back(d_query, w_query) + back(d_compressed, w_compress)
     d_tokens, d_attn_gain = norm_back(d_hidden_one, tokens_f, inverse_one, gain_attn)
     tokens_grad = d_tokens + d_residual
-    smalls = lax.psum(
-        jnp.concatenate([d_attn_gain, d_latent_gain, d_ffn_gain, local_shares]), ("expert", "fsdp")
-    )
-    device = eid * peers + fid
-
-    def own_piece(start, size):
-        count = size // (group * peers)
-        return lax.dynamic_slice(smalls, (start + device * count,), (count,))
-
-    attn_gain_grad = own_piece(0, dim)
-    kv_gain_grad = own_piece(dim, KVR)
-    ffn_gain_grad = own_piece(dim + KVR, dim)
-    share_sums = smalls[2 * dim + KVR :]
-    balance = jnp.sum(frequency * (share_sums / valid_total))
+    def lanes(vector):
+        piece = vector.reshape(devices, -1)
+        return jnp.pad(piece, ((0, 0), (0, tok_rows - piece.shape[1])))
+
+    small_grads = jnp.stack(
+        [
+            lanes(d_attn_gain),
+            lanes(d_latent_gain),
+            lanes(d_ffn_gain),
+            lanes(jnp.tile(local_shares, devices)),
+        ]
+        + [jnp.zeros((devices, tok_rows), f32)] * 4,
+        axis=1,
+    )
+    dense = [
+        w.astype(bf16).reshape(devices, -1, w.shape[-1])
+        for w in (d_query_w, d_compress_w, d_expand_w, d_output_w, router_grad)
+    ]
+    q_grad, kva_grad, kvb_grad, out_grad, router_out, smalls, *blocks = scatter(
+        dense + [small_grads],
+        True,
+        3,
+        [(up_term(r).astype(bf16), r) for r in turns]
+        + [(down_term(r).astype(bf16), r) for r in turns],
+    )
+    eup_grad = plus(up_term(0), blocks[: peers - 1])[None]
+    edown_grad = plus(down_term(0), blocks[peers - 1 :])[None]
+    attn_gain_grad = smalls[0, : attn_gain.shape[0]]
+    kv_gain_grad = smalls[1, : kv_gain.shape[0]]
+    ffn_gain_grad = smalls[2, : ffn_gain.shape[0]]
+    balance = jnp.sum(frequency * (smalls[3, :expert_count] / valid_total))
     return (
         mixed,
         tokens_grad,
         balance,
         attn_gain_grad,
-        scatter_all(d_query_w),
-        scatter_all(d_compress_w),
+        q_grad,
+        kva_grad,
         kv_gain_grad,
-        scatter_all(d_expand_w),
-        scatter_all(d_output_w),
+        kvb_grad,
+        out_grad,
         ffn_gain_grad,
-        scatter_all(router_grad),
+        router_out,
         sgate_grad,
         sup_grad,
         sdown_grad,

time: 1770 us -> 877 us (0.50)
  waiting for transfers between devices: 965 us -> 26.8 us
  Pallas kernels: 0 us -> 593 us
  blocking collectives: 360 us -> 6.81 us
  matrix products: 291 us -> 132 us
  local copies, waits for them, and re-layouts: 61.5 us -> 38.2 us
    pallas_call x0 -> x5, Pallas kernels: none -> 593 us  [the longest x2 262 us: scatter(): pl.pallas_call(functools.partial(scatter_kernel, place, count, shifts), o...]
    reduce_scatter x6 -> x0, waiting for transfers between devices: 420 us -> none  [the longest x4 248 us: scatter_all(): lax.psum_scatter(partial.astype(jnp.bfloat16), ('expert', 'fsdp'), scatte...]
    ppermute x7 -> x4, waiting for transfers between devices: 341 us -> 16.2 us  [sum_to_peers(): lax.ppermute(term(r), 'fsdp', [(j, (j + r) % size) for j in range(size)])]
    all_gather x4 -> x1, blocking collectives: 321 us -> 6.81 us  [body(): lax.all_gather(jnp.concatenate([latent, key_rot], axis=1), 'fsdp', axis=0...]
    all_gather x6 -> x0, waiting for transfers between devices: 183 us -> none  [the longest x4 183 us: gather_all(): return lax.all_gather(shard, ('expert', 'fsdp'), axis=0, tiled=True)]
    dot_general x15 -> x0, matrix products: 114 us -> none  [the longest x2 18.9 us: body(): jnp.dot(cut(rows_in, r), gate_parts[r], preferred_element_type=f32)]
    psum x1 -> x0, blocking collectives: 39.3 us -> none  [body(): lax.psum(jnp.concatenate([d_attn_gain, d_latent_gain, d_ffn_gain, local_s...]
    dot_general x12 -> x5, matrix products: 63.3 us -> 25.1 us  [back(): lax.dot_general(left, weight, (((1,), (1,)), ((), ())), preferred_element...]
  transfers between devices with their start and end apart: 27 -> 8, of which waited for: 11 -> 2; matrix products, arithmetic and copies ran while one was open for 17% -> 17% of each run, Pallas kernels for 0% -> 48%
where the time goes in v2:
time: 877 us; the launch traced here: 870 us
  Pallas kernels  593 us (68%)
  matrix products  132 us (15%)
  other arithmetic  50 us (6%)
  local copies, waits for them, and re-layouts  38.2 us (4%)
  waiting for transfers between devices  26.8 us (3%)
  starting transfers between devices  18.2 us (2%)
    pallas_call x2, Pallas kernels, scatter(): pl.pallas_call(functools.partial(scatter_kernel, place, count, shifts), o...  262 us
    pallas_call x2, Pallas kernels, gather(): pl.pallas_call(functools.partial(gather_kernel, place, count, shifts), ou...  257 us
    pallas_call x1, Pallas kernels, ffn(): pl.pallas_call(functools.partial(ffn_kernel, peers, sources), out_shape=[...  73.8 us
    dot_general x14, matrix products, outer(): lax.dot_general(left, right, (((0,), (0,)), ((), ())), preferred_element_...  68.5 us
    dot_general x5, matrix products, back(): lax.dot_general(left, weight, (((1,), (1,)), ((), ())), preferred_element...  25.1 us
  transfers between devices with their start and end apart: 8, of which 2 were waited for; matrix products, arithmetic and copies ran while one was open for 17% of the time, Pallas kernels for 48%

profile of v2, /device:TPU:0, one launch (start us, length us, event | category | flops | bytes accessed | tf_op | source)
XLA Modules:
  0.0 869.6 jit_solution(17297202507892838928)
XLA Ops:
  4.8 7.4 all-to-all-start
  16.6 162.6 %gather0.1 = (bf16[32,64,3072]{2,1,0:T(8,128)(2,1)}, bf16[32,64,576]{2,1,0:T(8,128)(2,1)}, bf16[32,16,4096]{2,1,0:T(8,128)(2,1)}, bf16[32,64,2048]{2,1,0:T(8,128...) custom-call(bf16[64,3072]{1,0:T(8,128)(2,1)} %refs_0_.1, ...), custom_call_target="tpu_custom_call" | custom-call | tf_op jit(solution)/shard_map/gather0/pallas_call | solution.py:318
  186.7 6.8 all_gather.3
  197.7 7.7 fusion.87
  210.6 6.3 convolution_convert_fusion.9
  216.9 4.9 multiply_reduce_fusion.3
  232.0 94.8 %gather1.1 = (bf16[16,128,2048]{2,1,0:T(8,128)(2,1)}, bf16[16,128,2048]{2,1,0:T(8,128)(2,1)}, bf16[1408,1024]{1,0:T(8,128)(2,1)}) custom-call(bf16[128,2048]{1,0:T(8,128)(2,1)} %get-tuple-element.258.refs_0_, bf16[128,2048]{1,0:T(8,128)(2,1)} %get-tuple-element.257.refs_1_, bf16[1408,1024]{1,0:T(8,128)(2,1)} %bitcast.191), custom_call_target="tpu_custom_call" | custom-call | tf_op jit(solution)/shard_map/gather1/pallas_call | solution.py:318
  326.9 14.1 %fusion.36.refs_3_ = bf16[16,128,64]{2,1,0:T(8,128)(2,1)} fusion(s32[16,128]{1,0:T(8,128)S(1)} %broadcast_add_fusion, pred[16,128]{1,0:T(8,128)(4,1)S(1)} %fusion.59), kind=kLoop, calls=%fused_computation.105 | loop fusion | flops 393216 | bytes 272384 | tf_op jit(solution)/shard_map/convert_element_type | solution.py:917
  345.7 10.6 %collective-permute-done = bf16[16,64,176]{2,1,0:T(8,128)(2,1)} collective-permute-done((bf16[16,64,176]{2,1,0:T(8,128)(2,1)}, bf16[16,64,176]{2,1,0:T(8,128)(2,1)}, u32[]{:S(2)}, u32[]{:S(2)}) %collective-permute-start) | collective-permute-done | bytes 360480 | tf_op jit(solution)/shard_map/ppermute | solution.py:735
  362.8 73.8 %ffn.1 = (bf16[16,128,2048]{2,1,0:T(8,128)(2,1)}, bf16[16,128,2048]{2,1,0:T(8,128)(2,1)}, bf16[1024,2048]{1,0:T(8,128)(2,1)}, bf16[1024,2048]{1,0:T(8,128)(2,1)}...) custom-call(s32[18]{0:T(128)} %pad_add_fusion.numbers, ...), custom_call_target="tpu_custom_call" | custom-call | flops 53150220288 | bytes 62914560 | tf_op jit(solution)/shard_map/ffn/pallas_call | solution.py:687
  436.6 7.5 convolution_convert_fusion.6.refs_2_
  444.1 98.2 %scatter2.1 = (f32[128,2048]{1,0:T(8,128)}, f32[128,2048]{1,0:T(8,128)}, bf16[1024,1408]{1,0:T(8,128)(2,1)}) custom-call(bf16[16,128,2048]{2,1,0:T(8,128)(2,1)} %get-tuple-element.62.refs_0_, bf16[16,128,2048]{2,1,0:T(8,128)(2,1)} %get-tuple-element.63.refs_1_, bf16[1024,1408]{1,0:T(8,128)(2,1)} %convolution_convert_fusion.6.refs_2_), custom_call_target="tpu_custom_call" | custom-call | tf_op jit(solution)/shard_map/scatter2/pallas_call | solution.py:523
  546.9 6.3 convolution_convert_fusion.8
  559.8 7.4 convolution_bitcast_fusion
  569.2 9.9 %fusion.96 = f32[128,2048]{1,0:T(8,128)} fusion(bf16[128,3072]{0,1:T(8,128)(2,1)S(1)} %bitcast.175, bf16[2048,3072]{1,0:T(8,128)(2,1)} %bitcast.156), kind=kOutput, calls=%fused_computation.236 | convolution fusion | flops 1610612736 | bytes 14417920 | tf_op jit(solution)/shard_map/dot_general | solution.py:955
  579.0 6.8 convolution_convert_fusion
  585.8 5.6 convolution_convert_fusion.1
  599.0 4.8 convolution_convert_fusion.5.refs_6_
  612.4 4.9 fusion.44
  617.6 9.5 %add_bitcast_fusion.2 = f32[1,1024,1408]{2,1,0:T(8,128)} fusion(bf16[1024,1408]{1,0:T(8,128)(2,1)} %get-tuple-element.80, bf16[1024,1408]{1,0:T(8,128)(2,1)} %get-tuple-element.65, bf16[1024,2048]{1,0:T(8,128)(2,1)} %get-tuple-element.64), kind=kOutput, calls=%fused_computation.6 | convolution fusion | flops 2955673600 | bytes 13631488 | tf_op jit(solution)/shard_map/dot_general | solution.py:952
  634.7 16.2 %collective-permute-done.5 = f32[44,2048]{1,0:T(8,128)S(1)} collective-permute-done((f32[44,2048]{1,0:T(8,128)S(1)}, f32[44,2048]{1,0:T(8,128)S(1)}, u32[]{:S(2)}, u32[]{:S(2)}) %collective-permute-start.5) | collective-permute-done | bytes 360480 | tf_op jit(solution)/shard_map/ppermute | solution.py:743
  677.0 163.9 %scatter3.1 = (f32[64,3072]{1,0:T(8,128)}, f32[64,576]{1,0:T(8,128)}, f32[16,4096]{1,0:T(8,128)}, f32[64,2048]{1,0:T(8,128)}, f32[64,16]{1,0:T(8,128)}, /*index=...) custom-call(bf16[32,64,3072]{2,1,0:T(8,128)(2,1)} %bitcast.157, bf16[32,64,576]{2,1,0:T(8,128)(2,1)} %bitcast.168, ...), custom_call_target="tpu_custom_call" | custom-call | tf_op jit(solution)/shard_map/scatter3/pallas_call | solution.py:523
  846.7 9.5 %add_bitcast_fusion.1 = f32[1,1024,1408]{2,1,0:T(8,128)} fusion(bf16[1024,1408]{1,0:T(8,128)(2,1)} %get-tuple-element.81, bf16[1024,1408]{1,0:T(8,128)(2,1)} %get-tuple-element.69, bf16[1024,2048]{1,0:T(8,128)(2,1)} %get-tuple-element.64), kind=kOutput, calls=%fused_computation.5 | convolution fusion | flops 2955673600 | bytes 13631488 | tf_op jit(solution)/shard_map/dot_general | solution.py:952
  858.3 5.0 add_bitcast_fusion
  (322 shorter events, 120.9 us)
Async XLA Ops:
  0.7 13.8 %copy-start.77 = (bf16[16]{0:T(256)(128)(2,1)S(1)}, bf16[16]{0:T(256)(128)(2,1)}, u32[]{:S(2)}) copy-start(bf16[16]{0:T(256)(128)(2,1)} %param.29) | copy-start | bytes 100
  4.8 337.0 %all-to-all-start = ((bf16[16,64,176]{2,1,0:T(8,128)(2,1)}), bf16[16,64,176]{2,1,0:T(8,128)(2,1)}, u32[]{:S(2)}, u32[]{:S(2)}) async-start(bf16[16,64,176]{2,1,0:T(8,128)(2,1)} %maximum_bitcast_fusion), calls=%async_computation | async-start | bytes 1048576 | tf_op jit(solution)/shard_map/all_to_all | solution.py:836
  12.2 330.9 %collective-permute-start.1 = (bf16[44,2048]{1,0:T(8,128)(2,1)}, bf16[44,2048]{1,0:T(8,128)(2,1)}, u32[]{:S(2)}, u32[]{:S(2)}) collective-permute-start(bf16[44,2048]{1,0:T(8,128)(2,1)} %param.36), channel_id=1, source_target_pairs={{0,1},{1,0},{2,3},{3,2},{4,5},{5,4},{6,7},{7,6},{8,9},{9,8},{10,11... | collective-permute-start | bytes 540680 | tf_op jit(solution)/shard_map/ppermute | solution.py:735
  13.8 172.6 %copy-start.64 = (f32[32]{0:T(128)}, f32[32]{0:T(128)S(1)}, u32[]{:S(2)}) copy-start(f32[32]{0:T(128)S(1)} %multiply_power_fusion) | copy-start | bytes 388
  15.2 171.2 %copy-start.66 = (f32[128]{0:T(128)}, f32[128]{0:T(128)S(1)}, u32[]{:S(2)}) copy-start(f32[128]{0:T(128)S(1)} %fusion.83) | copy-start | bytes 1540
  16.6 165.3 %copy-start = (bf16[128,2048]{1,0:T(8,128)(2,1)S(1)}, bf16[128,2048]{1,0:T(8,128)(2,1)}, u32[]{:S(2)}) copy-start(bf16[128,2048]{1,0:T(8,128)(2,1)} %param.22) | copy-start | bytes 1572868
  182.6 15.1 %copy-start.44 = (f32[128]{0:T(128)}, f32[128]{0:T(128)S(1)}, u32[]{:S(2)}) copy-start(f32[128]{0:T(128)S(1)} %get-tuple-element.239) | copy-start | bytes 1540
  186.6 21.4 %copy-start.41 = (f32[128,32]{0,1:T(8,128)}, f32[128,32]{0,1:T(8,128)S(1)}, u32[]{:S(2)}) copy-start(f32[128,32]{0,1:T(8,128)S(1)} %get-tuple-element.235) | copy-start | bytes 49156
  224.1 102.7 %copy-start.6 = (bf16[128,2048]{1,0:T(8,128)(2,1)}, bf16[128,2048]{1,0:T(8,128)(2,1)S(1)}, u32[]{:S(2)}) copy-start(bf16[128,2048]{1,0:T(8,128)(2,1)S(1)} %multiply_convert_fusion.1) | copy-start | bytes 1572868
  224.5 317.8 %copy-start.49 = (f32[128]{0:T(128)}, f32[128]{0:T(128)S(1)}, u32[]{:S(2)}) copy-start(f32[128]{0:T(128)S(1)} %get-tuple-element.248) | copy-start | bytes 1540
  230.0 312.3 %copy-start.51 = (f32[128]{0:T(128)}, f32[128]{0:T(128)S(1)}, u32[]{:S(2)}) copy-start(f32[128]{0:T(128)S(1)} %fusion.77) | copy-start | bytes 1540
  230.0 312.3 %copy-start.55 = (f32[16]{0:T(128)}, f32[16]{0:T(128)S(1)}, u32[]{:S(2)}) copy-start(f32[16]{0:T(128)S(1)} %broadcast_multiply_fusion) | copy-start | bytes 196
  230.1 312.3 %copy-start.53 = (f32[128]{0:T(128)}, f32[128]{0:T(128)S(1)}, u32[]{:S(2)}) copy-start(f32[128]{0:T(128)S(1)} %get-tuple-element.256) | copy-start | bytes 1540
  230.8 311.5 %copy-start.57 = (f32[128]{0:T(128)}, f32[128]{0:T(128)S(1)}, u32[]{:S(2)}) copy-start(f32[128]{0:T(128)S(1)} %get-tuple-element.213) | copy-start | bytes 1540
  341.7 14.5 %collective-permute-start = (bf16[16,64,176]{2,1,0:T(8,128)(2,1)}, bf16[16,64,176]{2,1,0:T(8,128)(2,1)}, u32[]{:S(2)}, u32[]{:S(2)}) collective-permute-start(bf16[16,64,176]{2,1,0:T(8,128)(2,1)} %all-to-all-done), channel_id=1, source_target_pairs={{0,1},{1,0},{2,3},{3,2},{4,5},{5,4},{6,7},{7,6},{8,9},{9,8},{10,11... | collective-permute-start | bytes 1081352 | tf_op jit(solution)/shard_map/ppermute | solution.py:735
  344.5 14.1 %copy-start.71 = (pred[128]{0:T(512)(128)(4,1)S(1)}, pred[128]{0:T(512)(128)(4,1)}, u32[]{:S(2)}) copy-start(pred[128]{0:T(512)(128)(4,1)} %constant.236.clone.1) | copy-start | bytes 388
  444.1 98.2 %copy-start.14 = (bf16[32,64,16]{2,1,0:T(8,128)(2,1)S(1)}, bf16[32,64,16]{2,1,0:T(8,128)(2,1)}, u32[]{:S(2)}) copy-start(bf16[32,64,16]{2,1,0:T(8,128)(2,1)} %get-tuple-element.61) | copy-start | bytes 196612
  559.8 31.6 %copy-start.37 = (f32[256,64]{0,1:T(8,128)}, f32[256,64]{0,1:T(8,128)S(1)}, u32[]{:S(2)}) copy-start(f32[256,64]{0,1:T(8,128)S(1)} %fusion.15) | copy-start | bytes 196612
  592.0 41.8 %collective-permute-start.3 = (bf16[128,64]{0,1:T(8,128)(2,1)}, bf16[128,64]{0,1:T(8,128)(2,1)}, u32[]{:S(2)}, u32[]{:S(2)}) collective-permute-start(bf16[128,64]{0,1:T(8,128)(2,1)} %dynamic-slice_convert_fusion.1), channel_id=1, source_target_pairs={{0,1},{1,0},{2,3},{3,2},{4,5},{5,4},{6,7},{7,6},{8,9},{9,8},{10,11... | collective-permute-start | bytes 49160 | tf_op jit(solution)/shard_map/ppermute | solution.py:743
  594.6 63.5 %collective-permute-start.2 = (bf16[128,4096]{0,1:T(8,128)(2,1)}, bf16[128,4096]{0,1:T(8,128)(2,1)}, u32[]{:S(2)}, u32[]{:S(2)}) collective-permute-start(bf16[128,4096]{0,1:T(8,128)(2,1)} %dynamic-slice_convert_fusion), channel_id=1, source_target_pairs={{0,1},{1,0},{2,3},{3,2},{4,5},{5,4},{6,7},{7,6},{8,9},{9,8},{10,11... | collective-permute-start | bytes 3145736 | tf_op jit(solution)/shard_map/ppermute | solution.py:743
  611.4 40.3 %collective-permute-start.4 = (f32[16,64,176]{2,1,0:T(8,128)}, f32[16,64,176]{2,1,0:T(8,128)}, u32[]{:S(2)}, u32[]{:S(2)}) collective-permute-start(f32[16,64,176]{2,1,0:T(8,128)} %dynamic-slice_bitcast_fusion), channel_id=1, source_target_pairs={{0,1},{1,0},{2,3},{3,2},{4,5},{5,4},{6,7},{7,6},{8,9},{9,8},{10,11... | collective-permute-start | bytes 2162696 | tf_op jit(solution)/shard_map/ppermute | solution.py:743
  632.8 18.1 %collective-permute-start.5 = (f32[44,2048]{1,0:T(8,128)S(1)}, f32[44,2048]{1,0:T(8,128)S(1)}, u32[]{:S(2)}, u32[]{:S(2)}) collective-permute-start(f32[44,2048]{1,0:T(8,128)S(1)} %dynamic-slice_bitcast_fusion.1), channel_id=1, source_target_pairs={{0,1},{1,0},{2,3},{3,2},{4,5},{5,4},{6,7},{7,6},{8,9},{9,8},{10,11... | collective-permute-start | bytes 1081352 | tf_op jit(solution)/shard_map/ppermute | solution.py:743
  654.3 209.0 %all-to-all-start.1 = ((f32[16,64,176]{2,1,0:T(8,128)}), f32[16,64,176]{2,1,0:T(8,128)S(1)}, u32[]{:S(2)}, u32[]{:S(2)}) async-start(f32[16,64,176]{2,1,0:T(8,128)} %bitcast_add_fusion.1), calls=%async_computation.1 | async-start | bytes 2097152 | tf_op jit(solution)/shard_map/all_to_all | solution.py:998
  677.0 163.9 %copy-start.61 = (f32[16]{0:T(128)S(1)}, f32[16]{0:T(128)}, u32[]{:S(2)}) copy-start(f32[16]{0:T(128)} %get-tuple-element.208) | copy-start | bytes 196
  (70 other events, 385.4 us)

commit v3 on v2

--- a/solution.py
+++ b/solution.py
@@ -94,6 +94,12 @@
         self.z = e // (2 * self.tall)
         self.x = self.fsdp if self.wide else 0
         return self
+
+    def detour(self, z):
+        return (self.depth - 1) * (1 - z % 2)
+
+    def partner(self):
+        return self.z + 1 - self.z % 2 * 2
 
     def slot(self, z, y, c, x):
         return ((z * self.tall + y) * 2 + c) * self.across + x
@@ -164,7 +170,7 @@
     total = count + len(shifts)
     ins, outs = refs[:count], refs[total : total + count]
     given, taken = refs[count:total], refs[total + count : 2 * total]
-    near, xs, ys, cs, rc, zs, got, given_sem, taken_sem = refs[2 * total :]
+    near, xs, ys, cs, rc, zs, got, given_sem, taken_sem, es = refs[2 * total :]
     p = place.here()
     depth, tall, across = p.depth, p.tall, p.across
     p.greet(len(shifts) > 0)
@@ -207,9 +213,21 @@
             def _():
                 to_z(a, src, z, x, way).start()
 
-        for k in range(1, tall):
-            to_y(a, src, z, x, k).start()
+        @pl.when((p.c == 1) | (z != p.detour(p.z)))
+        def _():
+            for k in range(1, tall):
+                to_y(a, src, z, x, k).start()
+
         to_sibling(a, src, z, p.y, x).start()
+
+    def to_partner(a, z, y, x, k):
+        return remote(
+            block(a, z, y, x),
+            block(a, z, y, x),
+            es.at[a, x * max(tall - 1, 1) + k - 1],
+            got.at[a, unit(z, y, x)],
+            p.device(p.partner(), p.y, p.c),
+        )
 
     def over_x(step):
         if across == 1:
@@ -243,6 +261,11 @@
                 y = (p.y + k) % tall
                 for a in range(count):
                     arrived(a, z, y, x)
+
+                    @pl.when((p.c == 0) & (z == p.detour(p.partner())))
+                    def _(a=a, y=y, k=k):
+                        to_partner(a, z, y, x, k).start()
+
                     to_sibling(a, block(a, z, y, x), z, y, x).start()
 
         over_x(step)
@@ -290,7 +313,18 @@
         if across > 1:
             many(across - 1, xs, rc).wait_send()
         if tall > 1:
-            many((tall - 1) * depth * across, ys, rc).wait_send()
+
+            @pl.when(p.c == 1)
+            def _():
+                many((tall - 1) * depth * across, ys, rc).wait_send()
+
+            @pl.when(p.c == 0)
+            def _(a=a):
+                many((tall - 1) * (depth - 1) * across, ys, rc).wait_send()
+                for x in range(across):
+                    for k in range(1, tall):
+                        to_partner(a, 0, p.y, x, k).wait_send()
+
         many(p.units, cs, rc).wait()
         for z in range(depth):
             for way in (0, 1):
@@ -327,6 +361,7 @@
             dma((count, place.units)),
             dma((max(extra, 1),)),
             dma((max(extra, 1),)),
+            dma((count, place.across * max(place.tall - 1, 1))),
         ],
         compiler_params=pltpu.CompilerParams(
             collective_id=collective_id, has_side_effects=True, vmem_limit_bytes=58 << 20
@@ -335,13 +370,52 @@
     )(*shards, *given)
 
 
-def scatter_kernel(place, count, shifts, *refs):
+class Products:
+    def __init__(self, lefts, rights, results, held_left, held_right, sems):
+        self.parts = list(zip(lefts, rights, results, held_left, held_right))
+        self.sems = sems
+
+    def copies(self, i):
+        left, right, _, held_left, held_right = self.parts[i]
+        return (
+            pltpu.make_async_copy(left, held_left, self.sems.at[i, 0]),
+            pltpu.make_async_copy(right, held_right, self.sems.at[i, 1]),
+        )
+
+    def start(self):
+        for i in range(len(self.parts)):
+            for copy in self.copies(i):
+                copy.start()
+
+    def run(self, i):
+        for copy in self.copies(i):
+            copy.wait()
+        _, _, result, left, right = self.parts[i]
+        wide = left.shape[1]
+        chunk = 256 if wide % 256 == 0 else 128
+
+        def go(j, _):
+            part = pl.ds(pl.multiple_of(j * chunk, chunk), chunk)
+            result[part, :] = dot_turned(left[:, part], right[...]).astype(result.dtype)
+            return 0
+
+        lax.fori_loop(0, wide // chunk, go, 0)
+
+
+def scatter_kernel(place, count, shifts, pairs, *refs):
     total = count + len(shifts)
-    ins, outs = refs[:count], refs[total : total + count]
-    given, taken = refs[count:total], refs[total + count : 2 * total]
-    refs = refs[2 * total :]
-    held, side, rows_y, rows_z, rows_x = (refs[i * count : (i + 1) * count] for i in range(5))
-    la, rc, yr, zr, zs, cs, ys, xs, xr, given_sem, taken_sem = refs[5 * count :]
+    ins, given = refs[:count], refs[count:total]
+    lefts, rights = refs[total : total + pairs], refs[total + pairs : total + 2 * pairs]
+    refs = refs[total + 2 * pairs :]
+    outs, taken, results = refs[:count], refs[count:total], refs[total : total + pairs]
+    held_left, held_right = (
+        refs[total + (i + 1) * pairs : total + (i + 2) * pairs] for i in range(2)
+    )
+    refs = refs[total + 3 * pairs :]
+    held, side, rows_y, rows_z, rows_x, rows_e = (
+        refs[i * count : (i + 1) * count] for i in range(6)
+    )
+    la, rc, yr, zr, zs, cs, ys, xs, xr, given_sem, taken_sem, es, er, product_sem = refs[6 * count :]
     p = place.here()
     depth, tall, across = p.depth, p.tall, p.across
     p.greet(len(shifts) > 0)
@@ -351,26 +425,27 @@
     def in_order(step):
         lower = 1 - p.z // half
 
-        def right(total):
+        def right(total, done):
             def go(j, _):
-                step(depth - 1 - j // across, (p.x + 1 + j % across) % across, 1)
+                step(depth - 1 - j // across, (p.x + 1 + j % across) % across, 1, done * across + j)
                 return 0
 
             lax.fori_loop(0, total * across, go, 0)
 
-        def left(total):
+        def left(total, done):
             def go(j, _):
-                step(j // across, (p.x + 1 + j % across) % across, 0)
+                step(j // across, (p.x + 1 + j % across) % across, 0, done * across + j)
                 return 0
 
             lax.fori_loop(0, total * across, go, 0)
 
-        right((depth - 1 - p.z) * lower)
-        left(p.z)
-        right((depth - 1 - p.z) * (1 - lower))
+        early = (depth - 1 - p.z) * lower
+        right(early, 0)
+        left(p.z, early)
+        right((depth - 1 - p.z) * (1 - lower), early + p.z)
 
         def own(j, _):
-            step(p.z, (p.x + 1 + j) % across, None)
+            step(p.z, (p.x + 1 + j) % across, None, (depth - 1) * across + j)
             return 0
 
         lax.fori_loop(0, across, own, 0)
@@ -378,7 +453,7 @@
     def local(a, k, z, y, x):
         return pltpu.make_async_copy(ins[a].at[p.slot(z, y, p.c, x)], held[a].at[k, y], la.at[a, k])
 
-    def begin(z, x, way):
+    def begin(z, x, way, number):
         k = z * across + x
         for a in range(count):
             for y in range(tall):
@@ -405,30 +480,66 @@
 
         lax.fori_loop(0, rows // chunk, go, 0)
 
-    def first(z, x, way):
+    def first(z, x, way, number):
         k = z * across + x
         for a in range(count):
             pltpu.make_async_copy(held[a].at[k], held[a].at[k], la.at[a, k]).wait()
             remote(side[a].at[k], side[a].at[k], cs.at[a], rc.at[a, k], sibling).wait_recv()
             for j in range(1, tall):
                 y = (p.y + j) % tall
-                add(a, held[a].at[k, y], [side[a].at[k, y]])
-                remote(
-                    held[a].at[k, y],
-                    rows_y[a].at[k, tall - j - 1],
-                    ys.at[a],
-                    yr.at[a, k],
-                    p.device(p.z, y, p.c),
-                ).start()
+                mine = held[a].at[k, y]
+
+                def along_y(sources, mine=mine, j=j, y=y, a=a):
+                    add(a, mine, sources)
+                    remote(
+                        mine,
+                        rows_y[a].at[k, tall - j - 1],
+                        ys.at[a],
+                        yr.at[a, k],
+                        p.device(p.z, y, p.c),
+                    ).start()
+
+                @pl.when((p.c == 0) & (z == p.detour(p.z)))
+                def _(mine=mine, j=j, y=y, a=a):
+                    add(a, mine, [side[a].at[k, y]])
+                    remote(
+                        mine,
+                        rows_e[a].at[x, j - 1],
+                        es.at[a],
+                        er.at[a, x * (tall - 1) + j - 1],
+                        p.device(p.partner(), p.y, p.c),
+                    ).start()
+
+                @pl.when((p.c == 0) & (z == p.detour(p.partner())))
+                def _(j=j, y=y, a=a, along_y=along_y):
+                    part = rows_e[a].at[x, j - 1]
+                    remote(
+                        part, part, cs.at[a], er.at[a, x * (tall - 1) + j - 1], sibling
+                    ).wait_recv()
+                    along_y([side[a].at[k, y], part])
+
+                @pl.when((p.c == 1) | ((z != p.detour(p.z)) & (z != p.detour(p.partner()))))
+                def _(y=y, a=a, along_y=along_y):
+                    along_y([side[a].at[k, y]])
+
             add(a, held[a].at[k, p.y], [side[a].at[k, p.y]])
 
-    def second(z, x, way):
+    products = Products(lefts, rights, results, held_left, held_right, product_sem)
+
+    def second(z, x, way, number):
         k = z * across + x
+        for i in range(pairs):
+            if (way is None) == (i >= (depth - 1) * across):
+                pl.when(number == i)(functools.partial(products.run, i))
         for a in range(count):
             mine = held[a].at[k, p.y]
             if tall > 1:
-                remote(rows_y[a].at[k], rows_y[a].at[k], cs.at[a], yr.at[a, k], sibling).wait_recv()
-                add(a, mine, [rows_y[a].at[k, j] for j in range(tall - 1)])
+
+                @pl.when((p.c == 1) | (z != p.detour(p.z)))
+                def _(a=a, mine=mine):
+                    part = rows_y[a].at[k]
+                    remote(part, part, cs.at[a], yr.at[a, k], sibling).wait_recv()
+                    add(a, mine, [rows_y[a].at[k, j] for j in range(tall - 1)])
 
             def from_z(index):
                 part = rows_z[a].at[index]
@@ -472,6 +583,7 @@
     swaps = Swaps(p, shifts, given, taken, given_sem, taken_sem)
     swaps.start()
     in_order(begin)
+    products.start()
     in_order(first)
     in_order(second)
     k = p.z * across + p.x
@@ -495,7 +607,16 @@
         lax.fori_loop(0, rows // chunk, go, 0)
         remote(side[a], side[a], cs.at[a], rc.at[a, 0], sibling).wait_send()
         if tall > 1:
-            remote(rows_y[a], rows_y[a], ys.at[a], rc.at[a, 0], sibling).wait_send()
+
+            @pl.when(p.c == 1)
+            def _(a=a):
+                remote(rows_y[a], rows_y[a], ys.at[a], rc.at[a, 0], sibling).wait_send()
+
+            @pl.when(p.c == 0)
+            def _(a=a):
+                part = rows_y[a].at[pl.ds(0, (depth - 1) * across)]
+                remote(part, part, ys.at[a], rc.at[a, 0], sibling).wait_send()
+                remote(rows_e[a], rows_e[a], es.at[a], rc.at[a, 0], sibling).wait_send()
 
         def wait_z(k, _):
             @pl.when(k // across != p.z)
@@ -509,11 +630,12 @@
     swaps.wait()
 
 
-def scatter(partials, wide, collective_id, swapped=()):
+def scatter(partials, wide, collective_id, swapped=(), products=()):
     group, peers = lax.axis_size("expert"), lax.axis_size("fsdp")
     place = Place(group, peers, wide)
     given, shifts = split_swaps(swapped)
-    count, extra = len(partials), len(given)
+    count, extra, pairs = len(partials), len(given), len(products)
+    lefts, rights = [v[0] for v in products], [v[1] for v in products]
     dma = pltpu.SemaphoreType.DMA
     items = place.depth * place.across
 
@@ -521,17 +643,21 @@
         return [pltpu.VMEM(lead + s.shape[1:], s.dtype) for s in partials]
 
     return pl.pallas_call(
-        functools.partial(scatter_kernel, place, count, shifts),
+        functools.partial(scatter_kernel, place, count, shifts, pairs),
         out_shape=[jax.ShapeDtypeStruct(s.shape[1:], jnp.float32) for s in partials]
-        + [jax.ShapeDtypeStruct(s.shape, s.dtype) for s in given],
-        in_specs=[pl.BlockSpec(memory_space=pl.ANY)] * (count + extra),
+        + [jax.ShapeDtypeStruct(s.shape, s.dtype) for s in given]
+        + [jax.ShapeDtypeStruct((v.shape[1], w.shape[1]), kind) for v, w, kind in products],
+        in_specs=[pl.BlockSpec(memory_space=pl.ANY)] * (count + extra + 2 * pairs),
         out_specs=[pl.BlockSpec(memory_space=pltpu.VMEM)] * count
-        + [pl.BlockSpec(memory_space=pl.ANY)] * extra,
-        scratch_shapes=room(items, place.tall)
+        + [pl.BlockSpec(memory_space=pl.ANY)] * extra
+        + [pl.BlockSpec(memory_space=pltpu.VMEM)] * pairs,
+        scratch_shapes=[pltpu.VMEM(v.shape, v.dtype) for v in lefts + rights]
+        + room(items, place.tall)
         + room(items, place.tall)
         + room(items, max(place.tall - 1, 1))
         + room(items + place.across)
         + room(max(place.across - 1, 1))
+        + room(place.across, max(place.tall - 1, 1))
         + [
             dma((count, items)),
             dma((count, items)),
@@ -544,12 +670,15 @@
             dma((count,)),
             dma((max(extra, 1),)),
             dma((max(extra, 1),)),
+            dma((count,)),
+            dma((count, place.across * max(place.tall - 1, 1))),
+            dma((max(pairs, 1), 2)),
         ],
         compiler_params=pltpu.CompilerParams(
             collective_id=collective_id, has_side_effects=True, vmem_limit_bytes=60 << 20
         ),
         name=f"scatter{collective_id}",
-    )(*partials, *given)
+    )(*partials, *given, *lefts, *rights)
 
 
 def dot_plain(left, right):
@@ -560,42 +689,55 @@
     return lax.dot_general(left, right, (((1,), (1,)), ((), ())), preferred_element_type=jnp.float32)
 
 
+def dot_turned(left, right):
+    return lax.dot_general(left, right, (((0,), (0,)), ((), ())), preferred_element_type=jnp.float32)
+
+
 def ffn_kernel(peers, sources, numbers, fill, *refs):
-    hid, cot, pick, turned = refs[:4]
-    gates, ups, downs = (refs[4 + i * peers : 4 + (i + 1) * peers] for i in range(3))
-    router, shared_in, shared_out = refs[4 + 3 * peers : 7 + 3 * peers]
-    out_part, back_part, rows, d_out, act, d_g, d_u, d_log, s_act, s_grad = refs[7 + 3 * peers :]
+    hid, cot, ranks = refs[:3]
+    gates, ups, downs = (refs[3 + i * peers : 3 + (i + 1) * peers] for i in range(3))
+    router, shared_in, shared_out = refs[3 + 3 * peers : 6 + 3 * peers]
+    refs = refs[6 + 3 * peers :]
+    rows, d_out = refs[:peers], refs[peers : 2 * peers]
+    out_part, back_part, act, d_g, d_u, d_log, s_act, s_grad = refs[2 * peers : 8 + 2 * peers]
+    rows_here, cots_here = refs[8 + 2 * peers :]
     f32, bf16 = jnp.float32, jnp.bfloat16
     step = pl.program_id(0)
-    slots, capacity, tok_rows = pick.shape
+    tok_rows = hid.shape[1]
+    capacity = rows_here.shape[0] // sources
     width = hid.shape[2] // peers
-    eid, start = numbers[0], numbers[1]
+    eid, start, fid = numbers[0], numbers[1], numbers[2]
     scale = fill[0]
 
     def length(s):
-        return numbers[2 + step * sources + s]
+        return numbers[3 + step * sources + s]
+
+    def columns(r):
+        return pl.ds(pl.multiple_of((fid + r) % peers * width, width), width)
 
     scales = []
-    cots = []
+    picks = []
     for s in range(sources):
         part = pl.ds(s * capacity, capacity)
-        rows[part, :] = dot_plain(pick[s], hid[s]).astype(bf16)
-        cots.append(dot_plain(pick[s], cot[s]))
+        slot = lax.broadcasted_iota(jnp.int32, (capacity, tok_rows), 0).astype(f32)
+        pick = jnp.where(ranks[s] == slot, 1.0, 0.0)
         lane = start + lax.broadcasted_iota(jnp.int32, (1, tok_rows), 1)
         alive = jnp.where(lane < length(s), scale, 0.0)
-        scales.append(jnp.sum(pick[s].astype(f32) * alive, axis=1, keepdims=True))
+        scales.append(jnp.sum(pick * alive, axis=1, keepdims=True))
+        pick = pick.astype(bf16)
+        picks.append(pick)
+        rows_here[part, :] = dot_plain(pick, hid[s]).astype(bf16)
+        cots_here[part, :] = dot_plain(pick, cot[s]).astype(bf16)
     row_scale = jnp.concatenate(scales, axis=0)
-    row_cot = jnp.concatenate(cots, axis=0)
-    rows_now = rows[...]
-    logits = dot_plain(rows_now, router[...])
+    logits = dot_plain(rows_here[...], router[...])
     top = jnp.max(logits, axis=1, keepdims=True)
     powers = jnp.exp(logits - top)
     probs = powers / jnp.sum(powers, axis=1, keepdims=True)
     own = (lax.broadcasted_iota(jnp.int32, (1, probs.shape[1]), 1) == eid).astype(f32)
     gate = jnp.sum(probs * own, axis=1, keepdims=True)
 
-    def cut(array, r):
-        return array[:, r * width : (r + 1) * width]
+    for r in range(peers):
+        rows[r][...] = rows_here[:, columns(r)]
 
     def summed(terms):
         total = terms[0]
@@ -603,21 +745,21 @@
             total = total + term
         return total
 
-    g = summed([dot_plain(cut(rows_now, r), gates[r][...]) for r in range(peers)])
-    u = summed([dot_plain(cut(rows_now, r), ups[r][...]) for r in range(peers)])
+    g = summed([dot_plain(rows[r][...], gates[r][...]) for r in range(peers)])
+    u = summed([dot_plain(rows[r][...], ups[r][...]) for r in range(peers)])
     sigma = 1.0 / (1.0 + jnp.exp(-g))
     act_now = (g * sigma * u).astype(bf16)
     act[...] = act_now
-    d_now = ((gate * row_scale) * row_cot).astype(bf16)
-    d_out[...] = d_now
     d_gate = jnp.zeros_like(gate)
     weighted = []
     for r in range(peers):
         out = dot_plain(act_now, downs[r][...]).astype(bf16).astype(f32)
-        d_gate = d_gate + jnp.sum(cut(row_cot, r) * out, axis=1, keepdims=True)
+        row_cot = cots_here[:, columns(r)].astype(f32)
+        d_out[r][...] = ((gate * row_scale) * row_cot).astype(bf16)
+        d_gate = d_gate + jnp.sum(row_cot * out, axis=1, keepdims=True)
         weighted.append((gate * out).astype(bf16))
     d_gate = d_gate * row_scale
-    d_act = summed([dot_across(cut(d_now, r), downs[r][...]) for r in range(peers)])
+    d_act = summed([dot_across(d_out[r][...], downs[r][...]) for r in range(peers)])
     dg_now = (d_act * u * (sigma * (1.0 + g * (1.0 - sigma)))).astype(bf16)
     du_now = (d_act * (g * sigma)).astype(bf16)
     d_g[...] = dg_now
@@ -627,7 +769,7 @@
     d_rows = []
     for r in range(peers):
         total = dot_across(dg_now, gates[r][...]) + dot_across(du_now, ups[r][...])
-        total = total + dot_across(dl_now, router[pl.ds(r * width, width), :])
+        total = total + dot_across(dl_now, router[columns(r), :])
         d_rows.append(total.astype(bf16))
     units = shared_out.shape[0]
     total_rows = sources * tok_rows
@@ -652,21 +794,19 @@
         part = slice(s * capacity, (s + 1) * capacity)
         span = slice(s * tok_rows, (s + 1) * tok_rows)
         for r in range(peers):
-            columns = pl.ds(r * width, width)
-            out_part[s, :, columns] = (
-                dot_plain(turned[s], weighted[r][part])
-                + dot_plain(s_low[span], shared_out[:, columns])
+            out_part[s, :, columns(r)] = (
+                dot_turned(picks[s], weighted[r][part])
+                + dot_plain(s_low[span], shared_out[:, columns(r)])
             ).astype(bf16)
-            back_part[s, :, columns] = (
-                dot_plain(turned[s], d_rows[r][part])
-                + dot_across(d_sg[span], shared_in[columns, pl.ds(0, units)])
-                + dot_across(d_su[span], shared_in[columns, pl.ds(units, units)])
+            back_part[s, :, columns(r)] = (
+                dot_turned(picks[s], d_rows[r][part])
+                + dot_across(d_sg[span], shared_in[columns(r), pl.ds(0, units)])
+                + dot_across(d_su[span], shared_in[columns(r), pl.ds(units, units)])
             ).astype(bf16)
 
 
-def ffn(numbers, fill, hid, cot, pick, turned, gates, ups, downs, router, shared_in, shared_out):
+def ffn(capacity, numbers, fill, hid, cot, ranks, gates, ups, downs, router, shared_in, shared_out):
     group, tok_rows, dim = hid.shape
-    capacity = pick.shape[1]
     peers = len(gates)
     sources = max(1, min(4, 256 // capacity))
     hidden = gates[0].shape[1]
@@ -686,11 +826,10 @@
     weights = [*gates, *ups, *downs, router, shared_in, shared_out]
     return pl.pallas_call(
         functools.partial(ffn_kernel, peers, sources),
-        out_shape=[
+        out_shape=[jax.ShapeDtypeStruct((pairs, dim // peers), bf16)] * (2 * peers)
+        + [
             jax.ShapeDtypeStruct((group, tok_rows, dim), bf16),
             jax.ShapeDtypeStruct((group, tok_rows, dim), bf16),
-            jax.ShapeDtypeStruct((pairs, dim), bf16),
-            jax.ShapeDtypeStruct((pairs, dim), bf16),
             jax.ShapeDtypeStruct((pairs, hidden), bf16),
             jax.ShapeDtypeStruct((pairs, hidden), bf16),
             jax.ShapeDtypeStruct((pairs, hidden), bf16),
@@ -704,15 +843,13 @@
             in_specs=[
                 tile(sources, tok_rows, dim),
                 tile(sources, tok_rows, dim),
-                tile(sources, capacity, tok_rows),
-                tile(sources, tok_rows, capacity),
+                tile(sources, 1, tok_rows),
             ]
             + [whole(w) for w in weights],
-            out_specs=[
+            out_specs=[tile(rows, dim // peers)] * (2 * peers)
+            + [
                 tile(sources, tok_rows, dim),
                 tile(sources, tok_rows, dim),
-                tile(rows, dim),
-                tile(rows, dim),
                 tile(rows, hidden),
                 tile(rows, hidden),
                 tile(rows, hidden),
@@ -720,13 +857,14 @@
                 tile(sources * tok_rows, units),
                 tile(sources * tok_rows, 2 * units),
             ],
+            scratch_shapes=[pltpu.VMEM((rows, dim), bf16)] * 2,
         ),
         compiler_params=pltpu.CompilerParams(vmem_limit_bytes=62 << 20),
         cost_estimate=pl.CostEstimate(
             flops=18 * pairs * dim * hidden, bytes_accessed=60 << 20, transcendentals=1 << 22
         ),
         name="ffn",
-    )(numbers, fill, hid, cot, pick, turned, *weights)
+    )(numbers, fill, hid, cot, ranks, *weights)
 
 
 def from_peers(block):
@@ -780,12 +918,6 @@
     plane_rows = group * tok_rows
     pairs = group * capacity
 
-    def roll_in(array, axis):
-        return jnp.roll(array, -fid * half, axis=axis)
-
-    def roll_out(array, axis):
-        return jnp.roll(array, fid * half, axis=axis)
-
     positions = fid * tok_rows + jnp.arange(tok_rows, dtype=jnp.int32)
     seq_length = lengths[0]
     valid_mask = (positions < seq_length).astype(f32)
@@ -826,29 +958,21 @@
         small_all.reshape(group, peers, 16, tok_rows), fid, axis=1, keepdims=False
     )
     units = shared_gate.shape[1] // group
+    lanes_more = -units % 128
     pieces = jnp.concatenate(
         [
-            shared_gate.reshape(-1, group, units),
-            shared_up.reshape(-1, group, units),
+            jnp.pad(w.reshape(-1, group, units), ((0, 0), (0, 0), (0, lanes_more)))
+            for w in (shared_gate, shared_up)
         ],
         axis=2,
     ).transpose(1, 0, 2)
     pieces = lax.all_to_all(pieces, "expert", split_axis=0, concat_axis=0, tiled=True)
-    gu_weight = jnp.roll(jnp.stack(from_peers(pieces)), fid, axis=0)
-    gu_weight = gu_weight.transpose(1, 0, 2, 3).reshape(dim, 2 * units)
-    lanes_more = -units % 128
-    gu_weight = jnp.concatenate(
-        [
-            jnp.pad(gu_weight[:, :units], ((0, 0), (0, lanes_more))),
-            jnp.pad(gu_weight[:, units:], ((0, 0), (0, lanes_more))),
-        ],
-        axis=1,
-    )
-    gu_weight = roll_in(gu_weight, 0)
     sd_weight = jnp.roll(jnp.stack(from_peers(shared_down)), fid, axis=0).reshape(units, dim)
-    sd_weight = jnp.pad(roll_in(sd_weight, 1), ((0, lanes_more), (0, 0)))
+    sd_weight = jnp.pad(sd_weight, ((0, lanes_more), (0, 0)))
     cosine, sine_vals = rope_tables(positions)
     tokens_f = tokens.astype(f32)
+    cot_ready, small_all = lax.optimization_barrier((cotangent, small_all))
+    cot_plane = lax.all_gather(cot_ready, "expert", axis=0, tiled=True)
     normed_one, inverse_one = rms_norm(tokens_f, gain_attn)
     hidden_one = normed_one.astype(bf16)
     query_proj = lax.optimization_barrier(
@@ -869,6 +993,8 @@
     latent_rot = lax.all_gather(
         jnp.concatenate([latent, key_rot], axis=1), "fsdp", axis=0, tiled=True
     )
+    down_own, latent_rot = lax.optimization_barrier((expert_down[0], latent_rot))
+    down_parts = from_peers(down_own)
     all_latent, all_rot = latent_rot[:, :KVR], latent_rot[:, KVR:]
     keyval = jnp.dot(all_latent, w_expand, preferred_element_type=f32).astype(bf16)
     keyval = keyval.reshape(seq_len, H, DN + DV)
@@ -895,14 +1021,11 @@
     residual = tokens_f + jnp.dot(context, w_output, preferred_element_type=f32)
     normed_two, inverse_two = rms_norm(residual, gain_ffn)
     hidden_two = normed_two.astype(bf16)
-    hid3, cot3, *more = gather(
-        [roll_in(hidden_two, 1), roll_in(cotangent, 1)],
-        False,
-        1,
-        [(expert_down[0], -r) for r in turns],
-    )
-    down_parts = [expert_down[0]] + more
-    hid_plane, cot_plane = hid3.reshape(plane_rows, dim), cot3.reshape(plane_rows, dim)
+    hid3, *more = gather([hidden_two], False, 1, [(pieces, -r) for r in turns])
+    gu_weight = jnp.roll(jnp.stack([pieces] + more), fid, axis=0)
+    gu_weight = gu_weight.transpose(1, 0, 2, 3).reshape(dim, -1)
+    hid_plane = hid3.reshape(plane_rows, dim)
+    cot3 = cot_plane.reshape(group, tok_rows, dim)
     router_probs = jax.nn.softmax(jnp.dot(hidden_two, w_router, preferred_element_type=f32), axis=-1)
     local_shares = jnp.sum(router_probs * valid_mask[:, None], axis=0)
     frequency = expert_count / (TOPK * valid_total) * route_counts
@@ -911,42 +1034,32 @@
         router_probs * (d_probs_own - jnp.sum(router_probs * d_probs_own, axis=-1, keepdims=True))
     ).astype(bf16)
     named = jnp.any(plane_small[:, :TOPK, :] == eid.astype(f32), axis=1)
-    rank = jnp.cumsum(named.astype(jnp.int32), axis=1) - 1
-    slots = jnp.arange(capacity, dtype=jnp.int32)
-    picker = (named[:, None, :] & (rank[:, None, :] == slots[None, :, None])).astype(bf16)
-    turned = (named[:, :, None] & (rank[:, :, None] == slots[None, None, :])).astype(bf16)
+    place = jnp.arange(tok_rows)
+    before = (place[:, None] < place[None, :]).astype(bf16)
+    ranks = jnp.dot(named.astype(bf16), before, preferred_element_type=f32)
+    ranks = jnp.where(named, ranks, -1.0)[:, None, :]
     numbers = jnp.concatenate(
-        [jnp.stack([eid, fid * tok_rows]).astype(jnp.int32), all_lengths.astype(jnp.int32)]
-    )
-    w_router_in = roll_in(w_router, 0)
-    (
-        out_part,
-        back_part,
-        rows_in,
-        d_out,
-        act,
-        d_hidden_g,
-        d_hidden_u,
-        dlog_rows,
-        shared_scaled,
-        d_gu,
-    ) = ffn(
+        [jnp.stack([eid, fid * tok_rows, fid]).astype(jnp.int32), all_lengths.astype(jnp.int32)]
+    )
+    made = ffn(
+        capacity,
         numbers,
         fill_scale.reshape(1),
         hid3,
         cot3,
-        picker,
-        turned,
+        ranks,
         gate_parts,
         up_parts,
         down_parts,
-        w_router_in,
+        w_router,
         gu_weight,
         sd_weight,
     )
 
-    def cut(array, r):
-        return array[:, r * half : (r + 1) * half]
+    rows_in, d_out = made[:peers], made[peers : 2 * peers]
+    out_part, back_part, act, d_hidden_g, d_hidden_u, dlog_rows, shared_scaled, d_gu = made[
+        2 * peers :
+    ]
 
     def outer(left, right):
         return lax.dot_general(left, right, (((0,), (0,)), ((), ())), preferred_element_type=f32)
@@ -955,13 +1068,13 @@
         return lax.dot_general(left, weight, (((1,), (1,)), ((), ())), preferred_element_type=f32)
 
     def gate_term(r):
-        return outer(cut(rows_in, r), d_hidden_g)
+        return outer(rows_in[r], d_hidden_g)
 
     def up_term(r):
-        return outer(cut(rows_in, r), d_hidden_u)
+        return outer(rows_in[r], d_hidden_u)
 
     def down_term(r):
-        return outer(act, cut(d_out, r))
+        return outer(act, d_out[r])
 
     def with_peers(term):
         arrived = sum_to_peers(lambda r: term(r).astype(bf16))
@@ -975,38 +1088,48 @@
             total = total + block.astype(f32)
         return total
 
-    d_sd = outer(shared_scaled, cot_plane)[:units]
-    d_gu_weight = outer(hid_plane, d_gu)
-    d_gu_weight = jnp.concatenate(
-        [d_gu_weight[:, :units], d_gu_weight[:, units + lanes_more : 2 * units + lanes_more]], axis=1
-    )
-    d_hidden_two, out_sum, *gate_blocks = scatter(
-        [back_part, out_part], False, 2, [(gate_term(r).astype(bf16), r) for r in turns]
+    d_hidden_two, *more = scatter(
+        [back_part],
+        False,
+        2,
+        [(gate_term(r).astype(bf16), r) for r in turns],
+        [
+            (hid_plane, d_gu, bf16),
+            (shared_scaled, cot_plane, bf16),
+            (rows_in[1], d_hidden_u, bf16),
+            (act, d_out[1], bf16),
+        ]
+        if peers == 2
+        else [],
+    )
+    gate_blocks = more[: peers - 1]
+    if peers == 2:
+        d_gu_weight, d_sd, *others = more[1:]
+    else:
+        d_gu_weight = outer(hid_plane, d_gu).astype(bf16)
+        d_sd = outer(shared_scaled, cot_plane).astype(bf16)
+        others = [up_term(r).astype(bf16) for r in turns]
+        others = others + [down_term(r).astype(bf16) for r in turns]
+    d_sd = d_sd[:units]
+    out_part, d_hidden_two = lax.optimization_barrier((out_part, d_hidden_two))
+    out_sum = lax.psum_scatter(
+        out_part.reshape(plane_rows, dim), "expert", scatter_dimension=0, tiled=True
     )
     egate_grad = plus(gate_term(0), gate_blocks)[None]
-    mixed = (residual + roll_out(out_sum, 1)).astype(bf16)
-    d_hidden_two = roll_out(d_hidden_two, 1) + back(dlog_own, w_router)
-    router_grad = roll_out(outer(rows_in, dlog_rows), 0) + outer(hidden_two, dlog_own)
-    d_gu_blocks = roll_out(d_gu_weight, 0).reshape(group, peers, dim // (group * peers), 2 * units)
+    d_hidden_two = d_hidden_two + back(dlog_own, w_router)
+    router_parts = jnp.stack([outer(rows_in[r], dlog_rows) for r in range(peers)])
+    router_grad = jnp.roll(router_parts, fid, axis=0).reshape(dim, -1) + outer(hidden_two, dlog_own)
+    d_gu_blocks = d_gu_weight.reshape(group, peers, dim // (group * peers), -1)
+    d_sd_blocks = d_sd.reshape(peers, units // peers, dim)
 
     def gu_term(r):
         return lax.dynamic_index_in_dim(d_gu_blocks, (fid + r) % peers, axis=1, keepdims=False)
 
-    gu_sum = gu_term(0)
-    for block in sum_to_peers(gu_term):
-        gu_sum = gu_sum + block
-    gu_sum = lax.all_to_all(gu_sum, "expert", split_axis=0, concat_axis=0, tiled=True)
-    gu_sum = gu_sum.transpose(1, 0, 2)
-    sgate_grad = gu_sum[:, :, :units].reshape(shared_gate.shape)
-    sup_grad = gu_sum[:, :, units:].reshape(shared_up.shape)
-    d_sd_blocks = roll_out(d_sd, 1).reshape(peers, units // peers, dim)
-
     def sd_term(r):
         return lax.dynamic_index_in_dim(d_sd_blocks, (fid + r) % peers, axis=0, keepdims=False)
 
-    sdown_grad = sd_term(0)
-    for block in sum_to_peers(sd_term):
-        sdown_grad = sdown_grad + block
+    gu_sum = plus(gu_term(0).astype(f32), sum_to_peers(gu_term)).astype(bf16)
+    sdown_grad = plus(sd_term(0).astype(f32), sum_to_peers(sd_term))
     grad_out = cotangent.astype(f32) * (valid_mask * fill_scale)[:, None]
     d_residual, d_ffn_gain = norm_back(d_hidden_two, residual, inverse_two, gain_ffn)
     d_residual = d_residual + grad_out
@@ -1039,6 +1162,8 @@
 
     own_dkeyval = with_peers(lambda r: own_rows(d_keyval_all, r))
     own_dkeyrot = with_peers(lambda r: own_rows(d_key_rot, r))
+    gu_sum, own_dkeyval = lax.optimization_barrier((gu_sum, own_dkeyval))
+    gu_sum = lax.all_to_all(gu_sum, "expert", split_axis=0, concat_axis=0, tiled=True)
     d_keyval = own_dkeyval.astype(bf16)
     d_expand_w = outer(latent, d_keyval)
     d_latent = back(d_keyval, w_expand)
@@ -1081,9 +1206,13 @@
         dense + [small_grads],
         True,
         3,
-        [(up_term(r).astype(bf16), r) for r in turns]
-        + [(down_term(r).astype(bf16), r) for r in turns],
-    )
+        [(w, r) for w, r in zip(others, [*turns, *turns])],
+    )
+    gu_sum, out_sum, smalls = lax.optimization_barrier((gu_sum, out_sum, smalls))
+    mixed = (residual + out_sum.astype(f32)).astype(bf16)
+    gu_sum = gu_sum.astype(f32).transpose(1, 0, 2)
+    sgate_grad = gu_sum[:, :, :units].reshape(shared_gate.shape)
+    sup_grad = gu_sum[:, :, units + lanes_more : 2 * units + lanes_more].reshape(shared_up.shape)
     eup_grad = plus(up_term(0), blocks[: peers - 1])[None]
     edown_grad = plus(down_term(0), blocks[peers - 1 :])[None]
     attn_gain_grad = smalls[0, : attn_gain.shape[0]]

time: 877 us -> 775 us (0.88)
  Pallas kernels: 593 us -> 509 us
  other arithmetic: 50 us -> 31.9 us
  between operations: 4.35 us -> 17.1 us
    pallas_call x2, Pallas kernels: 257 us -> 212 us  [gather(): pl.pallas_call(functools.partial(gather_kernel, place, count, shifts), ou...]
    pallas_call x2, Pallas kernels: 262 us -> 222 us  [scatter(): pl.pallas_call(functools.partial(scatter_kernel, place, count, shifts, pa...]
    convert_element_type x4 -> x2, other arithmetic: 17 us -> 4.1 us  [the longest x1 2.15 us: body(): gu_sum = plus(gu_term(0).astype(f32), sum_to_peers(gu_term)).astype(bf16)]
    concatenate x8 -> x1, other arithmetic: 12.9 us -> 0.59 us  [body(): jnp.concatenate([jnp.stack([eid, fid * tok_rows, fid]).astype(jnp.int32),...]
    ppermute x2, waiting for transfers between devices: 10.6 us -> 0.01 us  [from_peers(): lax.ppermute(block, 'fsdp', [(j, (j - r) % size) for j in range(size)])]
    dot_general x14 -> x11, matrix products: 68.5 us -> 59 us  [outer(): lax.dot_general(left, right, (((0,), (0,)), ((), ())), preferred_element_...]
  transfers between devices with their start and end apart: 8 -> 10, of which waited for: 2 -> 2; matrix products, arithmetic and copies ran while one was open for 17% -> 22% of each run, Pallas kernels for 48% -> 28%
where the time goes in v3:
time: 775 us; the launch traced here: 769 us
  Pallas kernels  509 us (66%)
  matrix products  124 us (16%)
  local copies, waits for them, and re-layouts  39.7 us (5%)
  other arithmetic  31.9 us (4%)
  waiting for transfers between devices  22.9 us (3%)
  between operations  17.1 us (2%)
  starting transfers between devices  17 us (2%)
    pallas_call x2, Pallas kernels, scatter(): pl.pallas_call(functools.partial(scatter_kernel, place, count, shifts, pa...  222 us
    pallas_call x2, Pallas kernels, gather(): pl.pallas_call(functools.partial(gather_kernel, place, count, shifts), ou...  212 us
    pallas_call x1, Pallas kernels, ffn(): pl.pallas_call(functools.partial(ffn_kernel, peers, sources), out_shape=[...  75.2 us
    dot_general x11, matrix products, outer(): lax.dot_general(left, right, (((0,), (0,)), ((), ())), preferred_element_...  59 us
    dot_general x5, matrix products, back(): lax.dot_general(left, weight, (((1,), (1,)), ((), ())), preferred_element...  23.6 us
    ppermute x4, waiting for transfers between devices, sum_to_peers(): lax.ppermute(term(r), 'fsdp', [(j, (j + r) % size) for j in range(size)])  22.8 us
  transfers between devices with their start and end apart: 10, of which 2 were waited for; matrix products, arithmetic and copies ran while one was open for 22% of the time, Pallas kernels for 28%

profile of v3, /device:TPU:0, one launch (start us, length us, event | category | flops | bytes accessed | tf_op | source)
XLA Modules:
  0.0 768.6 jit_solution(2716190128530843209)
XLA Ops:
  14.0 150.1 %gather0.1 = (bf16[32,64,3072]{2,1,0:T(8,128)(2,1)}, bf16[32,64,576]{2,1,0:T(8,128)(2,1)}, bf16[32,16,4096]{2,1,0:T(8,128)(2,1)}, bf16[32,64,2048]{2,1,0:T(8,128...) custom-call(bf16[64,3072]{1,0:T(8,128)(2,1)} %refs_0_.1, ...), custom_call_target="tpu_custom_call" | custom-call | tf_op jit(solution)/shard_map/gather0/pallas_call | solution.py:352
  169.5 5.9 all-to-all-start
  181.8 7.0 all_gather.6
  189.7 7.7 fusion.77
  212.2 5.8 convolution_convert_fusion.7
  218.0 5.0 multiply_reduce_fusion.3
  230.5 62.3 %gather1.1 = (bf16[16,128,2048]{2,1,0:T(8,128)(2,1)}, bf16[16,64,256]{2,1,0:T(8,128)(2,1)}) custom-call(bf16[128,2048]{1,0:T(8,128)(2,1)} %copy-done.11, bf16[16,64,256]{2,1,0:T(8,128)(2,1)} %all-to-all-done.refs_1_), custom_call_target="tpu_custom_call" | custom-call | tf_op jit(solution)/shard_map/gather1/pallas_call | solution.py:352
  295.9 75.2 %ffn.1 = (bf16[1024,1024]{1,0:T(8,128)(2,1)}, bf16[1024,1024]{1,0:T(8,128)(2,1)}, bf16[1024,1024]{1,0:T(8,128)(2,1)}, bf16[1024,1024]{1,0:T(8,128)(2,1)}, bf16[1...) custom-call(s32[19]{0:T(128)} %pad_add_fusion.numbers, ...), custom_call_target="tpu_custom_call" | custom-call | flops 53150220288 | bytes 62914560 | tf_op jit(solution)/shard_map/ffn/pallas_call | solution.py:827
  374.6 6.6 convolution_convert_fusion.4.refs_1_
  381.2 68.8 %scatter2.1 = (f32[128,2048]{1,0:T(8,128)}, bf16[1024,1408]{1,0:T(8,128)(2,1)}, bf16[2048,256]{1,0:T(8,128)(2,1)}, bf16[128,2048]{1,0:T(8,128)(2,1)}, bf16[1024,...) custom-call(bf16[16,128,2048]{2,1,0:T(8,128)(2,1)} %get-tuple-element.76.refs_0_, ...), custom_call_target="tpu_custom_call" | custom-call | tf_op jit(solution)/shard_map/scatter2/pallas_call | solution.py:645
  456.7 7.1 convolution_convert_fusion.6
  475.3 7.4 convolution_bitcast_fusion
  489.5 5.6 convolution_convert_fusion.1
  495.1 6.4 fusion.85
  501.5 9.7 %add_bitcast_fusion.2 = f32[1,1024,1408]{2,1,0:T(8,128)} fusion(bf16[1024,1408]{1,0:T(8,128)(2,1)} %get-tuple-element.105, bf16[1024,1024]{1,0:T(8,128)(2,1)} %get-tuple-element.91, bf16[1024,1408]{1,0:T(8,128)(2,1)} %get-tuple-element.78), kind=kOutput, calls=%fused_computation.6 | convolution fusion | flops 2955673600 | bytes 13631488 | tf_op jit(solution)/shard_map/dot_general | solution.py:1065
  511.2 6.6 convolution_convert_fusion
  521.8 5.9 collective-permute-done.5
  531.5 17.0 %collective-permute-done.3 = bf16[128,4096]{0,1:T(8,128)(2,1)S(1)} collective-permute-done((bf16[128,4096]{0,1:T(8,128)(2,1)}, bf16[128,4096]{0,1:T(8,128)(2,1)S(1)}, u32[]{:S(2)}, u32[]{:S(2)}) %collective-permute-start.3) | collective-permute-done | bytes 1048608 | tf_op jit(solution)/shard_map/ppermute | solution.py:881
  551.3 5.4 all-to-all-start.1
  567.1 4.4 copy.119
  572.3 4.5 convolution_convert_fusion.2
  576.8 153.0 %scatter3.1 = (f32[64,3072]{1,0:T(8,128)}, f32[64,576]{1,0:T(8,128)}, f32[16,4096]{1,0:T(8,128)}, f32[64,2048]{1,0:T(8,128)}, f32[64,16]{1,0:T(8,128)}, /*index=...) custom-call(bf16[32,64,3072]{2,1,0:T(8,128)(2,1)} %bitcast.172, bf16[32,64,576]{2,1,0:T(8,128)(2,1)} %bitcast.182, ...), custom_call_target="tpu_custom_call" | custom-call | tf_op jit(solution)/shard_map/scatter3/pallas_call | solution.py:645
  729.9 9.4 %add_bitcast_fusion.1 = f32[1,1024,1408]{2,1,0:T(8,128)} fusion(bf16[1024,1408]{1,0:T(8,128)(2,1)} %get-tuple-element.106, bf16[1024,1024]{1,0:T(8,128)(2,1)} %get-tuple-element.91, bf16[1024,1408]{1,0:T(8,128)(2,1)} %get-tuple-element.82.refs_8_), kind=kOutput, calls=%fused_computation.5 | convolution fusion | flops 2955673600 | bytes 13631488 | tf_op jit(solution)/shard_map/dot_general | solution.py:1065
  741.4 9.0 %add_bitcast_fusion = f32[1,1408,1024]{2,1,0:T(8,128)} fusion(bf16[1408,1024]{1,0:T(8,128)(2,1)} %get-tuple-element.108, bf16[1024,1408]{1,0:T(8,128)(2,1)} %get-tuple-element.80.refs_5_, bf16[1024,1024]{1,0:T(8,128)(2,1)} %get-tuple-element.107), kind=kOutput, calls=%fused_computation.4 | convolution fusion | flops 2955673600 | bytes 13631488 | tf_op jit(solution)/shard_map/dot_general | solution.py:1065
  (268 shorter events, 105.8 us)
Async XLA Ops:
  7.2 288.7 %all-gather.2.cloned.1.call-start = ((), (), s32[]{:S(2)}) async-start(), calls=%async_computation.3 | async-start | bytes 8912896 | tf_op jit(solution)/shard_map/all_gather | solution.py:975
  11.3 152.8 %copy-start.47 = (f32[128]{0:T(128)}, f32[128]{0:T(128)S(1)}, u32[]{:S(2)}) copy-start(f32[128]{0:T(128)S(1)} %fusion.73) | copy-start | bytes 1540
  14.0 150.7 %copy-start.35 = (bf16[64,1408]{1,0:T(8,128)(2,1)S(1)}, bf16[64,1408]{1,0:T(8,128)(2,1)}, u32[]{:S(2)}) copy-start(bf16[64,1408]{1,0:T(8,128)(2,1)} %param.30) | copy-start | bytes 540676
  164.1 14.2 %copy-start = (bf16[128,2048]{1,0:T(8,128)(2,1)S(1)}, bf16[128,2048]{1,0:T(8,128)(2,1)}, u32[]{:S(2)}) copy-start(bf16[128,2048]{1,0:T(8,128)(2,1)} %param.18) | copy-start | bytes 1572868
  164.1 64.0 %collective-permute-start.1 = (bf16[44,2048]{1,0:T(8,128)(2,1)}, bf16[44,2048]{1,0:T(8,128)(2,1)}, u32[]{:S(2)}, u32[]{:S(2)}) collective-permute-start(bf16[44,2048]{1,0:T(8,128)(2,1)} %param.32), channel_id=1, source_target_pairs={{0,1},{1,0},{2,3},{3,2},{4,5},{5,4},{6,7},{7,6},{8,9},{9,8},{10,11... | collective-permute-start | bytes 540680 | tf_op jit(solution)/shard_map/ppermute | solution.py:873
  165.2 13.8 %copy-start.5 = (bf16[32,64,576]{2,1,0:T(8,128)(2,1)S(1)}, bf16[32,64,576]{2,1,0:T(8,128)(2,1)}, u32[]{:S(2)}) copy-start(bf16[32,64,576]{2,1,0:T(8,128)(2,1)} %get-tuple-element.64) | copy-start | bytes 7077892
  169.5 61.0 %all-to-all-start = ((bf16[16,64,256]{2,1,0:T(8,128)(2,1)}), bf16[16,64,256]{2,1,0:T(8,128)(2,1)}, u32[]{:S(2)}, u32[]{:S(2)}) async-start(bf16[16,64,256]{2,1,0:T(8,128)(2,1)} %fusion.27), calls=%async_computation | async-start | bytes 1048576 | tf_op jit(solution)/shard_map/all_to_all | solution.py:969
  175.4 575.0 %reduce-scatter.2.cloned.1.call-start = ((), (), s32[]{:S(2)}) async-start(), calls=%async_computation.4 | async-start | bytes 8912896 | tf_op jit(solution)/shard_map/reduce_scatter | solution.py:1115
  180.8 16.6 %copy-start.53 = (f32[128]{0:T(128)}, f32[128]{0:T(128)S(1)}, u32[]{:S(2)}) copy-start(f32[128]{0:T(128)S(1)} %get-tuple-element.212) | copy-start | bytes 1540
  188.8 10.5 %copy-start.23 = (bf16[256,576]{0,1:T(8,128)(2,1)}, bf16[256,576]{0,1:T(8,128)(2,1)S(1)}, u32[]{:S(2)}) copy-start(bf16[256,576]{0,1:T(8,128)(2,1)S(1)} %all_gather.6) | copy-start | bytes 884740
  188.8 107.2 %collective-permute-start = (bf16[1408,1024]{1,0:T(8,128)(2,1)}, bf16[1408,1024]{1,0:T(8,128)(2,1)}, u32[]{:S(2)}, u32[]{:S(2)}) collective-permute-start(bf16[1408,1024]{1,0:T(8,128)(2,1)} %bitcast.refs_7_), channel_id=1, source_target_pairs={{0,1},{1,0},{2,3},{3,2},{4,5},{5,4},{6,7},{7,6},{8,9},{9,8},{10,11... | collective-permute-start | bytes 8650760 | tf_op jit(solution)/shard_map/ppermute | solution.py:873
  225.5 227.5 %copy-start.39 = (f32[128]{0:T(128)}, f32[128]{0:T(128)S(1)}, u32[]{:S(2)}) copy-start(f32[128]{0:T(128)S(1)} %fusion.66) | copy-start | bytes 1540
  225.6 227.4 %copy-start.41 = (f32[16]{0:T(128)}, f32[16]{0:T(128)S(1)}, u32[]{:S(2)}) copy-start(f32[16]{0:T(128)S(1)} %broadcast_multiply_fusion) | copy-start | bytes 196
  226.2 226.8 %copy-start.43 = (f32[128]{0:T(128)}, f32[128]{0:T(128)S(1)}, u32[]{:S(2)}) copy-start(f32[128]{0:T(128)S(1)} %get-tuple-element.188) | copy-start | bytes 1540
  469.7 51.9 %collective-permute-start.4 = (bf16[128,64]{0,1:T(8,128)(2,1)}, bf16[128,64]{0,1:T(8,128)(2,1)S(1)}, u32[]{:S(2)}, u32[]{:S(2)}) collective-permute-start(bf16[128,64]{0,1:T(8,128)(2,1)} %dynamic-slice_convert_fusion.1), channel_id=1, source_target_pairs={{0,1},{1,0},{2,3},{3,2},{4,5},{5,4},{6,7},{7,6},{8,9},{9,8},{10,11... | collective-permute-start | bytes 49160 | tf_op jit(solution)/shard_map/ppermute | solution.py:881
  472.0 57.3 %collective-permute-start.2 = (bf16[16,64,256]{2,1,0:T(8,128)(2,1)}, bf16[16,64,256]{2,1,0:T(8,128)(2,1)}, u32[]{:S(2)}, u32[]{:S(2)}) collective-permute-start(bf16[16,64,256]{2,1,0:T(8,128)(2,1)} %dynamic-slice_bitcast_fusion), channel_id=1, source_target_pairs={{0,1},{1,0},{2,3},{3,2},{4,5},{5,4},{6,7},{7,6},{8,9},{9,8},{10,11... | collective-permute-start | bytes 1572872 | tf_op jit(solution)/shard_map/ppermute | solution.py:881
  484.6 10.4 %slice-start = ((s8[12582912]{0:T(1024)(128)(4,1)}), s8[4194304]{0:T(1024)(128)(4,1)S(1)}, s32[]{:S(2)}) async-start(s8[12582912]{0:T(1024)(128)(4,1)} %bitcast.169), calls=%async_computation.5 | async-start | bytes 8388608
  501.5 9.7 %copy-start.13 = (bf16[128,16,192]{0,2,1:T(8,128)(2,1)S(1)}, bf16[128,16,192]{0,2,1:T(8,128)(2,1)}, u32[]{:S(2)}) copy-start(bf16[128,16,192]{0,2,1:T(8,128)(2,1)} %maximum_convert_fusion) | copy-start | bytes 2359300
  511.2 10.5 %copy-start.50 = (f32[128]{0:T(128)S(1)}, f32[128]{0:T(128)}, u32[]{:S(2)}) copy-start(f32[128]{0:T(128)} %copy-done.49) | copy-start | bytes 1540
  511.2 10.5 %copy-start.52 = (f32[32]{0:T(128)S(1)}, f32[32]{0:T(128)}, u32[]{:S(2)}) copy-start(f32[32]{0:T(128)} %copy-done.51) | copy-start | bytes 388
  519.5 8.2 %collective-permute-start.5 = (bf16[44,2048]{1,0:T(8,128)(2,1)}, bf16[44,2048]{1,0:T(8,128)(2,1)}, u32[]{:S(2)}, u32[]{:S(2)}) collective-permute-start(bf16[44,2048]{1,0:T(8,128)(2,1)} %dynamic-slice_bitcast_fusion.1), channel_id=1, source_target_pairs={{0,1},{1,0},{2,3},{3,2},{4,5},{5,4},{6,7},{7,6},{8,9},{9,8},{10,11... | collective-permute-start | bytes 540680 | tf_op jit(solution)/shard_map/ppermute | solution.py:881
  521.2 27.3 %collective-permute-start.3 = (bf16[128,4096]{0,1:T(8,128)(2,1)}, bf16[128,4096]{0,1:T(8,128)(2,1)S(1)}, u32[]{:S(2)}, u32[]{:S(2)}) collective-permute-start(bf16[128,4096]{0,1:T(8,128)(2,1)} %dynamic-slice_convert_fusion), channel_id=1, source_target_pairs={{0,1},{1,0},{2,3},{3,2},{4,5},{5,4},{6,7},{7,6},{8,9},{9,8},{10,11... | collective-permute-start | bytes 3145736 | tf_op jit(solution)/shard_map/ppermute | solution.py:881
  531.5 25.1 %copy-start.54 = (f32[128]{0:T(128)S(1)}, f32[128]{0:T(128)}, u32[]{:S(2)}) copy-start(f32[128]{0:T(128)} %copy-done.53) | copy-start | bytes 1540
  551.3 199.2 %all-to-all-start.1 = ((bf16[16,64,256]{2,1,0:T(8,128)(2,1)}), bf16[16,64,256]{2,1,0:T(8,128)(2,1)}, u32[]{:S(2)}, u32[]{:S(2)}) async-start(bf16[16,64,256]{2,1,0:T(8,128)(2,1)} %fusion.20), calls=%async_computation.1 | async-start | bytes 1048576 | tf_op jit(solution)/shard_map/all_to_all | solution.py:1166
  (48 other events, 174.3 us)
Sparse Core Ops, SparseCore 0:
  164.2 91.5 all-gather.1
  450.2 104.7 reduce-scatter.1

commit v4 on v3

--- a/solution.py
+++ b/solution.py
@@ -100,6 +100,17 @@
 
     def partner(self):
         return self.z + 1 - self.z % 2 * 2
+
+    def greet_peers(self):
+        barrier = pltpu.get_barrier_semaphore()
+        for k in range(1, self.peers):
+            pl.semaphore_signal(
+                barrier,
+                inc=1,
+                device_id=self.device(self.z, self.y, self.c, (self.fsdp + k) % self.peers),
+                device_id_type=MESH_IDS,
+            )
+        pl.semaphore_wait(barrier, self.peers - 1)
 
     def slot(self, z, y, c, x):
         return ((z * self.tall + y) * 2 + c) * self.across + x
@@ -370,16 +381,23 @@
     )(*shards, *given)
 
 
+def chunk_of(left):
+    return 256 if left.shape[1] % 256 == 0 else 128
+
+
 class Products:
-    def __init__(self, lefts, rights, results, held_left, held_right, sems):
-        self.parts = list(zip(lefts, rights, results, held_left, held_right))
-        self.sems = sems
+    def __init__(self, lefts, rights, results, refs):
+        count = len(lefts)
+        held_left, held_right, ready = refs[:count], refs[count : 2 * count], refs[2 * count : 3 * count]
+        self.parts = list(zip(lefts, rights, results, held_left, held_right, ready))
+        if count:
+            self.in_sems, self.out_sems = refs[3 * count :]
 
     def copies(self, i):
-        left, right, _, held_left, held_right = self.parts[i]
+        left, right, _, held_left, held_right, _ = self.parts[i]
         return (
-            pltpu.make_async_copy(left, held_left, self.sems.at[i, 0]),
-            pltpu.make_async_copy(right, held_right, self.sems.at[i, 1]),
+            pltpu.make_async_copy(left, held_left, self.in_sems.at[i, 0]),
+            pltpu.make_async_copy(right, held_right, self.in_sems.at[i, 1]),
         )
 
     def start(self):
@@ -390,16 +408,102 @@
     def run(self, i):
         for copy in self.copies(i):
             copy.wait()
-        _, _, result, left, right = self.parts[i]
-        wide = left.shape[1]
-        chunk = 256 if wide % 256 == 0 else 128
+        _, _, result, left, right, ready = self.parts[i]
+        chunk = chunk_of(left)
+        steps = left.shape[1] // chunk
+
+        def leave(j):
+            return pltpu.make_async_copy(
+                ready.at[j % 2],
+                result.at[pl.ds(pl.multiple_of(j * chunk, chunk), chunk)],
+                self.out_sems.at[i, j % 2],
+            )
+
+        def go(j, _):
+            @pl.when(j >= 2)
+            def _():
+                leave(j - 2).wait()
+
+            part = pl.ds(pl.multiple_of(j * chunk, chunk), chunk)
+            ready[j % 2] = dot_turned(left[:, part], right[...]).astype(ready.dtype)
+            leave(j).start()
+            return 0
+
+        lax.fori_loop(0, steps, go, 0)
+        for j in range(max(steps - 2, 0), steps):
+            leave(j).wait()
+
+
+def products_room(products):
+    room = [pltpu.VMEM(v[0].shape, v[0].dtype) for v in products]
+    room = room + [pltpu.VMEM(v[1].shape, v[1].dtype) for v in products]
+    room = room + [pltpu.VMEM((2, chunk_of(v), w.shape[1]), jnp.bfloat16) for v, w in products]
+    if products:
+        room = room + [pltpu.SemaphoreType.DMA((len(products), 2))] * 2
+    return room
+
+
+def products_shapes(products):
+    return [jax.ShapeDtypeStruct((v.shape[1], w.shape[1]), jnp.bfloat16) for v, w in products]
+
+
+def exchange_kernel(place, shifts, pairs, *refs):
+    extra = len(shifts)
+    given, refs = refs[:extra], refs[extra:]
+    lefts, rights, refs = refs[:pairs], refs[pairs : 2 * pairs], refs[2 * pairs :]
+    taken, results, refs = refs[:extra], refs[extra : extra + pairs], refs[extra + pairs :]
+    p = place.here()
+    p.greet_peers()
+    swaps = Swaps(p, shifts, given, taken, *refs[:2])
+    swaps.start()
+    products = Products(lefts, rights, results, refs[2:])
+    products.start()
+    for i in range(pairs):
+        products.run(i)
+    swaps.wait()
+
+
+def exchange(collective_id, swapped, products):
+    place = Place(lax.axis_size("expert"), lax.axis_size("fsdp"), False)
+    given, shifts = split_swaps(swapped)
+    extra, pairs = len(given), len(products)
+    lefts, rights = [v for v, _ in products], [w for _, w in products]
+    return pl.pallas_call(
+        functools.partial(exchange_kernel, place, shifts, pairs),
+        out_shape=[jax.ShapeDtypeStruct(s.shape, s.dtype) for s in given]
+        + products_shapes(products),
+        in_specs=[pl.BlockSpec(memory_space=pl.ANY)] * (extra + 2 * pairs),
+        out_specs=[pl.BlockSpec(memory_space=pl.ANY)] * (extra + pairs),
+        scratch_shapes=[pltpu.SemaphoreType.DMA((extra,))] * 2 + products_room(products),
+        compiler_params=pltpu.CompilerParams(
+            collective_id=collective_id, has_side_effects=True, vmem_limit_bytes=56 << 20
+        ),
+        name=f"exchange{collective_id}",
+    )(*given, *lefts, *rights)
+
+
+def outer_kernel(count, *refs):
+    for i in range(count):
+        left, right, result = refs[i], refs[count + i], refs[2 * count + i]
+        chunk = chunk_of(left)
 
         def go(j, _):
             part = pl.ds(pl.multiple_of(j * chunk, chunk), chunk)
             result[part, :] = dot_turned(left[:, part], right[...]).astype(result.dtype)
             return 0
 
-        lax.fori_loop(0, wide // chunk, go, 0)
+        lax.fori_loop(0, left.shape[1] // chunk, go, 0)
+
+
+def outer_products(products):
+    return pl.pallas_call(
+        functools.partial(outer_kernel, len(products)),
+        out_shape=products_shapes(products),
+        in_specs=[pl.BlockSpec(memory_space=pltpu.VMEM)] * (2 * len(products)),
+        out_specs=[pl.BlockSpec(memory_space=pltpu.VMEM)] * len(products),
+        compiler_params=pltpu.CompilerParams(vmem_limit_bytes=32 << 20),
+        name="outer",
+    )(*[v for v, _ in products], *[w for _, w in products])
 
 
 def scatter_kernel(place, count, shifts, pairs, *refs):
@@ -408,14 +512,11 @@
     lefts, rights = refs[total : total + pairs], refs[total + pairs : total + 2 * pairs]
     refs = refs[total + 2 * pairs :]
     outs, taken, results = refs[:count], refs[count:total], refs[total : total + pairs]
-    held_left, held_right = (
-        refs[total + (i + 1) * pairs : total + (i + 2) * pairs] for i in range(2)
-    )
-    refs = refs[total + 3 * pairs :]
+    refs = refs[total + pairs :]
     held, side, rows_y, rows_z, rows_x, rows_e = (
         refs[i * count : (i + 1) * count] for i in range(6)
     )
-    la, rc, yr, zr, zs, cs, ys, xs, xr, given_sem, taken_sem, es, er, product_sem = refs[6 * count :]
+    la, rc, yr, zr, zs, cs, ys, xs, xr, given_sem, taken_sem, es, er, *room = refs[6 * count :]
     p = place.here()
     depth, tall, across = p.depth, p.tall, p.across
     p.greet(len(shifts) > 0)
@@ -524,13 +625,15 @@
 
             add(a, held[a].at[k, p.y], [side[a].at[k, p.y]])
 
-    products = Products(lefts, rights, results, held_left, held_right, product_sem)
+    products = Products(lefts, rights, results, room)
+    last = depth * across - 1
 
     def second(z, x, way, number):
         k = z * across + x
         for i in range(pairs):
-            if (way is None) == (i >= (depth - 1) * across):
-                pl.when(number == i)(functools.partial(products.run, i))
+            turn = min(i, last)
+            if (way is None) == (turn >= (depth - 1) * across):
+                pl.when(number == turn)(functools.partial(products.run, i))
         for a in range(count):
             mine = held[a].at[k, p.y]
             if tall > 1:
@@ -646,13 +749,12 @@
         functools.partial(scatter_kernel, place, count, shifts, pairs),
         out_shape=[jax.ShapeDtypeStruct(s.shape[1:], jnp.float32) for s in partials]
         + [jax.ShapeDtypeStruct(s.shape, s.dtype) for s in given]
-        + [jax.ShapeDtypeStruct((v.shape[1], w.shape[1]), kind) for v, w, kind in products],
+        + products_shapes(products),
         in_specs=[pl.BlockSpec(memory_space=pl.ANY)] * (count + extra + 2 * pairs),
         out_specs=[pl.BlockSpec(memory_space=pltpu.VMEM)] * count
         + [pl.BlockSpec(memory_space=pl.ANY)] * extra
-        + [pl.BlockSpec(memory_space=pltpu.VMEM)] * pairs,
-        scratch_shapes=[pltpu.VMEM(v.shape, v.dtype) for v in lefts + rights]
-        + room(items, place.tall)
+        + [pl.BlockSpec(memory_space=pl.ANY)] * pairs,
+        scratch_shapes=room(items, place.tall)
         + room(items, place.tall)
         + room(items, max(place.tall - 1, 1))
         + room(items + place.across)
@@ -672,8 +774,8 @@
             dma((max(extra, 1),)),
             dma((count,)),
             dma((count, place.across * max(place.tall - 1, 1))),
-            dma((max(pairs, 1), 2)),
-        ],
+        ]
+        + products_room(products),
         compiler_params=pltpu.CompilerParams(
             collective_id=collective_id, has_side_effects=True, vmem_limit_bytes=60 << 20
         ),
@@ -800,8 +902,7 @@
             ).astype(bf16)
             back_part[s, :, columns(r)] = (
                 dot_turned(picks[s], d_rows[r][part])
-                + dot_across(d_sg[span], shared_in[columns(r), pl.ds(0, units)])
-                + dot_across(d_su[span], shared_in[columns(r), pl.ds(units, units)])
+                + dot_across(s_grad[span, :], shared_in[columns(r), :])
             ).astype(bf16)
 
 
@@ -867,6 +968,158 @@
     )(numbers, fill, hid, cot, ranks, *weights)
 
 
+def both_keys(keyval, rot):
+    f32 = jnp.float32
+    rot = rot.astype(f32)
+    first = jnp.concatenate([keyval[:, :DN].astype(f32), rot], axis=1)
+    second = jnp.concatenate([keyval[:, DN + DV : 2 * DN + DV].astype(f32), rot], axis=1)
+    second = pltpu.roll(second, DN + DR, 1)
+    return first.astype(jnp.bfloat16), second.astype(jnp.bfloat16)
+
+
+def turn(array, plain, ahead, behind):
+    width = array.shape[1]
+    return (
+        array * plain
+        + pltpu.roll(array, width - DR // 2, 1) * ahead
+        + pltpu.roll(array, DR // 2, 1) * behind
+    )
+
+
+def attend_kernel(numbers, hidden, w_query, latent, w_expand, rot, plain, ahead, behind, *outs):
+    query, keyval, probs, context = outs
+    bf16 = jnp.bfloat16
+    turned = turn(dot_plain(hidden[...], w_query[...]), plain[...], ahead[...], behind[...])
+    query_now = turned.astype(bf16)
+    query[...] = query_now
+    keyval[...] = dot_plain(latent[...], w_expand[...]).astype(bf16)
+    rows, keys = query.shape[0], keyval.shape[0]
+    row = lax.broadcasted_iota(jnp.int32, (rows, keys), 0) + numbers[0]
+    key = lax.broadcasted_iota(jnp.int32, (rows, keys), 1)
+    allowed = (key <= row) & (key < numbers[1])
+    for i, keys_now in enumerate(both_keys(keyval[...], rot[...])):
+        scores = dot_across(query_now, keys_now) * (DN + DR) ** (-0.5)
+        scores = jnp.where(allowed, scores, masked_value)
+        powers = jnp.exp(scores - jnp.max(scores, axis=1, keepdims=True))
+        share = powers / jnp.sum(powers, axis=1, keepdims=True)
+        probs[i] = share
+        value = keyval[:, pl.ds(i * (DN + DV) + DN, DV)]
+        context[:, pl.ds(i * DV, DV)] = dot_plain(share.astype(bf16), value).astype(bf16)
+
+
+def attend(numbers, hidden, w_query, latent, w_expand, rot, turns):
+    rows, dim = hidden.shape
+    keys, rank = latent.shape
+    bf16 = jnp.bfloat16
+
+    def still(array):
+        return pl.BlockSpec(array.shape, lambda i, *_: (0,) * array.ndim)
+
+    def columns(height, width):
+        return pl.BlockSpec((height, width), lambda i, *_: (0, i))
+
+    return pl.pallas_call(
+        attend_kernel,
+        out_shape=[
+            jax.ShapeDtypeStruct((rows, H * (DN + DR)), bf16),
+            jax.ShapeDtypeStruct((keys, H * (DN + DV)), bf16),
+            jax.ShapeDtypeStruct((H, rows, keys), jnp.float32),
+            jax.ShapeDtypeStruct((rows, H * DV), bf16),
+        ],
+        grid_spec=pltpu.PrefetchScalarGridSpec(
+            num_scalar_prefetch=1,
+            grid=(H // 2,),
+            in_specs=[
+                still(hidden),
+                columns(dim, 2 * (DN + DR)),
+                still(latent),
+                columns(rank, 2 * (DN + DV)),
+                still(rot),
+                *[still(t) for t in turns],
+            ],
+            out_specs=[
+                columns(rows, 2 * (DN + DR)),
+                columns(keys, 2 * (DN + DV)),
+                pl.BlockSpec((2, rows, keys), lambda i, *_: (i, 0, 0)),
+                columns(rows, 2 * DV),
+            ],
+        ),
+        compiler_params=pltpu.CompilerParams(vmem_limit_bytes=40 << 20),
+        name="attend",
+    )(numbers, hidden, w_query, latent, w_expand, rot, *turns)
+
+
+def attend_back_kernel(d_res, w_output, query, keyval, probs, rot, plain, ahead, behind, *outs):
+    d_query, d_keyval, d_rot = outs
+    f32, bf16 = jnp.float32, jnp.bfloat16
+    scale = (DN + DR) ** (-0.5)
+    query_now = query[...]
+    total = jnp.zeros(query.shape, f32)
+    rot_total = jnp.zeros(d_rot.shape, f32)
+    for i, keys_now in enumerate(both_keys(keyval[...], rot[...])):
+        d_context = dot_across(d_res[...], w_output[pl.ds(i * DV, DV), :]).astype(bf16)
+        share = probs[i]
+        at = i * (DN + DV)
+        d_value = dot_turned(share.astype(bf16), d_context)
+        d_share = dot_across(d_context, keyval[:, pl.ds(at + DN, DV)])
+        d_score = share * (d_share - jnp.sum(share * d_share, axis=1, keepdims=True))
+        d_score = d_score.astype(bf16)
+        total = total + dot_plain(d_score, keys_now) * scale
+        d_key = dot_turned(d_score, query_now) * scale
+        if i == 1:
+            d_key = pltpu.roll(d_key, DN + DR, 1)
+        d_keyval[:, pl.ds(at, DN)] = d_key[:, :DN].astype(bf16)
+        d_keyval[:, pl.ds(at + DN, DV)] = d_value.astype(bf16)
+        rot_total = rot_total + d_key[:, DN : 2 * DN]
+    d_query[...] = turn(total, plain[...], -ahead[...], -behind[...]).astype(bf16)
+
+    @pl.when(pl.program_id(0) == 0)
+    def _():
+        d_rot[...] = rot_total
+
+    @pl.when(pl.program_id(0) != 0)
+    def _():
+        d_rot[...] += rot_total
+
+
+def attend_back(d_res, w_output, query, keyval, probs, rot, turns):
+    rows, dim = d_res.shape
+    keys = keyval.shape[0]
+    bf16 = jnp.bfloat16
+
+    def still(array):
+        return pl.BlockSpec(array.shape, lambda i: (0,) * array.ndim)
+
+    def columns(height, width):
+        return pl.BlockSpec((height, width), lambda i: (0, i))
+
+    return pl.pallas_call(
+        attend_back_kernel,
+        out_shape=[
+            jax.ShapeDtypeStruct(query.shape, bf16),
+            jax.ShapeDtypeStruct(keyval.shape, bf16),
+            jax.ShapeDtypeStruct((keys, DN), jnp.float32),
+        ],
+        grid=(H // 2,),
+        in_specs=[
+            still(d_res),
+            pl.BlockSpec((2 * DV, dim), lambda i: (i, 0)),
+            columns(rows, 2 * (DN + DR)),
+            columns(keys, 2 * (DN + DV)),
+            pl.BlockSpec((2, rows, keys), lambda i: (i, 0, 0)),
+            still(rot),
+            *[still(t) for t in turns],
+        ],
+        out_specs=[
+            columns(rows, 2 * (DN + DR)),
+            columns(keys, 2 * (DN + DV)),
+            pl.BlockSpec((keys, DN), lambda i: (0, 0)),
+        ],
+        compiler_params=pltpu.CompilerParams(vmem_limit_bytes=40 << 20),
+        name="attend_back",
+    )(d_res, w_output, query, keyval, probs, rot, *turns)
+
+
 def from_peers(block):
     size = lax.axis_size("fsdp")
     return [block] + [
@@ -975,16 +1228,6 @@
     cot_plane = lax.all_gather(cot_ready, "expert", axis=0, tiled=True)
     normed_one, inverse_one = rms_norm(tokens_f, gain_attn)
     hidden_one = normed_one.astype(bf16)
-    query_proj = lax.optimization_barrier(
-        jnp.dot(hidden_one, w_query, preferred_element_type=f32)
-    ).reshape(tok_rows, H, DN + DR)
-    query_all = jnp.concatenate(
-        [
-            query_proj[..., :DN],
-            rotate(query_proj[..., DN:], cosine[:, None, :], sine_vals[:, None, :]),
-        ],
-        axis=-1,
-    ).astype(bf16)
     compressed = jnp.dot(hidden_one, w_compress, preferred_element_type=f32)
     latent_raw = compressed[:, :KVR]
     latent_norm, inverse_kv = rms_norm(latent_raw, gain_latent)
@@ -995,28 +1238,26 @@
     )
     down_own, latent_rot = lax.optimization_barrier((expert_down[0], latent_rot))
     down_parts = from_peers(down_own)
-    all_latent, all_rot = latent_rot[:, :KVR], latent_rot[:, KVR:]
-    keyval = jnp.dot(all_latent, w_expand, preferred_element_type=f32).astype(bf16)
-    keyval = keyval.reshape(seq_len, H, DN + DV)
-    key_nope = keyval[..., :DN]
-    value_all = keyval[..., DN:]
-    query_nope = query_all[..., :DN]
-    query_rope = query_all[..., DN:]
-    score_scale = (DN + DR) ** (-0.5)
-    key_place = jnp.arange(seq_len, dtype=jnp.int32)
-    allowed = (key_place[None, :] <= positions[:, None]) & (key_place[None, :] < seq_length)
-    raw_scores = jnp.einsum(
-        "thd,shd->hts", query_nope, key_nope, preferred_element_type=f32
-    ) + jnp.einsum("thr,sr->hts", query_rope, all_rot, preferred_element_type=f32)
-    scores = jnp.where(allowed[None], raw_scores * score_scale, masked_value)
-    row_max = jnp.max(scores, axis=-1, keepdims=True)
-    exp_scores = jnp.exp(scores - row_max)
-    probs_attn = exp_scores / jnp.sum(exp_scores, axis=-1, keepdims=True)
-    probs_low = probs_attn.astype(bf16)
-    context = (
-        jnp.einsum("hts,shd->thd", probs_low, value_all, preferred_element_type=f32)
-        .reshape(tok_rows, H * DV)
-        .astype(bf16)
+    all_rot = jnp.pad(latent_rot[:, KVR:], ((0, 0), (0, 2 * DN - DR)))
+
+    def spread_columns(first, second, rest):
+        one = jnp.concatenate([jnp.full((tok_rows, DN), rest, f32), first, second], axis=1)
+        return jnp.concatenate([one, one], axis=1)
+
+    zero = jnp.zeros_like(cosine)
+    rotations = [
+        spread_columns(cosine, cosine, 1.0),
+        spread_columns(-sine_vals, zero, 0.0),
+        spread_columns(zero, sine_vals, 0.0),
+    ]
+    query_all, keyval, probs_attn, context = attend(
+        jnp.stack([fid * tok_rows, seq_length]).astype(jnp.int32),
+        hidden_one,
+        w_query,
+        latent_rot[:, :KVR],
+        w_expand,
+        all_rot,
+        rotations,
     )
     residual = tokens_f + jnp.dot(context, w_output, preferred_element_type=f32)
     normed_two, inverse_two = rms_norm(residual, gain_ffn)
@@ -1094,28 +1335,30 @@
         2,
         [(gate_term(r).astype(bf16), r) for r in turns],
         [
-            (hid_plane, d_gu, bf16),
-            (shared_scaled, cot_plane, bf16),
-            (rows_in[1], d_hidden_u, bf16),
-            (act, d_out[1], bf16),
+            (hid_plane, d_gu),
+            (shared_scaled, cot_plane),
+            (rows_in[1], d_hidden_u),
+            (act, d_out[1]),
+            (rows_in[0], d_hidden_g),
         ]
         if peers == 2
         else [],
     )
     gate_blocks = more[: peers - 1]
     if peers == 2:
-        d_gu_weight, d_sd, *others = more[1:]
+        d_gu_weight, d_sd, *others, gate_own = more[1:]
     else:
         d_gu_weight = outer(hid_plane, d_gu).astype(bf16)
         d_sd = outer(shared_scaled, cot_plane).astype(bf16)
         others = [up_term(r).astype(bf16) for r in turns]
         others = others + [down_term(r).astype(bf16) for r in turns]
+        gate_own = gate_term(0)
     d_sd = d_sd[:units]
     out_part, d_hidden_two = lax.optimization_barrier((out_part, d_hidden_two))
     out_sum = lax.psum_scatter(
         out_part.reshape(plane_rows, dim), "expert", scatter_dimension=0, tiled=True
     )
-    egate_grad = plus(gate_term(0), gate_blocks)[None]
+    egate_grad = plus(gate_own.astype(f32), gate_blocks)[None]
     d_hidden_two = d_hidden_two + back(dlog_own, w_router)
     router_parts = jnp.stack([outer(rows_in[r], dlog_rows) for r in range(peers)])
     router_grad = jnp.roll(router_parts, fid, axis=0).reshape(dim, -1) + outer(hidden_two, dlog_own)
@@ -1134,53 +1377,37 @@
     d_residual, d_ffn_gain = norm_back(d_hidden_two, residual, inverse_two, gain_ffn)
     d_residual = d_residual + grad_out
     d_residual_low = d_residual.astype(bf16)
-    d_output_w = outer(context, d_residual_low)
-    d_context = back(d_residual_low, w_output).astype(bf16).reshape(tok_rows, H, DV)
-    d_value = jnp.einsum("hts,thd->shd", probs_low, d_context, preferred_element_type=f32)
-    d_weights = jnp.einsum("thd,shd->hts", d_context, value_all, preferred_element_type=f32)
-    d_scores = (
-        probs_attn * (d_weights - jnp.sum(probs_attn * d_weights, axis=-1, keepdims=True))
-    ).astype(bf16)
-    d_query_nope = score_scale * jnp.einsum(
-        "hts,shd->thd", d_scores, key_nope, preferred_element_type=f32
-    )
-    d_query_rope = score_scale * jnp.einsum(
-        "hts,sr->thr", d_scores, all_rot, preferred_element_type=f32
-    )
-    d_key_nope = score_scale * jnp.einsum(
-        "hts,thd->shd", d_scores, query_nope, preferred_element_type=f32
-    )
-    d_key_rot = score_scale * jnp.einsum(
-        "hts,thr->sr", d_scores, query_rope, preferred_element_type=f32
-    )
-    d_keyval_all = jnp.concatenate([d_key_nope, d_value], axis=-1).reshape(
-        seq_len, H * (DN + DV)
-    )
+    d_query, d_keyval_all, d_key_rot = attend_back(
+        d_residual_low, w_output, query_all, keyval, probs_attn, all_rot, rotations
+    )
+    d_key_rot = d_key_rot[:, :DR]
 
     def own_rows(array, r):
         return lax.dynamic_slice_in_dim(array, (fid + r) % peers * tok_rows, tok_rows, axis=0)
 
-    own_dkeyval = with_peers(lambda r: own_rows(d_keyval_all, r))
-    own_dkeyrot = with_peers(lambda r: own_rows(d_key_rot, r))
+    swapped = [(own_rows(d_keyval_all, r).astype(bf16), r) for r in turns]
+    swapped = swapped + [(own_rows(d_key_rot, r).astype(bf16), r) for r in turns]
+    *arrived, d_output_w, d_query_w, up_own, down_own = exchange(
+        4,
+        swapped,
+        [
+            (context, d_residual_low),
+            (hidden_one, d_query),
+            (rows_in[0], d_hidden_u),
+            (act, d_out[0]),
+        ],
+    )
+    own_dkeyval = plus(own_rows(d_keyval_all, 0).astype(f32), arrived[: peers - 1])
+    own_dkeyrot = plus(own_rows(d_key_rot, 0), arrived[peers - 1 :])
     gu_sum, own_dkeyval = lax.optimization_barrier((gu_sum, own_dkeyval))
     gu_sum = lax.all_to_all(gu_sum, "expert", split_axis=0, concat_axis=0, tiled=True)
     d_keyval = own_dkeyval.astype(bf16)
-    d_expand_w = outer(latent, d_keyval)
     d_latent = back(d_keyval, w_expand)
     d_latent_raw, d_latent_gain = norm_back(d_latent, latent_raw, inverse_kv, gain_latent)
     d_compressed = jnp.concatenate(
         [d_latent_raw, rotate_back(own_dkeyrot, cosine, sine_vals)], axis=-1
     ).astype(bf16)
-    d_compress_w = outer(hidden_one, d_compressed)
-    d_query = (
-        jnp.concatenate(
-            [d_query_nope, rotate_back(d_query_rope, cosine[:, None, :], sine_vals[:, None, :])],
-            axis=-1,
-        )
-        .reshape(tok_rows, H * (DN + DR))
-        .astype(bf16)
-    )
-    d_query_w = outer(hidden_one, d_query)
+    d_compress_w, d_expand_w = outer_products([(hidden_one, d_compressed), (latent, d_keyval)])
     d_hidden_one = back(d_query, w_query) + back(d_compressed, w_compress)
     d_tokens, d_attn_gain = norm_back(d_hidden_one, tokens_f, inverse_one, gain_attn)
     tokens_grad = d_tokens + d_residual
@@ -1213,8 +1440,8 @@
     gu_sum = gu_sum.astype(f32).transpose(1, 0, 2)
     sgate_grad = gu_sum[:, :, :units].reshape(shared_gate.shape)
     sup_grad = gu_sum[:, :, units + lanes_more : 2 * units + lanes_more].reshape(shared_up.shape)
-    eup_grad = plus(up_term(0), blocks[: peers - 1])[None]
-    edown_grad = plus(down_term(0), blocks[peers - 1 :])[None]
+    eup_grad = plus(up_own.astype(f32), blocks[: peers - 1])[None]
+    edown_grad = plus(down_own.astype(f32), blocks[peers - 1 :])[None]
     attn_gain_grad = smalls[0, : attn_gain.shape[0]]
     kv_gain_grad = smalls[1, : kv_gain.shape[0]]
     ffn_gain_grad = smalls[2, : ffn_gain.shape[0]]

time: 775 us -> 751 us (0.969)
  matrix products: 124 us -> 42.1 us
  Pallas kernels: 509 us -> 578 us
  waiting for transfers between devices: 22.9 us -> 0.05 us
  other arithmetic: 31.9 us -> 44.2 us
    pallas_call x0 -> x4, Pallas kernels: none -> 64.2 us  [the longest x1 29.3 us: exchange(): pl.pallas_call(functools.partial(exchange_kernel, place, shifts, pairs),...]
    dot_general x11 -> x4, matrix products: 59 us -> 12.5 us  [outer(): lax.dot_general(left, right, (((0,), (0,)), ((), ())), preferred_element_...]
    dot_general x11 -> x0, matrix products: 33.8 us -> none  [the longest x1 7.66 us: body(): jnp.dot(hidden_one, w_query, preferred_element_type=f32)]
    ppermute x4 -> x2, waiting for transfers between devices: 22.8 us -> 0.01 us  [sum_to_peers(): lax.ppermute(term(r), 'fsdp', [(j, (j + r) % size) for j in range(size)])]
    broadcast_in_dim x0 -> x3, other arithmetic: none -> 15.7 us  [the longest x1 6.52 us: body(): edown_grad = plus(down_own.astype(f32), blocks[peers - 1:])[None]]
    dot_general x5 -> x4, matrix products: 23.6 us -> 19.4 us  [back(): lax.dot_general(left, weight, (((1,), (1,)), ((), ())), preferred_element...]
    unnamed x133 -> x157, local copies, waits for them, and re-layouts: 11.4 us -> 15.6 us
  transfers between devices with their start and end apart: 10 -> 8, of which waited for: 2 -> 0; matrix products, arithmetic and copies ran while one was open for 22% -> 12% of each run, Pallas kernels for 28% -> 38%
where the time goes in v4:
time: 751 us; the launch traced here: 742 us
  Pallas kernels  578 us (77%)
  other arithmetic  44.2 us (6%)
  matrix products  42.1 us (6%)
  local copies, waits for them, and re-layouts  37.2 us (5%)
  between operations  17.5 us (2%)
  starting transfers between devices  17.1 us (2%)
    pallas_call x2, Pallas kernels, scatter(): pl.pallas_call(functools.partial(scatter_kernel, place, count, shifts, pa...  219 us
    pallas_call x2, Pallas kernels, gather(): pl.pallas_call(functools.partial(gather_kernel, place, count, shifts), ou...  218 us
    pallas_call x1, Pallas kernels, ffn(): pl.pallas_call(functools.partial(ffn_kernel, peers, sources), out_shape=[...  76.2 us
    pallas_call x1, Pallas kernels, exchange(): pl.pallas_call(functools.partial(exchange_kernel, place, shifts, pairs),...  29.3 us
    dot_general x4, matrix products, back(): lax.dot_general(left, weight, (((1,), (1,)), ((), ())), preferred_element...  19.4 us
    pallas_call x1, Pallas kernels, attend_back(): pl.pallas_call(attend_back_kernel, out_shape=[jax.ShapeDtypeStruct(query....  16.7 us
    unnamed x157, local copies, waits for them, and re-layouts  15.6 us
  transfers between devices with their start and end apart: 8, of which 0 were waited for; matrix products, arithmetic and copies ran while one was open for 12% of the time, Pallas kernels for 38%

profile of v4, /device:TPU:0, one launch (start us, length us, event | category | flops | bytes accessed | tf_op | source)
XLA Modules:
  0.0 741.8 jit_solution(11939249590158941616)
XLA Ops:
  14.0 150.1 %gather0.1 = (bf16[32,64,3072]{2,1,0:T(8,128)(2,1)}, bf16[32,64,576]{2,1,0:T(8,128)(2,1)}, bf16[32,16,4096]{2,1,0:T(8,128)(2,1)}, bf16[32,64,2048]{2,1,0:T(8,128...) custom-call(bf16[64,3072]{1,0:T(8,128)(2,1)} %refs_0_.1, ...), custom_call_target="tpu_custom_call" | custom-call | tf_op jit(solution)/shard_map/gather0/pallas_call | solution.py:363
  168.0 2.6 fusion.54
  171.9 6.0 all_gather.6
  181.4 5.3 all-to-all-start
  189.0 2.2 copy-done
  191.2 14.5 %attend.1 = (bf16[128,3072]{1,0:T(8,128)(2,1)S(1)}, bf16[256,4096]{1,0:T(8,128)(2,1)S(1)}, f32[16,128,256]{2,1,0:T(8,128)S(1)}, bf16[128,2048]{1,0:T(8,128)(2,1)S(1)}) custom-call(s32[2]{0:T(128)S(1)} %pad_add_fusion.numbers, bf16[128,2048]{1,0:T(8,128)(2,1)S(1)} %fusion.7.hidden.refs_3_.refs_0_, bf16[2048,3072]{1,0:T(8,128)(2,1)} %bitcast.122, ...), custom_call_target="tpu_custom_call" | custom-call | tf_op jit(solution)/shard_map/attend/pallas_call | solution.py:1021
  205.8 6.7 multiply_reduce_fusion.2
  218.7 67.8 %gather1.1 = (bf16[16,128,2048]{2,1,0:T(8,128)(2,1)}, bf16[16,64,256]{2,1,0:T(8,128)(2,1)}) custom-call(bf16[128,2048]{1,0:T(8,128)(2,1)} %multiply_convert_fusion.refs_0_, bf16[16,64,256]{2,1,0:T(8,128)(2,1)} %copy-done.22), custom_call_target="tpu_custom_call" | custom-call | tf_op jit(solution)/shard_map/gather1/pallas_call | solution.py:363
  289.7 76.2 %ffn.1 = (bf16[1024,1024]{1,0:T(8,128)(2,1)}, bf16[1024,1024]{1,0:T(8,128)(2,1)}, bf16[1024,1024]{1,0:T(8,128)(2,1)}, bf16[1024,1024]{1,0:T(8,128)(2,1)}, bf16[1...) custom-call(s32[19]{0:T(128)} %pad_add_fusion.1.numbers, ...), custom_call_target="tpu_custom_call" | custom-call | flops 53150220288 | bytes 62914560 | tf_op jit(solution)/shard_map/ffn/pallas_call | solution.py:928
  365.9 7.5 %convolution_convert_fusion.refs_1_ = bf16[1024,1408]{1,0:T(8,128)(2,1)} fusion(bf16[1024,1024]{1,0:T(8,128)(2,1)} %get-tuple-element.94.refs_4_, bf16[1024,1408]{1,0:T(8,128)(2,1)} %get-tuple-element.95.refs_11_), kind=kOutput, calls=%fused_computation.3 | convolution fusion | flops 2954231808 | bytes 7864320 | tf_op jit(solution)/shard_map/dot_general | solution.py:1306
  373.4 66.6 %scatter2.1 = (f32[128,2048]{1,0:T(8,128)}, bf16[1024,1408]{1,0:T(8,128)(2,1)}, bf16[2048,256]{1,0:T(8,128)(2,1)}, bf16[128,2048]{1,0:T(8,128)(2,1)}, bf16[1024,...) custom-call(bf16[16,128,2048]{2,1,0:T(8,128)(2,1)} %get-tuple-element.93.refs_0_, ...), custom_call_target="tpu_custom_call" | custom-call | tf_op jit(solution)/shard_map/scatter2/pallas_call | solution.py:748
  455.4 2.9 multiply_reduce_fusion
  461.8 16.7 %attend_back.1 = (bf16[128,3072]{1,0:T(8,128)(2,1)S(1)}, bf16[256,4096]{1,0:T(8,128)(2,1)S(1)}, f32[256,128]{1,0:T(8,128)S(1)}) custom-call(bf16[128,2048]{1,0:T(8,128)(2,1)S(1)} %get-tuple-element.221.d_res.refs_6_, bf16[2048,2048]{1,0:T(8,128)(2,1)} %bitcast.121, bf16[128,3072]{1,0:T(8,128)(2,1)S(1)} %copy-done.14, bf16[256,4096]{1,0:T(8,128)(2,1)S(1)} %copy-done.10, ...), custom_call_target="tpu_custom_call" | custom-call | tf_op jit(solution)/shard_map/attend_back/pallas_call | solution.py:1096
  481.1 29.3 %exchange4.1 = (bf16[128,4096]{1,0:T(8,128)(2,1)}, bf16[128,64]{1,0:T(8,128)(2,1)}, bf16[2048,2048]{1,0:T(8,128)(2,1)}, bf16[2048,3072]{1,0:T(8,128)(2,1)}, bf16...) custom-call(bf16[128,4096]{1,0:T(8,128)(2,1)} %constant_dynamic-slice_fusion.refs_0_, ...), custom_call_target="tpu_custom_call" | custom-call | tf_op jit(solution)/shard_map/exchange4/pallas_call | solution.py:471
  512.2 10.0 %fusion.55 = f32[128,2048]{1,0:T(8,128)} fusion(bf16[128,3072]{1,0:T(8,128)(2,1)S(1)} %copy-done.7, bf16[2048,3072]{1,0:T(8,128)(2,1)} %bitcast.123), kind=kOutput, calls=%fused_computation.151 | convolution fusion | flops 1610612736 | bytes 14417920 | tf_op jit(solution)/shard_map/dot_general | solution.py:1309
  522.2 3.3 add_bitcast_fusion.2
  529.9 2.2 fusion.14
  532.1 7.6 %all-to-all-start.1 = ((bf16[16,64,256]{2,1,0:T(8,128)(2,1)}), bf16[16,64,256]{2,1,0:T(8,128)(2,1)}, u32[]{:S(2)}, u32[]{:S(2)}) async-start(bf16[16,64,256]{2,1,0:T(8,128)(2,1)} %fusion.14), calls=%async_computation.1 | async-start | bytes 1048576 | tf_op jit(solution)/shard_map/all_to_all | solution.py:1403
  539.7 3.9 multiply_reduce_fusion.3
  545.4 3.7 outer.1
  552.7 2.5 fusion.13
  556.2 152.8 %scatter3.1 = (f32[64,3072]{1,0:T(8,128)}, f32[64,576]{1,0:T(8,128)}, f32[16,4096]{1,0:T(8,128)}, f32[64,2048]{1,0:T(8,128)}, f32[64,16]{1,0:T(8,128)}, /*index=...) custom-call(bf16[32,64,3072]{2,1,0:T(8,128)(2,1)} %bitcast.124, bf16[32,64,576]{2,1,0:T(8,128)(2,1)} %bitcast.117, ...), custom_call_target="tpu_custom_call" | custom-call | tf_op jit(solution)/shard_map/scatter3/pallas_call | solution.py:748
  709.0 5.9 add_bitcast_fusion.1
  717.1 6.5 add_bitcast_fusion
  (274 shorter events, 71.6 us)
Async XLA Ops:
  7.2 282.5 %all-gather.2.cloned.1.call-start = ((), (), s32[]{:S(2)}) async-start(), calls=%async_computation.3 | async-start | bytes 8912896 | tf_op jit(solution)/shard_map/all_gather | solution.py:1228
  14.0 153.1 %copy-start.15 = (bf16[128,2048]{1,0:T(8,128)(2,1)S(1)}, bf16[128,2048]{1,0:T(8,128)(2,1)}, u32[]{:S(2)}) copy-start(bf16[128,2048]{1,0:T(8,128)(2,1)} %param.18) | copy-start | bytes 1572868
  164.1 51.4 %collective-permute-start.1 = (bf16[44,2048]{1,0:T(8,128)(2,1)}, bf16[44,2048]{1,0:T(8,128)(2,1)}, u32[]{:S(2)}, u32[]{:S(2)}) collective-permute-start(bf16[44,2048]{1,0:T(8,128)(2,1)} %param.32), channel_id=1, source_target_pairs={{0,1},{1,0},{2,3},{3,2},{4,5},{5,4},{6,7},{7,6},{8,9},{9,8},{10,11... | collective-permute-start | bytes 540680 | tf_op jit(solution)/shard_map/ppermute | solution.py:1126
  165.8 275.7 %copy-start.70 = (f32[16]{0:T(128)}, f32[16]{0:T(128)S(1)}, u32[]{:S(2)}) copy-start(f32[16]{0:T(128)S(1)} %get-tuple-element.215) | copy-start | bytes 196
  168.0 21.0 %copy-start.1 = (bf16[128,2048]{1,0:T(8,128)(2,1)}, bf16[128,2048]{1,0:T(8,128)(2,1)S(1)}, u32[]{:S(2)}) copy-start(bf16[128,2048]{1,0:T(8,128)(2,1)S(1)} %fusion.7.hidden.refs_3_.refs_0_) | copy-start | bytes 1572868
  177.9 111.8 %collective-permute-start = (bf16[1408,1024]{1,0:T(8,128)(2,1)}, bf16[1408,1024]{1,0:T(8,128)(2,1)}, u32[]{:S(2)}, u32[]{:S(2)}) collective-permute-start(bf16[1408,1024]{1,0:T(8,128)(2,1)} %bitcast.11.refs_7_), channel_id=1, source_target_pairs={{0,1},{1,0},{2,3},{3,2},{4,5},{5,4},{6,7},{7,6},{8,9},{9,8},{10,11... | collective-permute-start | bytes 8650760 | tf_op jit(solution)/shard_map/ppermute | solution.py:1126
  181.4 36.5 %all-to-all-start = ((bf16[16,64,256]{2,1,0:T(8,128)(2,1)}), bf16[16,64,256]{2,1,0:T(8,128)(2,1)S(1)}, u32[]{:S(2)}, u32[]{:S(2)}) async-start(bf16[16,64,256]{2,1,0:T(8,128)(2,1)} %fusion.18), calls=%async_computation | async-start | bytes 1048576 | tf_op jit(solution)/shard_map/all_to_all | solution.py:1222
  186.8 536.8 %reduce-scatter.2.cloned.1.call-start = ((), (), s32[]{:S(2)}) async-start(), calls=%async_computation.4 | async-start | bytes 8912896 | tf_op jit(solution)/shard_map/reduce_scatter | solution.py:1358
  191.2 14.5 %copy-start.43 = (f32[32,16,128]{2,1,0:T(8,128)S(1)}, f32[32,16,128]{2,1,0:T(8,128)}, u32[]{:S(2)}) copy-start(f32[32,16,128]{2,1,0:T(8,128)} %get-tuple-element.79) | copy-start | bytes 786436
  441.1 14.2 %copy-start.54 = (f32[128]{0:T(128)}, f32[128]{0:T(128)S(1)}, u32[]{:S(2)}) copy-start(f32[128]{0:T(128)S(1)} %get-tuple-element.252) | copy-start | bytes 1540
  441.4 13.9 %copy-start.38 = (f32[128,16]{0,1:T(8,128)}, f32[128,16]{0,1:T(8,128)S(1)}, u32[]{:S(2)}) copy-start(f32[128,16]{0,1:T(8,128)S(1)} %get-tuple-element.247) | copy-start | bytes 24580
  451.3 76.8 %collective-permute-start.3 = (bf16[44,2048]{1,0:T(8,128)(2,1)}, bf16[44,2048]{1,0:T(8,128)(2,1)}, u32[]{:S(2)}, u32[]{:S(2)}) collective-permute-start(bf16[44,2048]{1,0:T(8,128)(2,1)} %dynamic-slice_bitcast_fusion.1), channel_id=1, source_target_pairs={{0,1},{1,0},{2,3},{3,2},{4,5},{5,4},{6,7},{7,6},{8,9},{9,8},{10,11... | collective-permute-start | bytes 540680 | tf_op jit(solution)/shard_map/ppermute | solution.py:1134
  455.0 74.9 %collective-permute-start.2 = (bf16[16,64,256]{2,1,0:T(8,128)(2,1)}, bf16[16,64,256]{2,1,0:T(8,128)(2,1)}, u32[]{:S(2)}, u32[]{:S(2)}) collective-permute-start(bf16[16,64,256]{2,1,0:T(8,128)(2,1)} %dynamic-slice_bitcast_fusion), channel_id=1, source_target_pairs={{0,1},{1,0},{2,3},{3,2},{4,5},{5,4},{6,7},{7,6},{8,9},{9,8},{10,11... | collective-permute-start | bytes 1572872 | tf_op jit(solution)/shard_map/ppermute | solution.py:1134
  459.7 18.8 %copy-start.3 = (bf16[128,2048]{1,0:T(8,128)(2,1)}, bf16[128,2048]{1,0:T(8,128)(2,1)S(1)}, u32[]{:S(2)}) copy-start(bf16[128,2048]{1,0:T(8,128)(2,1)S(1)} %get-tuple-element.221.d_res.refs_6_) | copy-start | bytes 1572868
  481.1 30.2 %copy-start.19 = (bf16[128,2048]{1,0:T(8,128)(2,1)S(1)}, bf16[128,2048]{1,0:T(8,128)(2,1)}, u32[]{:S(2)}) copy-start(bf16[128,2048]{1,0:T(8,128)(2,1)} %multiply_convert_fusion.refs_0_) | copy-start | bytes 1572868
  481.1 30.2 %copy-start.36 = (f32[2,2,8,1024]{3,2,0,1:T(8,128)S(1)}, f32[2,2,8,1024]{3,2,0,1:T(8,128)}, u32[]{:S(2)}) copy-start(f32[2,2,8,1024]{3,2,0,1:T(8,128)} %copy.90) | copy-start | bytes 393220
  481.1 30.2 %copy-start.39 = (f32[128,16]{0,1:T(8,128)S(1)}, f32[128,16]{0,1:T(8,128)}, u32[]{:S(2)}) copy-start(f32[128,16]{0,1:T(8,128)} %copy-done.38) | copy-start | bytes 24580
  481.1 30.2 %copy-start.53 = (f32[128]{0:T(128)S(1)}, f32[128]{0:T(128)}, u32[]{:S(2)}) copy-start(f32[128]{0:T(128)} %copy-done.52) | copy-start | bytes 1540
  481.1 30.2 %copy-start.55 = (f32[128]{0:T(128)S(1)}, f32[128]{0:T(128)}, u32[]{:S(2)}) copy-start(f32[128]{0:T(128)} %copy-done.54) | copy-start | bytes 1540
  481.1 30.2 %copy-start.57 = (f32[128]{0:T(128)S(1)}, f32[128]{0:T(128)}, u32[]{:S(2)}) copy-start(f32[128]{0:T(128)} %copy-done.56) | copy-start | bytes 1540
  481.1 30.2 %copy-start.63 = (f32[16]{0:T(128)S(1)}, f32[16]{0:T(128)}, u32[]{:S(2)}) copy-start(f32[16]{0:T(128)} %copy-done.62) | copy-start | bytes 196
  481.1 30.2 %copy-start.65 = (f32[128]{0:T(128)S(1)}, f32[128]{0:T(128)}, u32[]{:S(2)}) copy-start(f32[128]{0:T(128)} %copy-done.64) | copy-start | bytes 1540
  481.1 31.0 %copy-start.7 = (bf16[128,3072]{1,0:T(8,128)(2,1)S(1)}, bf16[128,3072]{1,0:T(8,128)(2,1)}, u32[]{:S(2)}) copy-start(bf16[128,3072]{1,0:T(8,128)(2,1)} %copy-done.6) | copy-start | bytes 2359300
  532.1 191.5 %all-to-all-start.1 = ((bf16[16,64,256]{2,1,0:T(8,128)(2,1)}), bf16[16,64,256]{2,1,0:T(8,128)(2,1)}, u32[]{:S(2)}, u32[]{:S(2)}) async-start(bf16[16,64,256]{2,1,0:T(8,128)(2,1)} %fusion.14), calls=%async_computation.1 | async-start | bytes 1048576 | tf_op jit(solution)/shard_map/all_to_all | solution.py:1403
  (59 other events, 350.4 us)
Sparse Core Ops, SparseCore 0:
  164.2 88.3 all-gather.1
  440.1 109.6 reduce-scatter.1

commit v5 on v4

--- a/solution.py
+++ b/solution.py
@@ -385,30 +385,63 @@
     return 256 if left.shape[1] % 256 == 0 else 128
 
 
+class Pairs:
+    def __init__(self, products):
+        self.arrays = []
+        self.uses = []
+        for pair in products:
+            use = []
+            for array in pair:
+                known = [i for i, other in enumerate(self.arrays) if other is array]
+                if not known:
+                    self.arrays.append(array)
+                    known = [len(self.arrays) - 1]
+                use.append(known[0])
+            self.uses.append(tuple(use))
+
+    def shapes(self):
+        arrays = self.arrays
+        return [
+            jax.ShapeDtypeStruct((arrays[i].shape[1], arrays[j].shape[1]), jnp.bfloat16)
+            for i, j in self.uses
+        ]
+
+    def room(self):
+        if not self.uses:
+            return []
+        arrays = self.arrays
+        held = [pltpu.VMEM(v.shape, v.dtype) for v in arrays]
+        ready = [
+            pltpu.VMEM((2, chunk_of(arrays[i]), arrays[j].shape[1]), jnp.bfloat16)
+            for i, j in self.uses
+        ]
+        dma = pltpu.SemaphoreType.DMA
+        return held + ready + [dma((len(arrays),)), dma((len(self.uses), 2))]
+
+
 class Products:
-    def __init__(self, lefts, rights, results, refs):
-        count = len(lefts)
-        held_left, held_right, ready = refs[:count], refs[count : 2 * count], refs[2 * count : 3 * count]
-        self.parts = list(zip(lefts, rights, results, held_left, held_right, ready))
-        if count:
-            self.in_sems, self.out_sems = refs[3 * count :]
-
-    def copies(self, i):
-        left, right, _, held_left, held_right, _ = self.parts[i]
-        return (
-            pltpu.make_async_copy(left, held_left, self.in_sems.at[i, 0]),
-            pltpu.make_async_copy(right, held_right, self.in_sems.at[i, 1]),
-        )
+    def __init__(self, uses, operands, results, refs):
+        self.uses = uses
+        if uses:
+            held = refs[: len(operands)]
+            self.loads = list(zip(operands, held))
+            self.in_sems, self.out_sems = refs[len(operands) + len(uses) :]
+            ready = refs[len(operands) : len(operands) + len(uses)]
+            self.parts = [(r, held[i], held[j], v) for (i, j), r, v in zip(uses, results, ready)]
+
+    def load(self, k):
+        source, held = self.loads[k]
+        return pltpu.make_async_copy(source, held, self.in_sems.at[k])
 
     def start(self):
-        for i in range(len(self.parts)):
-            for copy in self.copies(i):
-                copy.start()
+        for k in range(len(self.loads) if self.uses else 0):
+            self.load(k).start()
 
     def run(self, i):
-        for copy in self.copies(i):
-            copy.wait()
-        _, _, result, left, right, ready = self.parts[i]
+        earlier = [k for use in self.uses[:i] for k in use]
+        for k in sorted(set(self.uses[i]) - set(earlier)):
+            self.load(k).wait()
+        result, left, right, ready = self.parts[i]
         chunk = chunk_of(left)
         steps = left.shape[1] // chunk
 
@@ -434,52 +467,56 @@
             leave(j).wait()
 
 
-def products_room(products):
-    room = [pltpu.VMEM(v[0].shape, v[0].dtype) for v in products]
-    room = room + [pltpu.VMEM(v[1].shape, v[1].dtype) for v in products]
-    room = room + [pltpu.VMEM((2, chunk_of(v), w.shape[1]), jnp.bfloat16) for v, w in products]
-    if products:
-        room = room + [pltpu.SemaphoreType.DMA((len(products), 2))] * 2
-    return room
-
-
-def products_shapes(products):
-    return [jax.ShapeDtypeStruct((v.shape[1], w.shape[1]), jnp.bfloat16) for v, w in products]
-
-
-def exchange_kernel(place, shifts, pairs, *refs):
-    extra = len(shifts)
+def exchange_kernel(place, shifts, uses, operands, *refs):
+    extra, pairs = len(shifts), len(uses)
     given, refs = refs[:extra], refs[extra:]
-    lefts, rights, refs = refs[:pairs], refs[pairs : 2 * pairs], refs[2 * pairs :]
+    loads, refs = refs[:operands], refs[operands:]
+    left, right, refs = refs[0], refs[1], refs[2:]
     taken, results, refs = refs[:extra], refs[extra : extra + pairs], refs[extra + pairs :]
+    across, held, held_sem, refs = refs[0], refs[1], refs[2], refs[3:]
     p = place.here()
     p.greet_peers()
     swaps = Swaps(p, shifts, given, taken, *refs[:2])
     swaps.start()
-    products = Products(lefts, rights, results, refs[2:])
+    products = Products(uses, loads, results, refs[2:])
     products.start()
+    arrive = pltpu.make_async_copy(right, held, held_sem)
+    arrive.start()
     for i in range(pairs):
         products.run(i)
+    arrive.wait()
+    chunk = 256
+
+    def go(j, _):
+        part = pl.ds(pl.multiple_of(j * chunk, chunk), chunk)
+        across[:, part] = dot_across(left[...], held[part, :])
+        return 0
+
+    lax.fori_loop(0, held.shape[0] // chunk, go, 0)
     swaps.wait()
 
 
-def exchange(collective_id, swapped, products):
+def exchange(collective_id, swapped, products, left, right):
     place = Place(lax.axis_size("expert"), lax.axis_size("fsdp"), False)
     given, shifts = split_swaps(swapped)
-    extra, pairs = len(given), len(products)
-    lefts, rights = [v for v, _ in products], [w for _, w in products]
+    pairs = Pairs(products)
+    extra, operands = len(given), len(pairs.arrays)
+    anywhere, inside = pl.BlockSpec(memory_space=pl.ANY), pl.BlockSpec(memory_space=pltpu.VMEM)
+    dma = pltpu.SemaphoreType.DMA
     return pl.pallas_call(
-        functools.partial(exchange_kernel, place, shifts, pairs),
+        functools.partial(exchange_kernel, place, shifts, pairs.uses, operands),
         out_shape=[jax.ShapeDtypeStruct(s.shape, s.dtype) for s in given]
-        + products_shapes(products),
-        in_specs=[pl.BlockSpec(memory_space=pl.ANY)] * (extra + 2 * pairs),
-        out_specs=[pl.BlockSpec(memory_space=pl.ANY)] * (extra + pairs),
-        scratch_shapes=[pltpu.SemaphoreType.DMA((extra,))] * 2 + products_room(products),
+        + pairs.shapes()
+        + [jax.ShapeDtypeStruct((left.shape[0], right.shape[0]), jnp.float32)],
+        in_specs=[anywhere] * (extra + operands) + [inside, anywhere],
+        out_specs=[anywhere] * (extra + len(products)) + [inside],
+        scratch_shapes=[pltpu.VMEM(right.shape, right.dtype), dma, dma((extra,)), dma((extra,))]
+        + pairs.room(),
         compiler_params=pltpu.CompilerParams(
             collective_id=collective_id, has_side_effects=True, vmem_limit_bytes=56 << 20
         ),
         name=f"exchange{collective_id}",
-    )(*given, *lefts, *rights)
+    )(*given, *pairs.arrays, left, right)
 
 
 def outer_kernel(count, *refs):
@@ -498,7 +535,7 @@
 def outer_products(products):
     return pl.pallas_call(
         functools.partial(outer_kernel, len(products)),
-        out_shape=products_shapes(products),
+        out_shape=Pairs(products).shapes(),
         in_specs=[pl.BlockSpec(memory_space=pltpu.VMEM)] * (2 * len(products)),
         out_specs=[pl.BlockSpec(memory_space=pltpu.VMEM)] * len(products),
         compiler_params=pltpu.CompilerParams(vmem_limit_bytes=32 << 20),
@@ -506,11 +543,10 @@
     )(*[v for v, _ in products], *[w for _, w in products])
 
 
-def scatter_kernel(place, count, shifts, pairs, *refs):
-    total = count + len(shifts)
+def scatter_kernel(place, count, shifts, uses, operands, *refs):
+    total, pairs = count + len(shifts), len(uses)
     ins, given = refs[:count], refs[count:total]
-    lefts, rights = refs[total : total + pairs], refs[total + pairs : total + 2 * pairs]
-    refs = refs[total + 2 * pairs :]
+    loads, refs = refs[total : total + operands], refs[total + operands :]
     outs, taken, results = refs[:count], refs[count:total], refs[total : total + pairs]
     refs = refs[total + pairs :]
     held, side, rows_y, rows_z, rows_x, rows_e = (
@@ -625,13 +661,13 @@
 
             add(a, held[a].at[k, p.y], [side[a].at[k, p.y]])
 
-    products = Products(lefts, rights, results, room)
-    last = depth * across - 1
+    products = Products(uses, loads, results, room)
+    items = depth * across
 
     def second(z, x, way, number):
         k = z * across + x
         for i in range(pairs):
-            turn = min(i, last)
+            turn = i * items // pairs
             if (way is None) == (turn >= (depth - 1) * across):
                 pl.when(number == turn)(functools.partial(products.run, i))
         for a in range(count):
@@ -683,12 +719,36 @@
                         p.device(p.z, p.y, p.c, x),
                     ).start()
 
+    ahead = min(across + 1 if across > 1 else 2, items)
+    lower = 1 - p.z // half
+    switch = lower * (depth - 1 - p.z) + (1 - lower) * p.z
+
+    def first_at(number):
+        j = number // across
+        own = j // (depth - 1)
+        past = (j - switch + depth) // depth
+        down, up = depth - 1 - j, j
+        down_late, up_late = depth - 1 - (j - switch), j - switch
+        z = lower * ((1 - past) * down + past * up_late)
+        z = z + (1 - lower) * ((1 - past) * up + past * down_late)
+        z = own * p.z + (1 - own) * z
+        first(z, (p.x + 1 + number % across) % across, None, number)
+
+    def both(z, x, way, number):
+        if way is not None:
+
+            @pl.when(number + ahead < items)
+            def _():
+                first_at(number + ahead)
+
+        second(z, x, way, number)
+
     swaps = Swaps(p, shifts, given, taken, given_sem, taken_sem)
     swaps.start()
     in_order(begin)
     products.start()
-    in_order(first)
-    in_order(second)
+    lax.fori_loop(0, ahead, lambda n, _: (first_at(n), 0)[1], 0)
+    in_order(both)
     k = p.z * across + p.x
     for a in range(count):
         mine = held[a].at[k, p.y]
@@ -737,8 +797,8 @@
     group, peers = lax.axis_size("expert"), lax.axis_size("fsdp")
     place = Place(group, peers, wide)
     given, shifts = split_swaps(swapped)
-    count, extra, pairs = len(partials), len(given), len(products)
-    lefts, rights = [v[0] for v in products], [v[1] for v in products]
+    pairs = Pairs(products)
+    count, extra, operands = len(partials), len(given), len(pairs.arrays)
     dma = pltpu.SemaphoreType.DMA
     items = place.depth * place.across
 
@@ -746,14 +806,14 @@
         return [pltpu.VMEM(lead + s.shape[1:], s.dtype) for s in partials]
 
     return pl.pallas_call(
-        functools.partial(scatter_kernel, place, count, shifts, pairs),
+        functools.partial(scatter_kernel, place, count, shifts, pairs.uses, operands),
         out_shape=[jax.ShapeDtypeStruct(s.shape[1:], jnp.float32) for s in partials]
         + [jax.ShapeDtypeStruct(s.shape, s.dtype) for s in given]
-        + products_shapes(products),
-        in_specs=[pl.BlockSpec(memory_space=pl.ANY)] * (count + extra + 2 * pairs),
+        + pairs.shapes(),
+        in_specs=[pl.BlockSpec(memory_space=pl.ANY)] * (count + extra + operands),
         out_specs=[pl.BlockSpec(memory_space=pltpu.VMEM)] * count
         + [pl.BlockSpec(memory_space=pl.ANY)] * extra
-        + [pl.BlockSpec(memory_space=pl.ANY)] * pairs,
+        + [pl.BlockSpec(memory_space=pl.ANY)] * len(products),
         scratch_shapes=room(items, place.tall)
         + room(items, place.tall)
         + room(items, max(place.tall - 1, 1))
@@ -775,12 +835,12 @@
             dma((count,)),
             dma((count, place.across * max(place.tall - 1, 1))),
         ]
-        + products_room(products),
+        + pairs.room(),
         compiler_params=pltpu.CompilerParams(
             collective_id=collective_id, has_side_effects=True, vmem_limit_bytes=60 << 20
         ),
         name=f"scatter{collective_id}",
-    )(*partials, *given, *lefts, *rights)
+    )(*partials, *given, *pairs.arrays)
 
 
 def dot_plain(left, right):
@@ -1340,19 +1400,21 @@
             (rows_in[1], d_hidden_u),
             (act, d_out[1]),
             (rows_in[0], d_hidden_g),
+            (rows_in[0], d_hidden_u),
+            (act, d_out[0]),
         ]
         if peers == 2
         else [],
     )
     gate_blocks = more[: peers - 1]
     if peers == 2:
-        d_gu_weight, d_sd, *others, gate_own = more[1:]
+        d_gu_weight, d_sd, *others, gate_own, up_own, down_own = more[1:]
     else:
         d_gu_weight = outer(hid_plane, d_gu).astype(bf16)
         d_sd = outer(shared_scaled, cot_plane).astype(bf16)
         others = [up_term(r).astype(bf16) for r in turns]
         others = others + [down_term(r).astype(bf16) for r in turns]
-        gate_own = gate_term(0)
+        gate_own, up_own, down_own = gate_term(0), up_term(0), down_term(0)
     d_sd = d_sd[:units]
     out_part, d_hidden_two = lax.optimization_barrier((out_part, d_hidden_two))
     out_sum = lax.psum_scatter(
@@ -1387,16 +1449,19 @@
 
     swapped = [(own_rows(d_keyval_all, r).astype(bf16), r) for r in turns]
     swapped = swapped + [(own_rows(d_key_rot, r).astype(bf16), r) for r in turns]
-    *arrived, d_output_w, d_query_w, up_own, down_own = exchange(
+    *arrived, d_output_w, d_query_w, d_hidden_one = exchange(
         4,
         swapped,
-        [
-            (context, d_residual_low),
-            (hidden_one, d_query),
-            (rows_in[0], d_hidden_u),
-            (act, d_out[0]),
-        ],
-    )
+        [(context, d_residual_low), (hidden_one, d_query)],
+        d_query,
+        w_query,
+    )
+    up_others, arrived[0] = lax.optimization_barrier((others[: peers - 1], arrived[0]))
+    size = peers
+    up_blocks = [
+        lax.ppermute(w, "fsdp", [(j, (j + r) % size) for j in range(size)])
+        for w, r in zip(up_others, turns)
+    ]
     own_dkeyval = plus(own_rows(d_keyval_all, 0).astype(f32), arrived[: peers - 1])
     own_dkeyrot = plus(own_rows(d_key_rot, 0), arrived[peers - 1 :])
     gu_sum, own_dkeyval = lax.optimization_barrier((gu_sum, own_dkeyval))
@@ -1408,7 +1473,7 @@
         [d_latent_raw, rotate_back(own_dkeyrot, cosine, sine_vals)], axis=-1
     ).astype(bf16)
     d_compress_w, d_expand_w = outer_products([(hidden_one, d_compressed), (latent, d_keyval)])
-    d_hidden_one = back(d_query, w_query) + back(d_compressed, w_compress)
+    d_hidden_one = d_hidden_one + back(d_compressed, w_compress)
     d_tokens, d_attn_gain = norm_back(d_hidden_one, tokens_f, inverse_one, gain_attn)
     tokens_grad = d_tokens + d_residual
     def lanes(vector):
@@ -1433,15 +1498,15 @@
         dense + [small_grads],
         True,
         3,
-        [(w, r) for w, r in zip(others, [*turns, *turns])],
+        [(w, r) for w, r in zip(others[peers - 1 :], turns)],
     )
     gu_sum, out_sum, smalls = lax.optimization_barrier((gu_sum, out_sum, smalls))
     mixed = (residual + out_sum.astype(f32)).astype(bf16)
     gu_sum = gu_sum.astype(f32).transpose(1, 0, 2)
     sgate_grad = gu_sum[:, :, :units].reshape(shared_gate.shape)
     sup_grad = gu_sum[:, :, units + lanes_more : 2 * units + lanes_more].reshape(shared_up.shape)
-    eup_grad = plus(up_own.astype(f32), blocks[: peers - 1])[None]
-    edown_grad = plus(down_own.astype(f32), blocks[peers - 1 :])[None]
+    eup_grad = plus(up_own.astype(f32), up_blocks)[None]
+    edown_grad = plus(down_own.astype(f32), blocks)[None]
     attn_gain_grad = smalls[0, : attn_gain.shape[0]]
     kv_gain_grad = smalls[1, : kv_gain.shape[0]]
     ffn_gain_grad = smalls[2, : ffn_gain.shape[0]]

time: 751 us -> 732 us (0.975)
  Pallas kernels: 578 us -> 565 us
  matrix products: 42.1 us -> 32.2 us
    pallas_call x2, Pallas kernels: 219 us -> 209 us  [scatter(): pl.pallas_call(functools.partial(scatter_kernel, place, count, shifts, pa...]
    dot_general x4 -> x3, matrix products: 19.4 us -> 9.62 us  [back(): lax.dot_general(left, weight, (((1,), (1,)), ((), ())), preferred_element...]
    unnamed x157 -> x171, local copies, waits for them, and re-layouts: 15.6 us -> 14.6 us
  transfers between devices with their start and end apart: 8 -> 9, of which waited for: 0 -> 0; matrix products, arithmetic and copies ran while one was open for 12% -> 11% of each run, Pallas kernels for 38% -> 38%
where the time goes in v5:
time: 732 us; the launch traced here: 720 us
  Pallas kernels  565 us (77%)
  other arithmetic  47.4 us (6%)
  local copies, waits for them, and re-layouts  36.3 us (5%)
  matrix products  32.2 us (4%)
  between operations  17.5 us (2%)
  starting transfers between devices  15.7 us (2%)
    pallas_call x2, Pallas kernels, gather(): pl.pallas_call(functools.partial(gather_kernel, place, count, shifts), ou...  217 us
    pallas_call x2, Pallas kernels, scatter(): pl.pallas_call(functools.partial(scatter_kernel, place, count, shifts, pa...  209 us
    pallas_call x1, Pallas kernels, ffn(): pl.pallas_call(functools.partial(ffn_kernel, peers, sources), out_shape=[...  76.4 us
    pallas_call x1, Pallas kernels, exchange(): pl.pallas_call(functools.partial(exchange_kernel, place, shifts, pairs.us...  27.6 us
    pallas_call x1, Pallas kernels, attend_back(): pl.pallas_call(attend_back_kernel, out_shape=[jax.ShapeDtypeStruct(query....  16.7 us
  transfers between devices with their start and end apart: 9, of which 0 were waited for; matrix products, arithmetic and copies ran while one was open for 11% of the time, Pallas kernels for 38%

profile of v5, /device:TPU:0, one launch (start us, length us, event | category | flops | bytes accessed | tf_op | source)
XLA Modules:
  0.0 720.0 jit_solution(5716350052780658419)
XLA Ops:
  14.0 150.1 %gather0.1 = (bf16[32,64,3072]{2,1,0:T(8,128)(2,1)}, bf16[32,64,576]{2,1,0:T(8,128)(2,1)}, bf16[32,16,4096]{2,1,0:T(8,128)(2,1)}, bf16[32,64,2048]{2,1,0:T(8,128...) custom-call(bf16[64,3072]{1,0:T(8,128)(2,1)} %refs_0_.1, ...), custom_call_target="tpu_custom_call" | custom-call | tf_op jit(solution)/shard_map/gather0/pallas_call | solution.py:363
  168.3 2.4 fusion.54
  171.9 6.0 all_gather.6
  181.5 5.4 all-to-all-start
  189.2 2.2 copy-done
  191.4 14.2 %attend.1 = (bf16[128,3072]{1,0:T(8,128)(2,1)S(1)}, bf16[256,4096]{1,0:T(8,128)(2,1)S(1)}, f32[16,128,256]{2,1,0:T(8,128)S(1)}, bf16[128,2048]{1,0:T(8,128)(2,1)S(1)}) custom-call(s32[2]{0:T(128)S(1)} %pad_add_fusion.numbers, bf16[128,2048]{1,0:T(8,128)(2,1)S(1)} %fusion.7.hidden.refs_4_.refs_0_, bf16[2048,3072]{1,0:T(8,128)(2,1)} %bitcast.120, ...), custom_call_target="tpu_custom_call" | custom-call | tf_op jit(solution)/shard_map/attend/pallas_call | solution.py:1081
  205.8 6.7 multiply_reduce_fusion.2
  218.4 67.3 %gather1.1 = (bf16[16,128,2048]{2,1,0:T(8,128)(2,1)}, bf16[16,64,256]{2,1,0:T(8,128)(2,1)}) custom-call(bf16[128,2048]{1,0:T(8,128)(2,1)} %multiply_convert_fusion.refs_0_, bf16[16,64,256]{2,1,0:T(8,128)(2,1)} %all-to-all-done.refs_1_), custom_call_target="tpu_custom_call" | custom-call | tf_op jit(solution)/shard_map/gather1/pallas_call | solution.py:363
  285.8 2.1 fusion.4
  288.9 76.4 %ffn.1 = (bf16[1024,1024]{1,0:T(8,128)(2,1)}, bf16[1024,1024]{1,0:T(8,128)(2,1)}, bf16[1024,1024]{1,0:T(8,128)(2,1)}, bf16[1024,1024]{1,0:T(8,128)(2,1)}, bf16[1...) custom-call(s32[19]{0:T(128)} %pad_add_fusion.1.numbers, ...), custom_call_target="tpu_custom_call" | custom-call | flops 53150220288 | bytes 62914560 | tf_op jit(solution)/shard_map/ffn/pallas_call | solution.py:988
  365.3 7.5 %convolution_convert_fusion.refs_1_ = bf16[1024,1408]{1,0:T(8,128)(2,1)} fusion(bf16[1024,1024]{1,0:T(8,128)(2,1)} %get-tuple-element.96.refs_6_, bf16[1024,1408]{1,0:T(8,128)(2,1)} %get-tuple-element.97.refs_11_), kind=kOutput, calls=%fused_computation.3 | convolution fusion | flops 2954231808 | bytes 7864320 | tf_op jit(solution)/shard_map/dot_general | solution.py:1366
  372.8 66.6 %scatter2.1 = (f32[128,2048]{1,0:T(8,128)}, bf16[1024,1408]{1,0:T(8,128)(2,1)}, bf16[2048,256]{1,0:T(8,128)(2,1)}, bf16[128,2048]{1,0:T(8,128)(2,1)}, bf16[1024,...) custom-call(bf16[16,128,2048]{2,1,0:T(8,128)(2,1)} %get-tuple-elemen, ...), custom_call_target="tpu_custom_call" | custom-call | tf_op jit(solution)/shard_map/scatter2/pallas_call | solution.py:808
  455.7 3.2 multiply_reduce_fusion
  462.2 16.7 %attend_back.1 = (bf16[128,3072]{1,0:T(8,128)(2,1)S(1)}, bf16[256,4096]{1,0:T(8,128)(2,1)S(1)}, f32[256,128]{1,0:T(8,128)S(1)}) custom-call(bf16[128,2048]{1,0:T(8,128)(2,1)S(1)} %get-tuple-element.225.d_res.refs_3_, bf16[2048,2048]{1,0:T(8,128)(2,1)} %bitcast.119, bf16[128,3072]{1,0:T(8,128)(2,1)S(1)} %copy-done.13, bf16[256,4096]{1,0:T(8,128)(2,1)S(1)} %copy-done.9, ...), custom_call_target="tpu_custom_call" | custom-call | tf_op jit(solution)/shard_map/attend_back/pallas_call | solution.py:1156
  481.5 27.6 %exchange4.1 = (bf16[128,4096]{1,0:T(8,128)(2,1)}, bf16[128,64]{1,0:T(8,128)(2,1)}, bf16[2048,2048]{1,0:T(8,128)(2,1)}, bf16[2048,3072]{1,0:T(8,128)(2,1)}, f32[128,2048]{1,0:T(8,128)}) custom-call(bf16[128,4096]{1,0:T(8,128)(2,1)} %constant_dynamic-slice_fusion.refs_0_, bf16[128,64]{1,0:T(8,128)(2,1)} %dynamic-slice_convert_fusion.refs_1_, ...), custom_call_target="tpu_custom_call" | custom-call | tf_op jit(solution)/shard_map/exchange4/pallas_call | solution.py:506
  512.3 5.0 add_bitcast_fusion.2
  521.8 2.2 fusion.14
  523.9 4.7 all-to-all-start.1
  528.6 3.9 multiply_reduce_fusion.3
  534.3 3.7 outer.1
  541.6 2.6 fusion.13
  545.1 142.1 %scatter3.1 = (f32[64,3072]{1,0:T(8,128)}, f32[64,576]{1,0:T(8,128)}, f32[16,4096]{1,0:T(8,128)}, f32[64,2048]{1,0:T(8,128)}, f32[64,16]{1,0:T(8,128)}, /*index=5*/f32[8,128]{1,0:T(8,128)}, bf16[1408,1024]{1,0:T(8,128)(2,1)}) custom-call(bf16[32,64,3072]{2,1,0:T(8,128)(2,1)} %bitcast.122, bf16[32,64,576]{2,1,0:T(8,128)(2,1)} %bitcast.115, ...), custom_call_target="tpu_custom_call" | custom-call | tf_op jit(solution)/shard_map/scatter3/pallas_call | solution.py:808
  687.3 6.6 add_bitcast_fusion
  696.0 5.8 add_bitcast_fusion.1
  (289 shorter events, 71.8 us)
Async XLA Ops:
  7.2 281.7 %all-gather.2.cloned.1.call-start = ((), (), s32[]{:S(2)}) async-start(), calls=%async_computation.3 | async-start | bytes 8912896 | tf_op jit(solution)/shard_map/all_gather | solution.py:1288
  14.0 153.1 %copy-start.14 = (bf16[128,2048]{1,0:T(8,128)(2,1)S(1)}, bf16[128,2048]{1,0:T(8,128)(2,1)}, u32[]{:S(2)}) copy-start(bf16[128,2048]{1,0:T(8,128)(2,1)} %param.18) | copy-start | bytes 1572868
  164.1 51.9 %collective-permute-start.1 = (bf16[44,2048]{1,0:T(8,128)(2,1)}, bf16[44,2048]{1,0:T(8,128)(2,1)}, u32[]{:S(2)}, u32[]{:S(2)}) collective-permute-start(bf16[44,2048]{1,0:T(8,128)(2,1)} %param.32), channel_id=1, source_target_pairs={{0,1},{1,0},{2,3},{3,2},{4,5},{5,4},{6,7},{7,6},{8,9},{9,8},{10,11... | collective-permute-start | bytes 540680 | tf_op jit(solution)/shard_map/ppermute | solution.py:1186
  165.8 275.4 %copy-start.75 = (f32[16]{0:T(128)}, f32[16]{0:T(128)S(1)}, u32[]{:S(2)}) copy-start(f32[16]{0:T(128)S(1)} %get-tuple-element.219) | copy-start | bytes 196
  168.0 21.2 %copy-start.1 = (bf16[128,2048]{1,0:T(8,128)(2,1)}, bf16[128,2048]{1,0:T(8,128)(2,1)S(1)}, u32[]{:S(2)}) copy-start(bf16[128,2048]{1,0:T(8,128)(2,1)S(1)} %fusion.7.hidden.refs_4_.refs_0_) | copy-start | bytes 1572868
  168.0 11.5 %copy-start.34 = (bf16[64,1408]{1,0:T(8,128)(2,1)S(1)}, bf16[64,1408]{1,0:T(8,128)(2,1)}, u32[]{:S(2)}) copy-start(bf16[64,1408]{1,0:T(8,128)(2,1)} %param.30) | copy-start | bytes 540676
  168.3 11.7 %copy-start.35 = (bf16[64,1408]{1,0:T(8,128)(2,1)S(1)}, bf16[64,1408]{1,0:T(8,128)(2,1)}, u32[]{:S(2)}) copy-start(bf16[64,1408]{1,0:T(8,128)(2,1)} %param.31) | copy-start | bytes 540676
  177.9 111.0 %collective-permute-start = (bf16[1408,1024]{1,0:T(8,128)(2,1)}, bf16[1408,1024]{1,0:T(8,128)(2,1)}, u32[]{:S(2)}, u32[]{:S(2)}) collective-permute-start(bf16[1408,1024]{1,0:T(8,128)(2,1)} %bitcast.11.refs_7_), channel_id=1, source_target_pairs={{0,1},{1,0},{2,3},{3,2},{4,5},{5,4},{6,7},{7,6},{8,9},{9,8},{10,11... | collective-permute-start | bytes 8650760 | tf_op jit(solution)/shard_map/ppermute | solution.py:1186
  181.5 36.9 %all-to-all-start = ((bf16[16,64,256]{2,1,0:T(8,128)(2,1)}), bf16[16,64,256]{2,1,0:T(8,128)(2,1)}, u32[]{:S(2)}, u32[]{:S(2)}) async-start(bf16[16,64,256]{2,1,0:T(8,128)(2,1)} %fusion.18), calls=%async_computation | async-start | bytes 1048576 | tf_op jit(solution)/shard_map/all_to_all | solution.py:1282
  186.9 514.9 %reduce-scatter.2.cloned.1.call-start = ((), (), s32[]{:S(2)}) async-start(), calls=%async_computation.4 | async-start | bytes 8912896 | tf_op jit(solution)/shard_map/reduce_scatter | solution.py:1420
  191.4 14.3 %copy-start.37 = (f32[32,16,128]{2,1,0:T(8,128)S(1)}, f32[32,16,128]{2,1,0:T(8,128)}, u32[]{:S(2)}) copy-start(f32[32,16,128]{2,1,0:T(8,128)} %get-tuple-element.81) | copy-start | bytes 786436
  441.1 14.5 %copy-start.32 = (f32[128,16]{0,1:T(8,128)}, f32[128,16]{0,1:T(8,128)S(1)}, u32[]{:S(2)}) copy-start(f32[128,16]{0,1:T(8,128)S(1)} %get-tuple-element.251) | copy-start | bytes 24580
  451.7 68.4 %collective-permute-start.3 = (bf16[44,2048]{1,0:T(8,128)(2,1)}, bf16[44,2048]{1,0:T(8,128)(2,1)}, u32[]{:S(2)}, u32[]{:S(2)}) collective-permute-start(bf16[44,2048]{1,0:T(8,128)(2,1)} %dynamic-slice_bitcast_fusion.1), channel_id=1, source_target_pairs={{0,1},{1,0},{2,3},{3,2},{4,5},{5,4},{6,7},{7,6},{8,9},{9,8},{10,11... | collective-permute-start | bytes 540680 | tf_op jit(solution)/shard_map/ppermute | solution.py:1194
  454.6 67.1 %collective-permute-start.2 = (bf16[16,64,256]{2,1,0:T(8,128)(2,1)}, bf16[16,64,256]{2,1,0:T(8,128)(2,1)}, u32[]{:S(2)}, u32[]{:S(2)}) collective-permute-start(bf16[16,64,256]{2,1,0:T(8,128)(2,1)} %dynamic-slice_bitcast_fusion), channel_id=1, source_target_pairs={{0,1},{1,0},{2,3},{3,2},{4,5},{5,4},{6,7},{7,6},{8,9},{9,8},{10,11... | collective-permute-start | bytes 1572872 | tf_op jit(solution)/shard_map/ppermute | solution.py:1194
  460.4 18.5 %copy-start.3 = (bf16[128,2048]{1,0:T(8,128)(2,1)}, bf16[128,2048]{1,0:T(8,128)(2,1)S(1)}, u32[]{:S(2)}) copy-start(bf16[128,2048]{1,0:T(8,128)(2,1)S(1)} %get-tuple-element.225.d_res.refs_3_) | copy-start | bytes 1572868
  481.4 30.0 %copy-start.33 = (f32[128,16]{0,1:T(8,128)S(1)}, f32[128,16]{0,1:T(8,128)}, u32[]{:S(2)}) copy-start(f32[128,16]{0,1:T(8,128)} %copy-done.32) | copy-start | bytes 24580
  481.4 30.0 %copy-start.52 = (f32[128]{0:T(128)S(1)}, f32[128]{0:T(128)}, u32[]{:S(2)}) copy-start(f32[128]{0:T(128)} %copy-done.50) | copy-start | bytes 1540
  481.4 30.0 %copy-start.55 = (f32[128]{0:T(128)S(1)}, f32[128]{0:T(128)}, u32[]{:S(2)}) copy-start(f32[128]{0:T(128)} %copy-done.53) | copy-start | bytes 1540
  481.4 30.0 %copy-start.58 = (f32[128]{0:T(128)S(1)}, f32[128]{0:T(128)}, u32[]{:S(2)}) copy-start(f32[128]{0:T(128)} %copy-done.56) | copy-start | bytes 1540
  481.4 30.0 %copy-start.68 = (f32[16]{0:T(128)S(1)}, f32[16]{0:T(128)}, u32[]{:S(2)}) copy-start(f32[16]{0:T(128)} %copy-done.66) | copy-start | bytes 196
  481.5 30.0 %copy-start.70 = (f32[128]{0:T(128)S(1)}, f32[128]{0:T(128)}, u32[]{:S(2)}) copy-start(f32[128]{0:T(128)} %get-tuple-element.224) | copy-start | bytes 1540
  481.5 30.9 %copy-start.22 = (bf16[1024,1408]{1,0:T(8,128)(2,1)S(1)}, bf16[1024,1408]{1,0:T(8,128)(2,1)}, u32[]{:S(2)}) copy-start(bf16[1024,1408]{1,0:T(8,128)(2,1)} %get-tuple-element.140) | copy-start | bytes 8650756
  509.1 186.9 %collective-permute-start.4 = (bf16[1024,1408]{1,0:T(8,128)(2,1)}, bf16[1024,1408]{1,0:T(8,128)(2,1)}, u32[]{:S(2)}, u32[]{:S(2)}) collective-permute-start(bf16[1024,1408]{1,0:T(8,128)(2,1)} %get-tuple-element.142), channel_id=1, source_target_pairs={{0,1},{1,0},{2,3},{3,2},{4,5},{5,4},{6,7},{7,6},{8,9},{9,8},{10,11... | collective-permute-start | bytes 8650760 | tf_op jit(solution)/shard_map/ppermute | solution.py:1462
  523.9 177.9 %all-to-all-start.1 = ((bf16[16,64,256]{2,1,0:T(8,128)(2,1)}), bf16[16,64,256]{2,1,0:T(8,128)(2,1)}, u32[]{:S(2)}, u32[]{:S(2)}) async-start(bf16[16,64,256]{2,1,0:T(8,128)(2,1)} %fusion.14), calls=%async_computation.1 | async-start | bytes 1048576 | tf_op jit(solution)/shard_map/all_to_all | solution.py:1468
  (67 other events, 358.0 us)
Sparse Core Ops, SparseCore 0:
  164.2 88.5 all-gather.1
  439.6 115.7 reduce-scatter.1

commit v6 on v5

--- a/solution.py
+++ b/solution.py
@@ -177,10 +177,13 @@
             copy.wait()
 
 
-def gather_kernel(place, count, shifts, *refs):
+def gather_kernel(place, count, shifts, spans, into, *refs):
     total = count + len(shifts)
-    ins, outs = refs[:count], refs[total : total + count]
-    given, taken = refs[count:total], refs[total + count : 2 * total]
+    ins, given = refs[:count], refs[count:total]
+    refs = refs[:total] + refs[total + into :]
+    outs, taken = refs[total : total + count], refs[total + count : 2 * total]
+    given = [w if at is None else w.at[pl.ds(*at)] for w, at in zip(given, spans)]
+    taken = [w if at is None else w.at[pl.ds(*at)] for w, at in zip(taken, spans)]
     near, xs, ys, cs, rc, zs, got, given_sem, taken_sem, es = refs[2 * total :]
     p = place.here()
     depth, tall, across = p.depth, p.tall, p.across
@@ -357,15 +360,19 @@
 def gather(shards, wide, collective_id, swapped=()):
     group, peers = lax.axis_size("expert"), lax.axis_size("fsdp")
     place = Place(group, peers, wide)
-    given, shifts = split_swaps(swapped)
+    given, shifts = split_swaps([w[:2] for w in swapped])
+    spans = [w[2] if len(w) > 2 else None for w in swapped]
+    into = {i: w[3] for i, w in enumerate(swapped) if len(w) > 3}
     count, extra = len(shards), len(given)
+    aliases = {count + extra + j: count + i for j, i in enumerate(into)}
     dma = pltpu.SemaphoreType.DMA
     return pl.pallas_call(
-        functools.partial(gather_kernel, place, count, shifts),
+        functools.partial(gather_kernel, place, count, shifts, spans, len(into)),
         out_shape=[jax.ShapeDtypeStruct((place.slots,) + s.shape, s.dtype) for s in shards]
         + [jax.ShapeDtypeStruct(s.shape, s.dtype) for s in given],
-        in_specs=[pl.BlockSpec(memory_space=pl.ANY)] * (count + extra),
+        in_specs=[pl.BlockSpec(memory_space=pl.ANY)] * (count + extra + len(into)),
         out_specs=[pl.BlockSpec(memory_space=pl.ANY)] * (count + extra),
+        input_output_aliases=aliases,
         scratch_shapes=[dma((count,))] * 5
         + [
             dma((count, 2, place.depth * place.across)),
@@ -378,7 +385,7 @@
             collective_id=collective_id, has_side_effects=True, vmem_limit_bytes=58 << 20
         ),
         name=f"gather{collective_id}",
-    )(*shards, *given)
+    )(*shards, *given, *into.values())
 
 
 def chunk_of(left):
@@ -952,18 +959,20 @@
     d_su = (d_s * (sg * s_sigma)).astype(bf16)
     s_grad[:, pl.ds(0, units)] = d_sg
     s_grad[:, pl.ds(units, units)] = d_su
-    for s in range(sources):
-        part = slice(s * capacity, (s + 1) * capacity)
-        span = slice(s * tok_rows, (s + 1) * tok_rows)
-        for r in range(peers):
-            out_part[s, :, columns(r)] = (
-                dot_turned(picks[s], weighted[r][part])
-                + dot_plain(s_low[span], shared_out[:, columns(r)])
-            ).astype(bf16)
-            back_part[s, :, columns(r)] = (
-                dot_turned(picks[s], d_rows[r][part])
-                + dot_across(s_grad[span, :], shared_in[columns(r), :])
-            ).astype(bf16)
+    for r in range(peers):
+        for n in range(0, width, 256):
+            at = pl.ds(pl.multiple_of((fid + r) % peers * width + n, 256), 256)
+            s_out = dot_plain(s_low, shared_out[:, at])
+            s_back = dot_across(s_grad[...], shared_in[at, :])
+            for s in range(sources):
+                part = slice(s * capacity, (s + 1) * capacity)
+                span = slice(s * tok_rows, (s + 1) * tok_rows)
+                out_part[s, :, at] = (
+                    dot_turned(picks[s], weighted[r][part, n : n + 256]) + s_out[span]
+                ).astype(bf16)
+                back_part[s, :, at] = (
+                    dot_turned(picks[s], d_rows[r][part, n : n + 256]) + s_back[span]
+                ).astype(bf16)
 
 
 def ffn(capacity, numbers, fill, hid, cot, ranks, gates, ups, downs, router, shared_in, shared_out):
@@ -1253,10 +1262,10 @@
         [q_weight, kva_weight, kvb_weight, out_weight, router_weight, small],
         True,
         0,
-        [(expert_gate[0], -r) for r in turns] + [(expert_up[0], -r) for r in turns],
+        [(expert_gate[0], -r) for r in turns] + [(expert_up[0], -r, (0, half // 2)) for r in turns],
     )
     gate_parts = [expert_gate[0]] + more[: peers - 1]
-    up_parts = [expert_up[0]] + more[peers - 1 :]
+    up_begun = more[peers - 1 :]
     w_query, w_compress, w_expand, w_output, w_router = (
         w.reshape(-1, w.shape[-1]) for w in (w_query, w_compress, w_expand, w_output, w_router)
     )
@@ -1322,8 +1331,16 @@
     residual = tokens_f + jnp.dot(context, w_output, preferred_element_type=f32)
     normed_two, inverse_two = rms_norm(residual, gain_ffn)
     hidden_two = normed_two.astype(bf16)
-    hid3, *more = gather([hidden_two], False, 1, [(pieces, -r) for r in turns])
-    gu_weight = jnp.roll(jnp.stack([pieces] + more), fid, axis=0)
+    rest = (half // 2, half // 2)
+    hid3, *more = gather(
+        [hidden_two],
+        False,
+        1,
+        [(pieces, -r) for r in turns]
+        + [(expert_up[0], -r, rest, w) for r, w in zip(turns, up_begun)],
+    )
+    up_parts = [expert_up[0]] + more[peers - 1 :]
+    gu_weight = jnp.roll(jnp.stack([pieces] + more[: peers - 1]), fid, axis=0)
     gu_weight = gu_weight.transpose(1, 0, 2, 3).reshape(dim, -1)
     hid_plane = hid3.reshape(plane_rows, dim)
     cot3 = cot_plane.reshape(group, tok_rows, dim)

time: 732 us -> 722 us (0.986)
  Pallas kernels: 565 us -> 554 us
  transfers between devices with their start and end apart: 9 -> 9, of which waited for: 0 -> 0; matrix products, arithmetic and copies ran while one was open for 11% -> 12% of each run, Pallas kernels for 38% -> 38%
where the time goes in v6:
time: 722 us; the launch traced here: 710 us
  Pallas kernels  554 us (77%)
  other arithmetic  47.4 us (7%)
  local copies, waits for them, and re-layouts  36.1 us (5%)
  matrix products  32.7 us (5%)
  between operations  17.5 us (2%)
  starting transfers between devices  14.8 us (2%)
    pallas_call x2, Pallas kernels, gather(): pl.pallas_call(functools.partial(gather_kernel, place, count, shifts, spa...  211 us
    pallas_call x2, Pallas kernels, scatter(): pl.pallas_call(functools.partial(scatter_kernel, place, count, shifts, pa...  209 us
    pallas_call x1, Pallas kernels, ffn(): pl.pallas_call(functools.partial(ffn_kernel, peers, sources), out_shape=[...  73.3 us
    pallas_call x1, Pallas kernels, exchange(): pl.pallas_call(functools.partial(exchange_kernel, place, shifts, pairs.us...  26.4 us
    pallas_call x1, Pallas kernels, attend_back(): pl.pallas_call(attend_back_kernel, out_shape=[jax.ShapeDtypeStruct(query....  16.7 us
    pallas_call x1, Pallas kernels, attend(): pl.pallas_call(attend_kernel, out_shape=[jax.ShapeDtypeStruct((rows, H *...  14.6 us
  transfers between devices with their start and end apart: 9, of which 0 were waited for; matrix products, arithmetic and copies ran while one was open for 12% of the time, Pallas kernels for 38%

profile of v6, /device:TPU:0, one launch (start us, length us, event | category | flops | bytes accessed | tf_op | source)
XLA Modules:
  0.0 709.5 jit_solution(1327045145278568662)
XLA Ops:
  14.0 143.3 %gather0.1 = (bf16[32,64,3072]{2,1,0:T(8,128)(2,1)}, bf16[32,64,576]{2,1,0:T(8,128)(2,1)}, bf16[32,16,4096]{2,1,0:T(8,128)(2,1)}, bf16[32,64,2048]{2,1,0:T(8,128...) custom-call(bf16[64,3072]{1,0:T(8,128)(2,1)} %refs_0_.1, ...), custom_call_target="tpu_custom_call" | custom-call | tf_op jit(solution)/shard_map/gather0/pallas_call | solution.py:369
  162.5 2.4 fusion.54
  166.2 6.8 all_gather.6
  175.6 4.3 all-to-all-start
  182.2 2.2 copy-done
  184.4 14.6 %attend.1 = (bf16[128,3072]{1,0:T(8,128)(2,1)S(1)}, bf16[256,4096]{1,0:T(8,128)(2,1)S(1)}, f32[16,128,256]{2,1,0:T(8,128)S(1)}, bf16[128,2048]{1,0:T(8,128)(2,1)S(1)}) custom-call(s32[2]{0:T(128)S(1)} %pad_add_fusion.numbers, bf16[128,2048]{1,0:T(8,128)(2,1)S(1)} %fusion.7.hidden.refs_4_.refs_0_, bf16[2048,3072]{1,0:T(8,128)(2,1)} %bitcast.120, ...), custom_call_target="tpu_custom_call" | custom-call | tf_op jit(solution)/shard_map/attend/pallas_call | solution.py:1090
  199.1 6.7 multiply_reduce_fusion.2
  211.8 67.6 %gather1.1 = (bf16[16,128,2048]{2,1,0:T(8,128)(2,1)}, bf16[16,64,256]{2,1,0:T(8,128)(2,1)}, bf16[1024,1408]{1,0:T(8,128)(2,1)}) custom-call(bf16[128,2048]{1,0:T(8,128)(2,1)} %multiply_convert_fusion.refs_0_, bf16[16,64,256]{2,1,0:T(8,128)(2,1)} %all-to-all-done.refs_1_, bf16[1024,1408]{1,0:T(8,128)(2,1)} %bitcast.124, ...), custom_call_target="tpu_custom_call", output_to_operand_aliasing={{2}: (3, {})} | custom-call | tf_op jit(solution)/shard_map/gather1/pallas_call | solution.py:369
  282.5 73.3 %ffn.1 = (bf16[1024,1024]{1,0:T(8,128)(2,1)}, bf16[1024,1024]{1,0:T(8,128)(2,1)}, bf16[1024,1024]{1,0:T(8,128)(2,1)}, bf16[1024,1024]{1,0:T(8,128)(2,1)}, bf16[1...) custom-call(s32[19]{0:T(128)} %pad_add_fusion.1.numbers, ...), custom_call_target="tpu_custom_call" | custom-call | flops 53150220288 | bytes 62914560 | tf_op jit(solution)/shard_map/ffn/pallas_call | solution.py:997
  355.8 7.5 %convolution_convert_fusion.refs_1_ = bf16[1024,1408]{1,0:T(8,128)(2,1)} fusion(bf16[1024,1024]{1,0:T(8,128)(2,1)} %get-tuple-element.98.refs_6_, bf16[1024,1408]{1,0:T(8,128)(2,1)} %get-tuple-element.99.refs_11_), kind=kOutput, calls=%fused_computation.3 | convolution fusion | flops 2954231808 | bytes 7864320 | tf_op jit(solution)/shard_map/dot_general | solution.py:1383
  363.3 66.3 %scatter2.1 = (f32[128,2048]{1,0:T(8,128)}, bf16[1024,1408]{1,0:T(8,128)(2,1)}, bf16[2048,256]{1,0:T(8,128)(2,1)}, bf16[128,2048]{1,0:T(8,128)(2,1)}, bf16[1024,...) custom-call(bf16[16,128,2048]{2,1,0:T(8,128)(2,1)} %get-tuple-elemen, ...), custom_call_target="tpu_custom_call" | custom-call | tf_op jit(solution)/shard_map/scatter2/pallas_call | solution.py:815
  433.2 2.4 convolution_bitcast_fusion.1
  435.6 2.3 convolution_bitcast_fusion
  446.5 3.1 multiply_reduce_fusion
  452.8 16.7 %attend_back.1 = (bf16[128,3072]{1,0:T(8,128)(2,1)S(1)}, bf16[256,4096]{1,0:T(8,128)(2,1)S(1)}, f32[256,128]{1,0:T(8,128)S(1)}) custom-call(bf16[128,2048]{1,0:T(8,128)(2,1)S(1)} %get-tuple-element.227.d_res.refs_3_, bf16[2048,2048]{1,0:T(8,128)(2,1)} %bitcast.119, bf16[128,3072]{1,0:T(8,128)(2,1)S(1)} %copy-done.13, bf16[256,4096]{1,0:T(8,128)(2,1)S(1)} %copy-done.9, ...), custom_call_target="tpu_custom_call" | custom-call | tf_op jit(solution)/shard_map/attend_back/pallas_call | solution.py:1165
  472.1 26.4 %exchange4.1 = (bf16[128,4096]{1,0:T(8,128)(2,1)}, bf16[128,64]{1,0:T(8,128)(2,1)}, bf16[2048,2048]{1,0:T(8,128)(2,1)}, bf16[2048,3072]{1,0:T(8,128)(2,1)}, f32[128,2048]{1,0:T(8,128)}) custom-call(bf16[128,4096]{1,0:T(8,128)(2,1)} %constant_dynamic-slice_fusion.refs_0_, bf16[128,64]{1,0:T(8,128)(2,1)} %dynamic-slice_convert_fusion.refs_1_, ...), custom_call_target="tpu_custom_call" | custom-call | tf_op jit(solution)/shard_map/exchange4/pallas_call | solution.py:513
  501.5 5.0 add_bitcast_fusion.2
  513.1 4.9 all-to-all-start.1
  518.0 3.9 multiply_reduce_fusion.3
  523.7 3.7 outer.1
  531.0 2.6 fusion.13
  534.5 142.2 %scatter3.1 = (f32[64,3072]{1,0:T(8,128)}, f32[64,576]{1,0:T(8,128)}, f32[16,4096]{1,0:T(8,128)}, f32[64,2048]{1,0:T(8,128)}, f32[64,16]{1,0:T(8,128)}, /*index=5*/f32[8,128]{1,0:T(8,128)}, bf16[1408,1024]{1,0:T(8,128)(2,1)}) custom-call(bf16[32,64,3072]{2,1,0:T(8,128)(2,1)} %bitcast.122, bf16[32,64,576]{2,1,0:T(8,128)(2,1)} %bitcast.115, ...), custom_call_target="tpu_custom_call" | custom-call | tf_op jit(solution)/shard_map/scatter3/pallas_call | solution.py:815
  676.8 6.6 add_bitcast_fusion
  685.5 5.8 add_bitcast_fusion.1
  (289 shorter events, 71.6 us)
Async XLA Ops:
  7.2 275.3 %all-gather.2.cloned.1.call-start = ((), (), s32[]{:S(2)}) async-start(), calls=%async_computation.3 | async-start | bytes 8912896 | tf_op jit(solution)/shard_map/all_gather | solution.py:1297
  14.0 147.2 %copy-start.14 = (bf16[128,2048]{1,0:T(8,128)(2,1)S(1)}, bf16[128,2048]{1,0:T(8,128)(2,1)}, u32[]{:S(2)}) copy-start(bf16[128,2048]{1,0:T(8,128)(2,1)} %param.18) | copy-start | bytes 1572868
  157.3 52.0 %collective-permute-start.1 = (bf16[44,2048]{1,0:T(8,128)(2,1)}, bf16[44,2048]{1,0:T(8,128)(2,1)}, u32[]{:S(2)}, u32[]{:S(2)}) collective-permute-start(bf16[44,2048]{1,0:T(8,128)(2,1)} %param.32), channel_id=1, source_target_pairs={{0,1},{1,0},{2,3},{3,2},{4,5},{5,4},{6,7},{7,6},{8,9},{9,8},{10,11... | collective-permute-start | bytes 540680 | tf_op jit(solution)/shard_map/ppermute | solution.py:1195
  160.0 271.4 %copy-start.75 = (f32[16]{0:T(128)}, f32[16]{0:T(128)S(1)}, u32[]{:S(2)}) copy-start(f32[16]{0:T(128)S(1)} %get-tuple-element.221) | copy-start | bytes 196
  162.2 20.1 %copy-start.1 = (bf16[128,2048]{1,0:T(8,128)(2,1)}, bf16[128,2048]{1,0:T(8,128)(2,1)S(1)}, u32[]{:S(2)}) copy-start(bf16[128,2048]{1,0:T(8,128)(2,1)S(1)} %fusion.7.hidden.refs_4_.refs_0_) | copy-start | bytes 1572868
  162.2 11.4 %copy-start.34 = (bf16[64,1408]{1,0:T(8,128)(2,1)S(1)}, bf16[64,1408]{1,0:T(8,128)(2,1)}, u32[]{:S(2)}) copy-start(bf16[64,1408]{1,0:T(8,128)(2,1)} %param.30) | copy-start | bytes 540676
  162.5 11.6 %copy-start.35 = (bf16[64,1408]{1,0:T(8,128)(2,1)S(1)}, bf16[64,1408]{1,0:T(8,128)(2,1)}, u32[]{:S(2)}) copy-start(bf16[64,1408]{1,0:T(8,128)(2,1)} %param.31) | copy-start | bytes 540676
  173.0 109.5 %collective-permute-start = (bf16[1408,1024]{1,0:T(8,128)(2,1)}, bf16[1408,1024]{1,0:T(8,128)(2,1)}, u32[]{:S(2)}, u32[]{:S(2)}) collective-permute-start(bf16[1408,1024]{1,0:T(8,128)(2,1)} %bitcast.11.refs_7_), channel_id=1, source_target_pairs={{0,1},{1,0},{2,3},{3,2},{4,5},{5,4},{6,7},{7,6},{8,9},{9,8},{10,11... | collective-permute-start | bytes 8650760 | tf_op jit(solution)/shard_map/ppermute | solution.py:1195
  175.6 36.2 %all-to-all-start = ((bf16[16,64,256]{2,1,0:T(8,128)(2,1)}), bf16[16,64,256]{2,1,0:T(8,128)(2,1)}, u32[]{:S(2)}, u32[]{:S(2)}) async-start(bf16[16,64,256]{2,1,0:T(8,128)(2,1)} %fusion.18), calls=%async_computation | async-start | bytes 1048576 | tf_op jit(solution)/shard_map/all_to_all | solution.py:1291
  179.9 511.4 %reduce-scatter.2.cloned.1.call-start = ((), (), s32[]{:S(2)}) async-start(), calls=%async_computation.4 | async-start | bytes 8912896 | tf_op jit(solution)/shard_map/reduce_scatter | solution.py:1437
  184.4 14.6 %copy-start.37 = (f32[32,16,128]{2,1,0:T(8,128)S(1)}, f32[32,16,128]{2,1,0:T(8,128)}, u32[]{:S(2)}) copy-start(f32[32,16,128]{2,1,0:T(8,128)} %get-tuple-element.82) | copy-start | bytes 786436
  431.3 15.1 %copy-start.32 = (f32[128,16]{0,1:T(8,128)}, f32[128,16]{0,1:T(8,128)S(1)}, u32[]{:S(2)}) copy-start(f32[128,16]{0,1:T(8,128)S(1)} %get-tuple-element.253) | copy-start | bytes 24580
  442.4 66.8 %collective-permute-start.3 = (bf16[44,2048]{1,0:T(8,128)(2,1)}, bf16[44,2048]{1,0:T(8,128)(2,1)}, u32[]{:S(2)}, u32[]{:S(2)}) collective-permute-start(bf16[44,2048]{1,0:T(8,128)(2,1)} %dynamic-slice_bitcast_fusion.1), channel_id=1, source_target_pairs={{0,1},{1,0},{2,3},{3,2},{4,5},{5,4},{6,7},{7,6},{8,9},{9,8},{10,11... | collective-permute-start | bytes 540680 | tf_op jit(solution)/shard_map/ppermute | solution.py:1203
  444.9 66.1 %collective-permute-start.2 = (bf16[16,64,256]{2,1,0:T(8,128)(2,1)}, bf16[16,64,256]{2,1,0:T(8,128)(2,1)}, u32[]{:S(2)}, u32[]{:S(2)}) collective-permute-start(bf16[16,64,256]{2,1,0:T(8,128)(2,1)} %dynamic-slice_bitcast_fusion), channel_id=1, source_target_pairs={{0,1},{1,0},{2,3},{3,2},{4,5},{5,4},{6,7},{7,6},{8,9},{9,8},{10,11... | collective-permute-start | bytes 1572872 | tf_op jit(solution)/shard_map/ppermute | solution.py:1203
  451.1 18.3 %copy-start.3 = (bf16[128,2048]{1,0:T(8,128)(2,1)}, bf16[128,2048]{1,0:T(8,128)(2,1)S(1)}, u32[]{:S(2)}) copy-start(bf16[128,2048]{1,0:T(8,128)(2,1)S(1)} %get-tuple-element.227.d_res.refs_3_) | copy-start | bytes 1572868
  472.0 28.6 %copy-start.33 = (f32[128,16]{0,1:T(8,128)S(1)}, f32[128,16]{0,1:T(8,128)}, u32[]{:S(2)}) copy-start(f32[128,16]{0,1:T(8,128)} %copy-done.32) | copy-start | bytes 24580
  472.0 28.6 %copy-start.52 = (f32[128]{0:T(128)S(1)}, f32[128]{0:T(128)}, u32[]{:S(2)}) copy-start(f32[128]{0:T(128)} %copy-done.50) | copy-start | bytes 1540
  472.0 28.6 %copy-start.55 = (f32[128]{0:T(128)S(1)}, f32[128]{0:T(128)}, u32[]{:S(2)}) copy-start(f32[128]{0:T(128)} %copy-done.53) | copy-start | bytes 1540
  472.0 28.6 %copy-start.58 = (f32[128]{0:T(128)S(1)}, f32[128]{0:T(128)}, u32[]{:S(2)}) copy-start(f32[128]{0:T(128)} %copy-done.56) | copy-start | bytes 1540
  472.0 28.6 %copy-start.68 = (f32[16]{0:T(128)S(1)}, f32[16]{0:T(128)}, u32[]{:S(2)}) copy-start(f32[16]{0:T(128)} %copy-done.66) | copy-start | bytes 196
  472.0 28.6 %copy-start.70 = (f32[128]{0:T(128)S(1)}, f32[128]{0:T(128)}, u32[]{:S(2)}) copy-start(f32[128]{0:T(128)} %get-tuple-element.226) | copy-start | bytes 1540
  472.0 29.5 %copy-start.22 = (bf16[1024,1408]{1,0:T(8,128)(2,1)S(1)}, bf16[1024,1408]{1,0:T(8,128)(2,1)}, u32[]{:S(2)}) copy-start(bf16[1024,1408]{1,0:T(8,128)(2,1)} %get-tuple-element.142) | copy-start | bytes 8650756
  498.5 187.1 %collective-permute-start.4 = (bf16[1024,1408]{1,0:T(8,128)(2,1)}, bf16[1024,1408]{1,0:T(8,128)(2,1)}, u32[]{:S(2)}, u32[]{:S(2)}) collective-permute-start(bf16[1024,1408]{1,0:T(8,128)(2,1)} %get-tuple-element.144), channel_id=1, source_target_pairs={{0,1},{1,0},{2,3},{3,2},{4,5},{5,4},{6,7},{7,6},{8,9},{9,8},{10,11... | collective-permute-start | bytes 8650760 | tf_op jit(solution)/shard_map/ppermute | solution.py:1479
  513.1 178.2 %all-to-all-start.1 = ((bf16[16,64,256]{2,1,0:T(8,128)(2,1)}), bf16[16,64,256]{2,1,0:T(8,128)(2,1)}, u32[]{:S(2)}, u32[]{:S(2)}) async-start(bf16[16,64,256]{2,1,0:T(8,128)(2,1)} %fusion.14), calls=%async_computation.1 | async-start | bytes 1048576 | tf_op jit(solution)/shard_map/all_to_all | solution.py:1485
  (67 other events, 359.3 us)
Sparse Core Ops, SparseCore 0:
  157.5 87.2 all-gather.1
  429.8 114.9 reduce-scatter.1

commit v7 on v6

--- a/solution.py
+++ b/solution.py
@@ -1406,6 +1406,7 @@
             total = total + block.astype(f32)
         return total
 
+    dlog_wide = jnp.pad(dlog_rows, ((0, 0), (0, -expert_count % 128)))
     d_hidden_two, *more = scatter(
         [back_part],
         False,
@@ -1419,19 +1420,22 @@
             (rows_in[0], d_hidden_g),
             (rows_in[0], d_hidden_u),
             (act, d_out[0]),
+            *[(w, dlog_wide) for w in rows_in],
         ]
         if peers == 2
         else [],
     )
     gate_blocks = more[: peers - 1]
     if peers == 2:
-        d_gu_weight, d_sd, *others, gate_own, up_own, down_own = more[1:]
+        router_parts = more[-peers:]
+        d_gu_weight, d_sd, *others, gate_own, up_own, down_own = more[1:-peers]
     else:
         d_gu_weight = outer(hid_plane, d_gu).astype(bf16)
         d_sd = outer(shared_scaled, cot_plane).astype(bf16)
         others = [up_term(r).astype(bf16) for r in turns]
         others = others + [down_term(r).astype(bf16) for r in turns]
         gate_own, up_own, down_own = gate_term(0), up_term(0), down_term(0)
+        router_parts = [outer(w, dlog_rows) for w in rows_in]
     d_sd = d_sd[:units]
     out_part, d_hidden_two = lax.optimization_barrier((out_part, d_hidden_two))
     out_sum = lax.psum_scatter(
@@ -1439,7 +1443,7 @@
     )
     egate_grad = plus(gate_own.astype(f32), gate_blocks)[None]
     d_hidden_two = d_hidden_two + back(dlog_own, w_router)
-    router_parts = jnp.stack([outer(rows_in[r], dlog_rows) for r in range(peers)])
+    router_parts = jnp.stack([w[:, :expert_count].astype(f32) for w in router_parts])
     router_grad = jnp.roll(router_parts, fid, axis=0).reshape(dim, -1) + outer(hidden_two, dlog_own)
     d_gu_blocks = d_gu_weight.reshape(group, peers, dim // (group * peers), -1)
     d_sd_blocks = d_sd.reshape(peers, units // peers, dim)

time: 722 us -> 748 us (1.036)
  waiting for transfers between devices: 0.06 us -> 28.6 us
    ppermute x2, waiting for transfers between devices: 0.01 us -> 28.6 us  [from_peers(): lax.ppermute(block, 'fsdp', [(j, (j - r) % size) for j in range(size)])]
    pallas_call x2, Pallas kernels: 209 us -> 227 us  [scatter(): pl.pallas_call(functools.partial(scatter_kernel, place, count, shifts, pa...]
    pallas_call x2, Pallas kernels: 211 us -> 194 us  [gather(): pl.pallas_call(functools.partial(gather_kernel, place, count, shifts, spa...]
    unnamed x171 -> x155, local copies, waits for them, and re-layouts: 14.4 us -> 15.2 us
  transfers between devices with their start and end apart: 9 -> 9, of which waited for: 0 -> 1; matrix products, arithmetic and copies ran while one was open for 12% -> 11% of each run, Pallas kernels for 38% -> 36%
where the time goes in v7:
time: 748 us; the launch traced here: 738 us
  Pallas kernels  557 us (74%)
  other arithmetic  47 us (6%)
  local copies, waits for them, and re-layouts  37.2 us (5%)
  matrix products  30.5 us (4%)
  waiting for transfers between devices  28.6 us (4%)
  between operations  17.5 us (2%)
  starting transfers between devices  13.2 us (2%)
    pallas_call x2, Pallas kernels, scatter(): pl.pallas_call(functools.partial(scatter_kernel, place, count, shifts, pa...  227 us
    pallas_call x2, Pallas kernels, gather(): pl.pallas_call(functools.partial(gather_kernel, place, count, shifts, spa...  194 us
    pallas_call x1, Pallas kernels, ffn(): pl.pallas_call(functools.partial(ffn_kernel, peers, sources), out_shape=[...  73.3 us
    ppermute x2, waiting for transfers between devices, from_peers(): lax.ppermute(block, 'fsdp', [(j, (j - r) % size) for j in range(size)])  28.6 us
    pallas_call x1, Pallas kernels, exchange(): pl.pallas_call(functools.partial(exchange_kernel, place, shifts, pairs.us...  27.9 us
    pallas_call x1, Pallas kernels, attend_back(): pl.pallas_call(attend_back_kernel, out_shape=[jax.ShapeDtypeStruct(query....  16.8 us
    unnamed x155, local copies, waits for them, and re-layouts  15.2 us
  transfers between devices with their start and end apart: 9, of which 1 were waited for; matrix products, arithmetic and copies ran while one was open for 11% of the time, Pallas kernels for 36%

profile of v7, /device:TPU:0, one launch (start us, length us, event | category | flops | bytes accessed | tf_op | source)
XLA Modules:
  0.0 738.5 jit_solution(11518450739553612009)
XLA Ops:
  14.3 143.3 %gather0.1 = (bf16[32,64,3072]{2,1,0:T(8,128)(2,1)}, bf16[32,64,576]{2,1,0:T(8,128)(2,1)}, bf16[32,16,4096]{2,1,0:T(8,128)(2,1)}, bf16[32,64,2048]{2,1,0:T(8,128...) custom-call(bf16[64,3072]{1,0:T(8,128)(2,1)} %refs_0_.1, ...), custom_call_target="tpu_custom_call" | custom-call | tf_op jit(solution)/shard_map/gather0/pallas_call | solution.py:369
  161.4 2.5 fusion.53
  165.9 7.1 all_gather.6
  176.6 4.3 all-to-all-start
  183.8 2.2 copy-done
  186.0 14.3 %attend.1 = (bf16[128,3072]{1,0:T(8,128)(2,1)S(1)}, bf16[256,4096]{1,0:T(8,128)(2,1)S(1)}, f32[16,128,256]{2,1,0:T(8,128)S(1)}, bf16[128,2048]{1,0:T(8,128)(2,1)S(1)}) custom-call(s32[2]{0:T(128)S(1)} %pad_add_fusion.numbers, bf16[128,2048]{1,0:T(8,128)(2,1)S(1)} %fusion.7.hidden.refs_4_.refs_0_, bf16[2048,3072]{1,0:T(8,128)(2,1)} %bitcast.116, ...), custom_call_target="tpu_custom_call" | custom-call | tf_op jit(solution)/shard_map/attend/pallas_call | solution.py:1090
  200.5 7.7 %multiply_reduce_fusion.2 = (f32[128]{0:T(128)S(1)}, f32[128,2048]{1,0:T(8,128)}) fusion(bf16[128,2048]{1,0:T(8,128)(2,1)S(1)} %get-tuple-element.89.refs_2_, bf16[2048,2048]{1,0:T(8,128)(2,1)} %bitcast.114, bf16[128,2048]{1,0:T(8,128)(2,1)S(1)} %copy-done.23), kind=kOutput, calls=%fused_computation.42 | convolution fusion | flops 1074790272 | bytes 10486272 | tf_op jit(solution)/shard_map/dot_general | solution.py:1331
  210.0 2.2 multiply_convert_fusion.refs_0_
  213.0 28.6 %collective-permute-done.1 = bf16[44,2048]{1,0:T(8,128)(2,1)S(1)} collective-permute-done((bf16[44,2048]{1,0:T(8,128)(2,1)S(1)}, bf16[44,2048]{1,0:T(8,128)(2,1)S(1)}, u32[]{:S(2)}, u32[]{:S(2)}) %collective-permute-start.1) | collective-permute-done | bytes 180256 | tf_op jit(solution)/shard_map/ppermute | solution.py:1195
  242.8 51.0 %gather1.1 = (bf16[16,128,2048]{2,1,0:T(8,128)(2,1)}, bf16[16,64,256]{2,1,0:T(8,128)(2,1)}, bf16[1024,1408]{1,0:T(8,128)(2,1)}) custom-call(bf16[128,2048]{1,0:T(8,128)(2,1)} %multiply_convert_fusion.refs_0_, bf16[16,64,256]{2,1,0:T(8,128)(2,1)} %all-to-all-done.refs_1_, bf16[1024,1408]{1,0:T(8,128)(2,1)} %bitcast.120, ...), custom_call_target="tpu_custom_call", output_to_operand_aliasing={{2}: (3, {})} | custom-call | tf_op jit(solution)/shard_map/gather1/pallas_call | solution.py:369
  297.0 73.3 %ffn.1 = (bf16[1024,1024]{1,0:T(8,128)(2,1)}, bf16[1024,1024]{1,0:T(8,128)(2,1)}, bf16[1024,1024]{1,0:T(8,128)(2,1)}, bf16[1024,1024]{1,0:T(8,128)(2,1)}, bf16[1...) custom-call(s32[19]{0:T(128)} %pad_add_fusion.1.numbers, ...), custom_call_target="tpu_custom_call" | custom-call | flops 53150220288 | bytes 62914560 | tf_op jit(solution)/shard_map/ffn/pallas_call | solution.py:997
  372.0 7.5 %convolution_convert_fusion.refs_1_ = bf16[1024,1408]{1,0:T(8,128)(2,1)} fusion(bf16[1024,1024]{1,0:T(8,128)(2,1)} %get-tuple-element.100.refs_6_, bf16[1024,1408]{1,0:T(8,128)(2,1)} %get-tuple-element.101.refs_11_), kind=kOutput, calls=%fused_computation.3 | convolution fusion | flops 2954231808 | bytes 7864320 | tf_op jit(solution)/shard_map/dot_general | solution.py:1383
  379.5 75.6 %scatter2.1 = (f32[128,2048]{1,0:T(8,128)}, bf16[1024,1408]{1,0:T(8,128)(2,1)}, bf16[2048,256]{1,0:T(8,128)(2,1)}, bf16[128,2048]{1,0:T(8,128)(2,1)}, bf16[1024,...) custom-call(bf16[16,128,2048]{2,1,0:T(8,128)(2,1)} %get-tuple-elemen, ...), custom_call_target="tpu_custom_call" | custom-call | tf_op jit(solution)/shard_map/scatter2/pallas_call | solution.py:815
  462.8 3.1 multiply_reduce_fusion
  469.1 16.8 %attend_back.1 = (bf16[128,3072]{1,0:T(8,128)(2,1)S(1)}, bf16[256,4096]{1,0:T(8,128)(2,1)S(1)}, f32[256,128]{1,0:T(8,128)S(1)}) custom-call(bf16[128,2048]{1,0:T(8,128)(2,1)S(1)} %get-tuple-element.248.d_res.refs_3_, bf16[2048,2048]{1,0:T(8,128)(2,1)} %bitcast.115, bf16[128,3072]{1,0:T(8,128)(2,1)S(1)} %copy-done.19, bf16[256,4096]{1,0:T(8,128)(2,1)S(1)} %copy-done.9, ...), custom_call_target="tpu_custom_call" | custom-call | tf_op jit(solution)/shard_map/attend_back/pallas_call | solution.py:1165
  488.4 27.9 %exchange4.1 = (bf16[128,4096]{1,0:T(8,128)(2,1)}, bf16[128,64]{1,0:T(8,128)(2,1)}, bf16[2048,2048]{1,0:T(8,128)(2,1)}, bf16[2048,3072]{1,0:T(8,128)(2,1)}, f32[128,2048]{1,0:T(8,128)}) custom-call(bf16[128,4096]{1,0:T(8,128)(2,1)} %constant_dynamic-slice_fusion.refs_0_, bf16[128,64]{1,0:T(8,128)(2,1)} %dynamic-slice_convert_fusion.refs_1_, ...), custom_call_target="tpu_custom_call" | custom-call | tf_op jit(solution)/shard_map/exchange4/pallas_call | solution.py:513
  520.9 2.5 fusion
  523.4 5.9 add_bitcast_fusion.2
  537.2 4.3 all-to-all-start.1
  541.6 4.0 multiply_reduce_fusion.3
  545.8 3.7 outer.1
  555.2 151.4 %scatter3.1 = (f32[64,3072]{1,0:T(8,128)}, f32[64,576]{1,0:T(8,128)}, f32[16,4096]{1,0:T(8,128)}, f32[64,2048]{1,0:T(8,128)}, f32[64,16]{1,0:T(8,128)}, /*index=5*/f32[8,128]{1,0:T(8,128)}, bf16[1408,1024]{1,0:T(8,128)(2,1)}) custom-call(bf16[32,64,3072]{2,1,0:T(8,128)(2,1)} %bitcast.118, bf16[32,64,576]{2,1,0:T(8,128)(2,1)} %bitcast.111, ...), custom_call_target="tpu_custom_call" | custom-call | tf_op jit(solution)/shard_map/scatter3/pallas_call | solution.py:815
  706.7 6.6 add_bitcast_fusion
  715.4 5.9 add_bitcast_fusion.1
  (275 shorter events, 69.4 us)
Async XLA Ops:
  7.2 289.8 %all-gather.2.cloned.1.call-start = ((), (), s32[]{:S(2)}) async-start(), calls=%async_computation.3 | async-start | bytes 8912896 | tf_op jit(solution)/shard_map/all_gather | solution.py:1297
  14.3 146.1 %copy-start.22 = (bf16[128,2048]{1,0:T(8,128)(2,1)S(1)}, bf16[128,2048]{1,0:T(8,128)(2,1)}, u32[]{:S(2)}) copy-start(bf16[128,2048]{1,0:T(8,128)(2,1)} %param.18) | copy-start | bytes 1572868
  161.4 22.4 %copy-start.1 = (bf16[128,2048]{1,0:T(8,128)(2,1)}, bf16[128,2048]{1,0:T(8,128)(2,1)S(1)}, u32[]{:S(2)}) copy-start(bf16[128,2048]{1,0:T(8,128)(2,1)S(1)} %fusion.7.hidden.refs_4_.refs_0_) | copy-start | bytes 1572868
  161.4 13.1 %copy-start.41 = (bf16[64,1408]{1,0:T(8,128)(2,1)S(1)}, bf16[64,1408]{1,0:T(8,128)(2,1)}, u32[]{:S(2)}) copy-start(bf16[64,1408]{1,0:T(8,128)(2,1)} %param.31) | copy-start | bytes 540676
  161.4 13.7 %copy-start.42 = (bf16[64,1408]{1,0:T(8,128)(2,1)S(1)}, bf16[64,1408]{1,0:T(8,128)(2,1)}, u32[]{:S(2)}) copy-start(bf16[64,1408]{1,0:T(8,128)(2,1)} %param.30) | copy-start | bytes 540676
  164.1 16.9 %copy-start.40 = (bf16[44,2048]{1,0:T(8,128)(2,1)S(1)}, bf16[44,2048]{1,0:T(8,128)(2,1)}, u32[]{:S(2)}) copy-start(bf16[44,2048]{1,0:T(8,128)(2,1)} %param.32) | copy-start | bytes 540676
  173.0 123.9 %collective-permute-start = (bf16[1408,1024]{1,0:T(8,128)(2,1)}, bf16[1408,1024]{1,0:T(8,128)(2,1)}, u32[]{:S(2)}, u32[]{:S(2)}) collective-permute-start(bf16[1408,1024]{1,0:T(8,128)(2,1)} %bitcast.11.refs_7_), channel_id=1, source_target_pairs={{0,1},{1,0},{2,3},{3,2},{4,5},{5,4},{6,7},{7,6},{8,9},{9,8},{10,11... | collective-permute-start | bytes 8650760 | tf_op jit(solution)/shard_map/ppermute | solution.py:1195
  176.6 66.1 %all-to-all-start = ((bf16[16,64,256]{2,1,0:T(8,128)(2,1)}), bf16[16,64,256]{2,1,0:T(8,128)(2,1)}, u32[]{:S(2)}, u32[]{:S(2)}) async-start(bf16[16,64,256]{2,1,0:T(8,128)(2,1)} %fusion.18), calls=%async_computation | async-start | bytes 1048576 | tf_op jit(solution)/shard_map/all_to_all | solution.py:1291
  180.9 540.4 %reduce-scatter.2.cloned.1.call-start = ((), (), s32[]{:S(2)}) async-start(), calls=%async_computation.4 | async-start | bytes 8912896 | tf_op jit(solution)/shard_map/reduce_scatter | solution.py:1441
  181.0 60.5 %collective-permute-start.1 = (bf16[44,2048]{1,0:T(8,128)(2,1)S(1)}, bf16[44,2048]{1,0:T(8,128)(2,1)S(1)}, u32[]{:S(2)}, u32[]{:S(2)}) collective-permute-start(bf16[44,2048]{1,0:T(8,128)(2,1)S(1)} %copy-done.40), channel_id=1, source_target_pairs={{0,1},{1,0},{2,3},{3,2},{4,5},{5,4},{6,7},{7,6},{8,9},{9,8},{10,11... | collective-permute-start | bytes 540680 | tf_op jit(solution)/shard_map/ppermute | solution.py:1195
  183.5 16.8 %copy-start.14 = (bf16[256,256]{1,0:T(8,128)(2,1)}, bf16[256,256]{1,0:T(8,128)(2,1)S(1)}, u32[]{:S(2)}) copy-start(bf16[256,256]{1,0:T(8,128)(2,1)S(1)} %pad.59.rot) | copy-start | bytes 393220
  183.7 16.6 %copy-start.12 = (f32[128,384]{1,0:T(8,128)}, f32[128,384]{1,0:T(8,128)S(1)}, u32[]{:S(2)}) copy-start(f32[128,384]{1,0:T(8,128)S(1)} %concatenate.54.plain) | copy-start | bytes 589828
  186.0 14.3 %copy-start.44 = (f32[32,16,128]{2,1,0:T(8,128)S(1)}, f32[32,16,128]{2,1,0:T(8,128)}, u32[]{:S(2)}) copy-start(f32[32,16,128]{2,1,0:T(8,128)} %get-tuple-element.84) | copy-start | bytes 786436
  186.0 14.5 %copy-start.23 = (bf16[128,2048]{1,0:T(8,128)(2,1)S(1)}, bf16[128,2048]{1,0:T(8,128)(2,1)}, u32[]{:S(2)}) copy-start(bf16[128,2048]{1,0:T(8,128)(2,1)} %param.18) | copy-start | bytes 1572868
  208.7 85.1 %copy-start.56 = (f32[128]{0:T(128)}, f32[128]{0:T(128)S(1)}, u32[]{:S(2)}) copy-start(f32[128]{0:T(128)S(1)} %get-tuple-element.270) | copy-start | bytes 1540
  209.4 84.4 %copy-start.45 = (f32[2048]{0:T(1024)}, f32[2048]{0:T(1024)S(1)}, u32[]{:S(2)}) copy-start(f32[2048]{0:T(1024)S(1)} %mul.326) | copy-start | bytes 24580
  462.5 72.6 %collective-permute-start.2 = (bf16[16,64,256]{2,1,0:T(8,128)(2,1)}, bf16[16,64,256]{2,1,0:T(8,128)(2,1)}, u32[]{:S(2)}, u32[]{:S(2)}) collective-permute-start(bf16[16,64,256]{2,1,0:T(8,128)(2,1)} %dynamic-slice_bitcast_fusion), channel_id=1, source_target_pairs={{0,1},{1,0},{2,3},{3,2},{4,5},{5,4},{6,7},{7,6},{8,9},{9,8},{10,11... | collective-permute-start | bytes 1572872 | tf_op jit(solution)/shard_map/ppermute | solution.py:1203
  467.4 18.5 %copy-start.3 = (bf16[128,2048]{1,0:T(8,128)(2,1)}, bf16[128,2048]{1,0:T(8,128)(2,1)S(1)}, u32[]{:S(2)}) copy-start(bf16[128,2048]{1,0:T(8,128)(2,1)S(1)} %get-tuple-element.248.d_res.refs_3_) | copy-start | bytes 1572868
  488.4 28.0 %copy-start.38 = (bf16[1024,128]{1,0:T(8,128)(2,1)S(1)}, bf16[1024,128]{1,0:T(8,128)(2,1)}, u32[]{:S(2)}) copy-start(bf16[1024,128]{1,0:T(8,128)(2,1)} %get-tuple-element.131) | copy-start | bytes 786436
  488.4 28.0 %copy-start.39 = (bf16[1024,128]{1,0:T(8,128)(2,1)S(1)}, bf16[1024,128]{1,0:T(8,128)(2,1)}, u32[]{:S(2)}) copy-start(bf16[1024,128]{1,0:T(8,128)(2,1)} %get-tuple-element.132) | copy-start | bytes 786436
  519.2 14.1 %collective-permute-start.3 = (bf16[44,2048]{1,0:T(8,128)(2,1)}, bf16[44,2048]{1,0:T(8,128)(2,1)}, u32[]{:S(2)}, u32[]{:S(2)}) collective-permute-start(bf16[44,2048]{1,0:T(8,128)(2,1)} %dynamic-slice_bitcast_fusion.1), channel_id=1, source_target_pairs={{0,1},{1,0},{2,3},{3,2},{4,5},{5,4},{6,7},{7,6},{8,9},{9,8},{10,11... | collective-permute-start | bytes 540680 | tf_op jit(solution)/shard_map/ppermute | solution.py:1203
  530.0 11.6 %copy-start.59 = (f32[128]{0:T(128)S(1)}, f32[128]{0:T(128)}, u32[]{:S(2)}) copy-start(f32[128]{0:T(128)} %copy-done.58) | copy-start | bytes 1540
  532.9 182.5 %collective-permute-start.4 = (bf16[1024,1408]{1,0:T(8,128)(2,1)}, bf16[1024,1408]{1,0:T(8,128)(2,1)}, u32[]{:S(2)}, u32[]{:S(2)}) collective-permute-start(bf16[1024,1408]{1,0:T(8,128)(2,1)} %get-tuple-element.148), channel_id=1, source_target_pairs={{0,1},{1,0},{2,3},{3,2},{4,5},{5,4},{6,7},{7,6},{8,9},{9,8},{10,11... | collective-permute-start | bytes 8650760 | tf_op jit(solution)/shard_map/ppermute | solution.py:1483
  537.2 184.1 %all-to-all-start.1 = ((bf16[16,64,256]{2,1,0:T(8,128)(2,1)}), bf16[16,64,256]{2,1,0:T(8,128)(2,1)S(1)}, u32[]{:S(2)}, u32[]{:S(2)}) async-start(bf16[16,64,256]{2,1,0:T(8,128)(2,1)} %fusion.14), calls=%async_computation.1 | async-start | bytes 1048576 | tf_op jit(solution)/shard_map/all_to_all | solution.py:1489
  (59 other events, 308.7 us)
Sparse Core Ops, SparseCore 0:
  157.8 78.5 all-gather.1
  455.3 115.0 reduce-scatter.1
